TPU v7x, 32 devices: a whole 2x2x4 slice. The times are simulated.
32 devices in a mesh: tm: 8 (over z, y), batch: 4 (over x, core).
Axes of the slice: x: 2, y: 2, z: 4, core: 2. Of those that a mesh axis runs over, the one named last changes fastest.
Arguments:
- audio: float32 [4, 61440], P(None, ('tm', 'batch')), may hold values from -6 to 6
- lengths: int32 [4], replicated, may hold values from 15360 to 61440
- kernel0: float32 [10, 512], replicated, may hold values from -2 to 2
- kernel1: bfloat16 [1536, 512], replicated, may hold values from -0.15625 to 0.15625
- kernel2: bfloat16 [1536, 512], replicated, may hold values from -0.15625 to 0.15625
- conv_bias: float32 [3, 512], replicated, may hold values from -3 to 3
- norm_gain: float32 [3, 512], replicated, may hold values from 0.25 to 1.75
- norm_shift: float32 [3, 512], replicated, may hold values from -2 to 2
- cotangent: bfloat16 [4, 3072, 512], P('batch', 'tm'), may hold values from -6 to 6
- left_prev: float32 [64, 192, 192], P('tm'), may hold values from -0.4 to 2.4, as said below
- right_prev: float32 [64, 128, 128], P('tm'), may hold values from -0.4 to 2.4, as said below
Outputs:
- frames: bfloat16 [4, 3072, 512], P('batch', 'tm')
- left_stat: float32 [64, 192, 192], P('tm')
- right_stat: float32 [64, 128, 128], P('tm')
Inputs may be any that keep to these rules, and one draw needn't show every extreme that they name: `left_prev`: symmetric running statistics of earlier steps. `right_prev`: symmetric running statistics of earlier steps.
All inputs are finite; a program needn't handle non-finite values.
Results may differ from a plain program's by a relative error of at most 0.0048.
The roundings to bfloat16 on the way count: a program that leaves them out, or rounds other values in their place, can miss the bound.
Values may be sent and summed in bfloat16 or wider, within the bound.
No kernel may reach another device: no remote copies, remote signals or barrier semaphores. Data moves between devices by JAX's collectives and lax.ppermute only.
A program may use at most 64 MiB of HBM per device.

v0:
```python
import math

import jax
import jax.numpy as jnp
from jax import lax
from jax.sharding import PartitionSpec as P

BR = 192
BC = 128


EPS = 1e-05
BETA = 0.95


def passed_along(block, axis, distance):
    devices = range(lax.axis_size(axis))
    route = [(i - distance, i) for i in devices if i - distance in devices]
    return lax.ppermute(block, axis, route)


def norm_act(preact, offset, scaling, moving):
    shifted = preact + offset
    average = jnp.mean(shifted, -1, keepdims=True)
    centred = shifted - average
    spread = jnp.mean(centred * centred, -1, keepdims=True)
    normalized = centred * lax.rsqrt(spread + EPS)
    return jax.nn.gelu(normalized * scaling + moving, approximate=False)


def sample_taps(samples, rows):
    leading = samples.shape[:-1]
    opening = samples[..., : 5 * rows].reshape(leading + (rows, 5))
    second = samples[..., 5 : 5 * rows + 5].reshape(leading + (rows, 5))
    return jnp.concatenate([opening, second], -1)


def frame_windows(source, rows):
    leading = source.shape[:-2]
    channels = source.shape[-1]
    paired = source[..., : 2 * rows, :].reshape(leading + (rows, 2 * channels))
    following = source[..., 2 : 2 * rows + 1 : 2, :]
    return jnp.concatenate([paired, following], -1)


def to_blocks(gradient):
    rows_all, cols_all = gradient.shape
    split = gradient.reshape(rows_all // BR, BR, cols_all // BC, BC)
    return jnp.transpose(split, (0, 2, 1, 3)).reshape(-1, BR, BC)


def next_frame(source):
    incoming = passed_along(source[:, :1], ("tm", "batch"), -1)
    return jnp.concatenate([source, incoming], 1)


def body(
    audio,
    lengths,
    kernel0,
    kernel1,
    kernel2,
    conv_bias,
    norm_gain,
    norm_shift,
    cotangent,
    left_prev,
    right_prev,
):
    recordings, samples_dev = audio.shape
    channels = kernel1.shape[1]
    rows_zero = samples_dev // 5
    rows_one = rows_zero // 2
    rows_two = rows_one // 2
    devices = lax.axis_size(("tm", "batch"))
    device_place = lax.axis_index(("tm", "batch"))
    scale = 1.0 / math.sqrt(rows_two * devices)

    def layer_map(layer_index, row_keep):

        def mapping(preact):
            return (
                norm_act(
                    preact, conv_bias[layer_index], norm_gain[layer_index], norm_shift[layer_index]
                )
                * row_keep
            )

        return mapping

    sample_pos = device_place * samples_dev + jnp.arange(samples_dev, dtype=jnp.int32)
    masked = jnp.where(sample_pos[None, :] < lengths[:, None], audio, jnp.zeros_like(audio))
    tail_samples = passed_along(masked[:, :5], ("tm", "batch"), -1)
    samples = jnp.concatenate([masked, tail_samples], 1)
    preact0 = jnp.einsum(
        "rnt,tc->rnc", sample_taps(samples, rows_zero), kernel0, precision=lax.Precision.HIGHEST
    )
    act_zero = layer_map(0, 1.0)(preact0).astype(jnp.bfloat16)
    win_zero = frame_windows(next_frame(act_zero), rows_one)
    preact1 = jnp.einsum("rnk,kc->rnc", win_zero, kernel1, preferred_element_type=jnp.float32)
    act_one, back_one = jax.vjp(layer_map(1, 1.0), preact1)
    source_one = next_frame(act_one.astype(jnp.bfloat16))
    win_one = frame_windows(source_one, rows_two)
    preact2 = jnp.einsum("rnk,kc->rnc", win_one, kernel2, preferred_element_type=jnp.float32)
    act_two, back_two = jax.vjp(layer_map(2, 1.0), preact2)
    frame_pos = device_place * rows_two + jnp.arange(rows_two, dtype=jnp.int32)
    valid = (frame_pos[None, :] < (lengths // 20)[:, None])[..., None]
    local_frames = jnp.where(valid, act_two, jnp.zeros_like(act_two)).astype(jnp.bfloat16)
    pooled = lax.all_gather(local_frames, "batch", axis=1, tiled=True)
    frames = lax.dynamic_slice_in_dim(pooled, lax.axis_index("batch"), 1, 0)
    pooled_cot = lax.all_gather(cotangent, "batch", axis=0, tiled=True)
    local_cot = lax.dynamic_slice_in_dim(
        pooled_cot, lax.axis_index("batch") * rows_two, rows_two, 1
    )
    upstream = jnp.where(valid, local_cot.astype(jnp.float32) * scale, jnp.zeros_like(act_two))
    dpre_two = back_two(upstream)[0].astype(jnp.bfloat16)
    grad_two = jnp.einsum("rnk,rnc->kc", win_one, dpre_two, preferred_element_type=jnp.float32)
    dwin = jnp.einsum("rnc,kc->rnk", dpre_two, kernel2, preferred_element_type=jnp.float32)
    paired = dwin[..., : 2 * channels].reshape(recordings, rows_two, 2, channels)
    third_tap = dwin[..., 2 * channels :]
    incoming = passed_along(third_tap[:, -1:], ("tm", "batch"), 1)
    lower = jnp.concatenate([incoming, third_tap[:, :-1]], 1)
    d_one = jnp.stack([paired[:, :, 0] + lower, paired[:, :, 1]], 2).reshape(
        recordings, rows_one, channels
    )
    dpre_one = back_one(d_one)[0].astype(jnp.bfloat16)
    grad_one = jnp.einsum("rnk,rnc->kc", win_zero, dpre_one, preferred_element_type=jnp.float32)
    stacked = jnp.concatenate([to_blocks(grad_one), to_blocks(grad_two)], 0)
    owned = lax.psum_scatter(stacked, "tm", scatter_dimension=0, tiled=True)
    owned = lax.psum(owned.astype(jnp.bfloat16), "batch").astype(jnp.float32)
    left_stat = BETA * left_prev + (1.0 - BETA) * jnp.einsum(
        "bik,bjk->bij", owned, owned, precision=lax.Precision.HIGHEST
    )
    right_stat = BETA * right_prev + (1.0 - BETA) * jnp.einsum(
        "bki,bkj->bij", owned, owned, precision=lax.Precision.HIGHEST
    )
    return (frames, left_stat, right_stat)


def solution(mesh):
    return jax.shard_map(
        body,
        mesh=mesh,
        in_specs=(
            P(None, ("tm", "batch")),
            P(),
            P(),
            P(),
            P(),
            P(),
            P(),
            P(),
            P("batch", "tm", None),
            P("tm", None, None),
            P("tm", None, None),
        ),
        out_specs=(P("batch", "tm", None), P("tm", None, None), P("tm", None, None)),
        check_vma=False,
    )
```

profile of v0, /device:TPU:0, one launch (start us, length us, event | category | flops | bytes accessed | tf_op | source)
XLA Modules:
  0.0 315.4 jit_solution(733642698864054999)
XLA Ops:
  13.4 2.9 add_reduce_fusion
  17.0 8.3 %fusion.2 = bf16[4,384,512]{2,1,0:T(8,128)(2,1)S(1)} fusion(f32[4,384,512]{2,1,0:T(8,128)S(1)} %get-tuple-element.21, f32[512]{0:T(512)S(1)} %bitcast.73, f32[512]{0:T(512)S(1)} %bitcast.72, f32[4,384]{1,0:T(4,128)S(1)} %add_rsqrt_fusion, f32[4,384]{1,0:T(4,128)S(1)} %broadcast_multiply_fusion, f32[512]{0:T(512)S(1)} %bitcast.71), kind=kLoop, calls=%fused_computation.6 | loop fusion | flops 55050240 | bytes 4737024 | tf_op jit(solution)/shard_map/convert_element_type | solution.py:98
  26.6 2.0 reshape.146
  31.3 9.4 %slice.69 = bf16[4,192,512]{2,1,0:T(8,128)(2,1)} slice(bf16[4,385,512]{2,1,0:T(8,128)(2,1)} %pad_maximum_fusion.2), slice={[0:4:1], [2:385:2], [0:512:1]} | slice | bytes 1572864 | tf_op jit(solution)/shard_map/slice | solution.py:42
  40.7 3.6 %add_reduce_fusion.1 = (f32[4,192]{1,0:T(4,128)S(1)}, f32[4,192,512]{2,1,0:T(8,128)S(1)}) fusion(f32[512]{0:T(512)S(1)} %bitcast.49, bf16[1536,512]{1,0:T(8,128)(2,1)} %param.14, bf16[4,192,512]{2,1,0:T(8,128)(2,1)} %slice.69, bf16[4,192,1024]{2,1,0:T(8,128)(2,1)} %reshape.146), kind=kOutput, calls=%fused_computation.58 | convolution fusion | flops 1213463808 | bytes 5510144 | tf_op jit(solution)/shard_map/rnk,kc->rnc/dot_general | solution.py:100
  44.7 4.9 %multiply_convert_fusion = (bf16[4,192,512]{2,1,0:T(8,128)(2,1)S(1)}, f32[4,192,512]{2,1,0:T(8,128)}) fusion(f32[512]{0:T(512)S(1)} %bitcast.59, f32[512]{0:T(512)S(1)} %bitcast.55, f32[4,192]{1,0:T(4,128)S(1)} %fusion.40, f32[4,192]{1,0:T(4,128)S(1)} %broadcast_multiply_fusion.1, f32[4,192,512]{2,1,0:T(8,128)S(1)} %get-tuple-element.23, f32[512]{0:T(512)S(1)} %bitcast.51), kind=kLoop, calls=%fused_computation.41 | loop fusion | flops 27525120 | bytes 3944448 | tf_op jit(solution)/shard_map/convert_element_type | solution.py:102
  52.7 2.1 reshape.147
  55.5 2.1 pad_maximum_fusion.7
  57.6 2.2 slice.74
  59.9 2.1 fusion.53
  63.3 3.7 %multiply_reduce_fusion.3 = (f32[4,96]{1,0:T(4,128)S(1)}, f32[4,96,512]{2,1,0:T(8,128)S(1)}) fusion(f32[4,96,512]{2,1,0:T(8,128)} %copy-done.4, f32[4,96]{1,0:T(4,128)S(1)} %broadcast_multiply_fusion.2, bf16[4,384,512]{2,1,0:T(8,128)(2,1)} %all-gather.5.cloned.1.call-done, s32[]{:T(128)S(6)} %select_n.26, pred[4,96]{1,0:T(4,128)(4,1)} %broadcast_compare_fusion, ...), kind=kLoop, calls=%fused_computation.71 | loop fusion | flops 15924864 | bytes 1975172 | tf_op jit(solution)/shard_map/transpose(jvp())/reduce_sum | solution.py:27
  67.0 1.8 fusion.34
  68.9 2.5 add_convert_fusion.2
  73.9 2.5 reshape.148
  76.4 3.4 %fusion.49 = (f32[4,96,1,512]{3,2,1,0:T(1,128)S(1)}, f32[4,96,1,512]{3,2,1,0:T(1,128)S(1)}) fusion(f32[4,96,2,512]{3,2,1,0:T(2,128)} %reshape.148), kind=kLoop, calls=%fused_computation.120 | loop fusion | bytes 3145728 | tf_op jit(solution)/shard_map/slice | solution.py:123
  79.8 4.9 %collective-permute-start.3 = (f32[4,1,512]{2,1,0:T(1,128)}, f32[4,1,512]{2,1,0:T(1,128)}, u32[]{:S(2)}, u32[]{:S(2)}) collective-permute-start(f32[4,1,512]{2,1,0:T(1,128)} %slice.88), channel_id=1, source_target_pairs={{0,1},{1,2},{2,3},{3,4},{4,5},{5,6},{6,7},{7,8},{8,9},{9,10},{10,1... | collective-permute-start | bytes 24584 | tf_op jit(solution)/shard_map/ppermute | solution.py:19
  84.7 2.7 convolution_bitcast_fusion.1
  88.3 4.9 %reshape.152 = f32[8,192,4,128]{3,2,1,0:T(4,128)} reshape(f32[1536,512]{1,0:T(8,128)} %convolution_bitcast_fusion.1) | data formatting | bytes 6291456 | tf_op jit(solution)/shard_map/reshape | solution.py:48
  93.2 4.0 %copy.30 = f32[8,4,192,128]{3,2,1,0:T(8,128)} copy(f32[8,4,192,128]{3,1,2,0:T(4,128)} %bitcast.45) | data formatting | bytes 6291456 | tf_op jit(solution)/shard_map/transpose | solution.py:49
  98.6 2.4 copy.28
  101.0 3.3 %reshape.149 = f32[4,192,512]{2,1,0:T(8,128)} reshape(f32[4,96,2,512]{3,2,1,0:T(2,128)} %copy.28) | data formatting | bytes 3145728 | tf_op jit(solution)/shard_map/reshape | solution.py:123
  104.3 2.8 multiply_reduce_fusion.1
  108.8 4.1 %convolution_bitcast_fusion = f32[1536,512]{1,0:T(8,128)} fusion(bf16[4,192,512]{2,1,0:T(8,128)(2,1)S(1)} %copy-done.13, bf16[4,192,1024]{2,1,0:T(8,128)(2,1)S(1)} %copy-done.11, f32[4,192]{1,0:T(4,128)S(1)} %negate_multiply_fusion.3, f32[4,192,512]{2,1,0:T(8,128)S(1)} %get-tuple-element.23, f32[4,192]{1,0:T(4,128)S(1)} %multiply_multiply_fusion.15, ...), kind=kOutput, calls=%fused_computation.2 | convolution fusion | flops 1222508544 | bytes 10242048 | tf_op jit(solution)/shard_map/rnk,rnc->kc/dot_general | solution.py:127
  112.9 5.0 %reshape.150 = f32[8,192,4,128]{3,2,1,0:T(4,128)} reshape(f32[1536,512]{1,0:T(8,128)} %convolution_bitcast_fusion) | data formatting | bytes 6291456 | tf_op jit(solution)/shard_map/reshape | solution.py:48
  117.9 2.5 copy.29
  120.7 3.1 pad_maximum_fusion
  124.6 123.8 %reduce-scatter.2.cloned.1.call-done = f32[8,192,128]{2,1,0:T(8,128)} async-done(((f32[64,192,128]{2,1,0:T(8,128)}), f32[8,192,128]{2,1,0:T(8,128)}) %reduce-scatter.2.cloned.1.call-update) | async-done | bytes 786448 | tf_op jit(solution)/shard_map/reduce_scatter | solution.py:129
  248.5 1.9 convert_element_type.28
  250.4 19.0 %all-gather.3.cloned.1.call-done = bf16[4,384,512]{2,1,0:T(8,128)(2,1)} async-done(((bf16[4,96,512]{2,1,0:T(8,128)(2,1)}), bf16[4,384,512]{2,1,0:T(8,128)(2,1)}) %all-gather.3.cloned.1.call-update) | async-done | bytes 1572880 | tf_op jit(solution)/shard_map/all_gather | solution.py:109
  269.4 1.8 constant_dynamic-slice_fusion
  271.2 33.6 %all-reduce.2.cloned.1.call-done = bf16[8,192,128]{2,1,0:T(8,128)(2,1)} async-done(((bf16[8,192,128]{2,1,0:T(8,128)(2,1)}), bf16[8,192,128]{2,1,0:T(8,128)(2,1)}) %all-reduce.2.cloned.1.call-update) | async-done | bytes 393232 | tf_op jit(solution)/shard_map/psum | solution.py:130
  304.9 2.8 multiply_add_fusion.1
  (125 shorter events, 25.0 us)
Async XLA Ops:
  7.2 52.7 %copy-start = (bf16[1536,512]{1,0:T(8,128)(2,1)S(1)}, bf16[1536,512]{1,0:T(8,128)(2,1)}, u32[]{:S(2)}) copy-start(bf16[1536,512]{1,0:T(8,128)(2,1)} %param.15) | copy-start | bytes 4718596
  7.2 4.0 %copy-start.30 = (f32[3,512]{1,0:T(4,128)S(1)}, f32[3,512]{1,0:T(4,128)}, u32[]{:S(2)}) copy-start(f32[3,512]{1,0:T(4,128)} %param.16) | copy-start | bytes 18436
  7.2 4.0 %copy-start.31 = (f32[3,512]{1,0:T(4,128)S(1)}, f32[3,512]{1,0:T(4,128)}, u32[]{:S(2)}) copy-start(f32[3,512]{1,0:T(4,128)} %param.17) | copy-start | bytes 18436
  7.2 4.6 %copy-start.32 = (f32[3,512]{1,0:T(4,128)S(1)}, f32[3,512]{1,0:T(4,128)}, u32[]{:S(2)}) copy-start(f32[3,512]{1,0:T(4,128)} %param.18) | copy-start | bytes 18436
  7.2 56.0 %all-gather.5.cloned.1.call-start = ((), (), s32[]{:S(2)}) async-start(), calls=%async_computation.2 | async-start | bytes 1966080 | tf_op jit(solution)/shard_map/all_gather | solution.py:111
  8.2 4.2 %collective-permute-start = (f32[4,5]{1,0:T(4,128)S(1)}, f32[4,5]{1,0:T(4,128)S(1)}, u32[]{:S(2)}, u32[]{:S(2)}) collective-permute-start(f32[4,5]{1,0:T(4,128)S(1)} %slice.83), channel_id=1, source_target_pairs={{1,0},{2,1},{3,2},{4,3},{5,4},{6,5},{7,6},{8,7},{9,8},{10,9},{11,1... | collective-permute-start | bytes 248 | tf_op jit(solution)/shard_map/ppermute | solution.py:19
  9.5 3.8 %copy-start.24 = (f32[10,512]{1,0:T(8,128)S(1)}, f32[10,512]{1,0:T(8,128)}, u32[]{:S(2)}) copy-start(f32[10,512]{1,0:T(8,128)} %param.13) | copy-start | bytes 61444
  9.5 238.9 %reduce-scatter.2.cloned.1.call-start = ((), (), s32[]{:S(2)}) async-start(), calls=%async_computation.3 | async-start | bytes 7077888 | tf_op jit(solution)/shard_map/reduce_scatter | solution.py:129
  11.8 32.9 %copy-start.20 = (f32[1,512]{1,0:T(1,128)}, f32[1,512]{1,0:T(1,128)S(1)}, u32[]{:S(2)}) copy-start(f32[1,512]{1,0:T(1,128)S(1)} %get-tuple-element.13) | copy-start | bytes 6148
  12.4 32.4 %copy-start.22 = (f32[1,512]{1,0:T(1,128)}, f32[1,512]{1,0:T(1,128)S(1)}, u32[]{:S(2)}) copy-start(f32[1,512]{1,0:T(1,128)S(1)} %get-tuple-element.16) | copy-start | bytes 6148
  25.3 4.6 %collective-permute-start.1 = (bf16[4,1,512]{2,1,0:T(2,128)(2,1)S(1)}, bf16[4,1,512]{2,1,0:T(2,128)(2,1)S(1)}, u32[]{:S(2)}, u32[]{:S(2)}) collective-permute-start(bf16[4,1,512]{2,1,0:T(2,128)(2,1)S(1)} %slice.84), channel_id=1, source_target_pairs={{1,0},{2,1},{3,2},{4,3},{5,4},{6,5},{7,6},{8,7},{9,8},{10,9},{11,1... | collective-permute-start | bytes 12296 | tf_op jit(solution)/shard_map/ppermute | solution.py:19
  44.7 4.9 %copy-start.18 = (f32[4,192]{1,0:T(4,128)}, f32[4,192]{1,0:T(4,128)S(1)}, u32[]{:S(2)}) copy-start(f32[4,192]{1,0:T(4,128)S(1)} %multiply_reduce_fusion.2) | copy-start | bytes 9220
  50.5 5.0 %collective-permute-start.2 = (bf16[4,1,512]{2,1,0:T(2,128)(2,1)S(1)}, bf16[4,1,512]{2,1,0:T(2,128)(2,1)S(1)}, u32[]{:S(2)}, u32[]{:S(2)}) collective-permute-start(bf16[4,1,512]{2,1,0:T(2,128)(2,1)S(1)} %slice.85), channel_id=1, source_target_pairs={{1,0},{2,1},{3,2},{4,3},{5,4},{6,5},{7,6},{8,7},{9,8},{10,9},{11,1... | collective-permute-start | bytes 12296 | tf_op jit(solution)/shard_map/ppermute | solution.py:19
  62.0 4.9 %copy-start.25 = (f32[1,512]{1,0:T(1,128)S(1)}, f32[1,512]{1,0:T(1,128)}, u32[]{:S(2)}) copy-start(f32[1,512]{1,0:T(1,128)} %get-tuple-element.11) | copy-start | bytes 6148
  62.1 4.9 %copy-start.27 = (f32[1,512]{1,0:T(1,128)S(1)}, f32[1,512]{1,0:T(1,128)}, u32[]{:S(2)}) copy-start(f32[1,512]{1,0:T(1,128)} %get-tuple-element.14) | copy-start | bytes 6148
  62.1 4.9 %copy-start.33 = (pred[4,96]{1,0:T(4,128)(4,1)S(1)}, pred[4,96]{1,0:T(4,128)(4,1)}, u32[]{:S(2)}) copy-start(pred[4,96]{1,0:T(4,128)(4,1)} %broadcast_compare_fusion) | copy-start | bytes 1156
  63.2 5.6 %copy-start.29 = (f32[4,96]{1,0:T(4,128)}, f32[4,96]{1,0:T(4,128)S(1)}, u32[]{:S(2)}) copy-start(f32[4,96]{1,0:T(4,128)S(1)} %fusion.41) | copy-start | bytes 4612
  63.2 3.8 %copy-start.5 = (f32[4,96,512]{2,1,0:T(8,128)S(1)}, f32[4,96,512]{2,1,0:T(8,128)}, u32[]{:S(2)}) copy-start(f32[4,96,512]{2,1,0:T(8,128)} %copy-done.4) | copy-start | bytes 2359300
  63.2 5.6 %copy-start.26 = (f32[1,512]{1,0:T(1,128)S(1)}, f32[1,512]{1,0:T(1,128)}, u32[]{:S(2)}) copy-start(f32[1,512]{1,0:T(1,128)} %get-tuple-element.11) | copy-start | bytes 6148
  63.2 5.6 %copy-start.28 = (f32[1,512]{1,0:T(1,128)S(1)}, f32[1,512]{1,0:T(1,128)}, u32[]{:S(2)}) copy-start(f32[1,512]{1,0:T(1,128)} %get-tuple-element.14) | copy-start | bytes 6148
  63.3 5.6 %copy-start.34 = (pred[4,96]{1,0:T(4,128)(4,1)S(1)}, pred[4,96]{1,0:T(4,128)(4,1)}, u32[]{:S(2)}) copy-start(pred[4,96]{1,0:T(4,128)(4,1)} %broadcast_compare_fusion) | copy-start | bytes 1156
  76.4 8.3 %copy-start.14 = (bf16[4,96,1024]{2,1,0:T(8,128)(2,1)S(1)}, bf16[4,96,1024]{2,1,0:T(8,128)(2,1)}, u32[]{:S(2)}) copy-start(bf16[4,96,1024]{2,1,0:T(8,128)(2,1)} %reshape.147) | copy-start | bytes 2359300
  76.4 8.3 %copy-start.17 = (bf16[4,96,512]{2,1,0:T(8,128)(2,1)S(1)}, bf16[4,96,512]{2,1,0:T(8,128)(2,1)}, u32[]{:S(2)}) copy-start(bf16[4,96,512]{2,1,0:T(8,128)(2,1)} %copy-done.16) | copy-start | bytes 1179652
  79.8 17.4 %collective-permute-start.3 = (f32[4,1,512]{2,1,0:T(1,128)}, f32[4,1,512]{2,1,0:T(1,128)}, u32[]{:S(2)}, u32[]{:S(2)}) collective-permute-start(f32[4,1,512]{2,1,0:T(1,128)} %slice.88), channel_id=1, source_target_pairs={{0,1},{1,2},{2,3},{3,4},{4,5},{5,6},{6,7},{7,8},{8,9},{9,10},{10,1... | collective-permute-start | bytes 24584 | tf_op jit(solution)/shard_map/ppermute | solution.py:19
  93.2 4.0 %copy-start.9 = (f32[4,95,1,512]{3,1,0,2:T(8,128)S(1)}, f32[4,95,1,512]{3,1,0,2:T(8,128)}, u32[]{:S(2)}) copy-start(f32[4,95,1,512]{3,1,0,2:T(8,128)} %slice_bitcast_fusion) | copy-start | bytes 2334724
  101.0 3.3 %copy-start.2 = (f32[4,192,512]{2,1,0:T(8,128)S(1)}, f32[4,192,512]{2,1,0:T(8,128)}, u32[]{:S(2)}) copy-start(f32[4,192,512]{2,1,0:T(8,128)} %get-tuple-element.6) | copy-start | bytes 4718596
  101.0 3.3 %copy-start.21 = (f32[1,512]{1,0:T(1,128)S(1)}, f32[1,512]{1,0:T(1,128)}, u32[]{:S(2)}) copy-start(f32[1,512]{1,0:T(1,128)} %copy-done.20) | copy-start | bytes 6148
  101.0 3.3 %copy-start.23 = (f32[1,512]{1,0:T(1,128)S(1)}, f32[1,512]{1,0:T(1,128)}, u32[]{:S(2)}) copy-start(f32[1,512]{1,0:T(1,128)} %copy-done.22) | copy-start | bytes 6148
  123.8 181.0 %copy-start.12 = (f32[8,192,192]{2,1,0:T(8,128)S(1)}, f32[8,192,192]{2,1,0:T(8,128)}, u32[]{:S(2)}) copy-start(f32[8,192,192]{2,1,0:T(8,128)} %param.20) | copy-start | bytes 3538948
  123.8 145.6 %all-gather.3.cloned.1.call-start = ((), (), s32[]{:S(2)}) async-start(), calls=%async_computation.1 | async-start | bytes 1966080 | tf_op jit(solution)/shard_map/all_gather | solution.py:109
  124.6 180.3 %all-reduce.2.cloned.1.call-start = ((), (), s32[]{:S(2)}) async-start(), calls=%async_computation.4 | async-start | bytes 786432 | tf_op jit(solution)/shard_map/psum | solution.py:130
  304.9 4.0 %copy-start.1 = (bf16[1536,512]{1,0:T(8,128)(2,1)S(1)}, bf16[1536,512]{1,0:T(8,128)(2,1)}, u32[]{:S(2)}) copy-start(bf16[1536,512]{1,0:T(8,128)(2,1)} %param.15) | copy-start | bytes 4718596
  (11 other events, 22.6 us)
Sparse Core Ops, SparseCore 0:
  9.6 23.1 all-gather.4
  124.0 124.4 reduce-scatter.1
  250.6 18.7 all-gather.2
  272.2 32.5 all-reduce.1
where the time goes:
time: 316 us; the launch traced here: 315 us
  waiting for transfers between devices  179 us (57%)
  local copies, waits for them, and re-layouts  53.5 us (17%)
  other arithmetic  38.9 us (12%)
  matrix products  20.2 us (6%)
  between operations  14.3 us (5%)
  starting transfers between devices  9.1 us (3%)
    reduce_scatter x1, waiting for transfers between devices, body(): owned = lax.psum_scatter(stacked, 'tm', scatter_dimension=0, tiled=True)  124 us
    psum x1, waiting for transfers between devices, body(): owned = lax.psum(owned.astype(jnp.bfloat16), 'batch').astype(jnp.float32)  33.6 us
    all_gather x1, waiting for transfers between devices, body(): pooled = lax.all_gather(local_frames, 'batch', axis=1, tiled=True)  19 us
    slice x2, local copies, waits for them, and re-layouts, frame_windows(): following = source[..., 2:2 * rows + 1:2, :]  11.6 us
    reshape x2, local copies, waits for them, and re-layouts, to_blocks(): split = gradient.reshape(rows_all // BR, BR, cols_all // BC, BC)  9.84 us
    ppermute x4, starting transfers between devices, passed_along(): return lax.ppermute(block, axis, route)  8.95 us
    convert_element_type x1, other arithmetic, body(): act_zero = layer_map(0, 1.0)(preact0).astype(jnp.bfloat16)  8.27 us
    reduce_sum x2, other arithmetic, norm_act(): normalized = centred * lax.rsqrt(spread + EPS)  6.49 us
  transfers between devices with their start and end apart: 8, of which 5 were waited for; matrix products, arithmetic and copies ran while one was open for 20% of the time, Pallas kernels for 0%

commit v1 on v0

v1 whole, which is shorter than its diff:
```python
import functools
import math

import jax
import jax.numpy as jnp
from jax import lax
from jax.experimental import pallas as pl
from jax.experimental.pallas import tpu as pltpu
from jax.sharding import PartitionSpec as P

BR = 192
BC = 128
EPS = 1e-05
BETA = 0.95
AXES = ("tm", "batch")
F32 = jnp.float32
BF16 = jnp.bfloat16
VMEM_LIMIT = 50 * 1024 * 1024
CH = 16
TAIL = 16

VM = pl.BlockSpec(memory_space=pltpu.VMEM)
SM = pl.BlockSpec(memory_space=pltpu.SMEM)


def params():
    return pltpu.CompilerParams(vmem_limit_bytes=VMEM_LIMIT)


def cost(flops, nbytes, trans=0):
    return pl.CostEstimate(flops=flops, bytes_accessed=nbytes, transcendentals=trans)


def sds(shape, dtype):
    return jax.ShapeDtypeStruct(shape, dtype)


def normal_cdf(z):
    bell = jnp.exp(z * z * -0.5)
    t = 1.0 / (1.0 + jnp.abs(z) * (0.3275911 / math.sqrt(2.0)))
    poly = t * (0.5 * 1.061405429) + (0.5 * -1.453152027)
    poly = poly * t + (0.5 * 1.421413741)
    poly = poly * t + (0.5 * -0.284496736)
    poly = poly * t + (0.5 * 0.254829592)
    q = poly * t * bell
    return jnp.where(z < 0.0, q, 1.0 - q), bell


INV_SQRT_2PI = 1.0 / math.sqrt(2.0 * math.pi)


def split3(x):
    hi = x.astype(BF16).astype(F32)
    rest = x - hi
    mid = rest.astype(BF16).astype(F32)
    return hi, mid, rest - mid


def prep_kernel(k0_ref, bias_ref, w_ref, wide):
    channels = k0_ref.shape[1]
    k0 = k0_ref[...]
    k0 = k0 - jnp.mean(k0, -1, keepdims=True)
    bias = bias_ref[0:1, :]
    bias = bias - jnp.mean(bias, -1, keepdims=True)
    parts = split3(k0)
    bparts = split3(bias)
    wide[...] = jnp.zeros_like(wide)
    for block, part in enumerate((0, 1, 2, 0, 1, 0)):
        for g in range(4):
            cols = pl.ds(g * channels, channels)
            wide[pl.ds(block * 32 + 5 * g, 10), cols] = parts[part]
            if block < 3:
                wide[pl.ds(block * 32 + 31, 1), cols] = bparts[part]
    w_ref[...] = wide[...].astype(BF16)


def prep(kernel0, conv_bias):
    channels = kernel0.shape[1]
    return pl.pallas_call(
        prep_kernel,
        out_shape=sds((256, 4 * channels), BF16),
        in_specs=[VM, VM],
        out_specs=VM,
        scratch_shapes=[pltpu.VMEM((256, 4 * channels), F32)],
        compiler_params=params(),
        cost_estimate=cost(4 * 256 * 2048, 1 << 20),
        name="prep",
    )(kernel0, conv_bias)


def dot(a, b):
    return lax.dot_general(a, b, (((1,), (0,)), ((), ())), preferred_element_type=F32)


def dot_tn(a, b):
    return lax.dot_general(a, b, (((0,), (0,)), ((), ())), preferred_element_type=F32)


def dot_nt(a, b):
    return lax.dot_general(a, b, (((1,), (1,)), ((), ())), preferred_element_type=F32)


def put_gradient(core, keep_ref, send_ref, pairs, chunk):
    half = keep_ref.shape[-1] * 2
    width = keep_ref.shape[-1]
    for which, out in ((core, keep_ref), (1 - core, send_ref)):
        start = pl.multiple_of(which * half, half)
        for row in range(keep_ref.shape[1]):
            total = None
            for a_ref, offset, d_ref in pairs:
                groups = d_ref.shape[0]
                a = a_ref[0:groups, offset + row * chunk : offset + (row + 1) * chunk]
                piece = dot_tn(a, d_ref[:, pl.ds(start, half)])
                total = piece if total is None else total + piece
            out[0, row] = total[:, :width].astype(out.dtype)
            out[1, row] = total[:, width:].astype(out.dtype)


def forward_kernel(
    groups,
    scale,
    info,
    p0,
    p1,
    p2,
    p3,
    edge_ref,
    w0_ref,
    k1_ref,
    k2_ref,
    bias_ref,
    gain_ref,
    shift_ref,
    cot_ref,
    cotprev_ref,
    frames_ref,
    keep_ref,
    send_ref,
    a0_ref,
    hat_ref,
    slope_ref,
    rstd_ref,
    d2_ref,
    samples,
    pre0,
    pre1,
    pre2,
    a1_ref,
    ahead,
    cotall,
    d2own,
):
    rows = groups + TAIL
    channels = k1_ref.shape[1]
    length = info[0]
    base = info[1]
    total = info[2]
    me = info[3]
    core = info[4]
    count = rows // CH
    is_last = base + groups >= total

    samples[...] = jnp.zeros_like(samples)
    piece_rows = p0.shape[0]
    for k, piece in enumerate((p0, p1, p2, p3)):
        place = pl.multiple_of((me ^ k) * piece_rows, 8)
        samples[pl.ds(place, piece_rows), 0:20] = piece[...]
    samples[groups : groups + 1, 0:20] = edge_ref[0:1, :]
    samples[rows - 1 : rows, 0:20] = edge_ref[1:2, :]
    row = lax.broadcasted_iota(jnp.int32, (rows, 128), 0)
    lane = lax.broadcasted_iota(jnp.int32, (rows, 128), 1)
    group = base + jnp.where(row == rows - 1, -1, row)
    s = jnp.where((group * 20 + lane < length) & (lane < 20), samples[...], 0.0)
    after = pltpu.roll(pltpu.roll(s, rows - 1, 0), 20, 1)
    s = jnp.where(lane < 20, s, jnp.where(lane < 25, after, jnp.where(lane == 31, 1.0, 0.0)))
    hi, mid, low = split3(s)
    first = hi + pltpu.roll(hi, 32, 1) + pltpu.roll(hi, 64, 1) + pltpu.roll(mid, 96, 1)
    second = mid + pltpu.roll(low, 32, 1)
    x6 = jnp.concatenate([first.astype(BF16), second.astype(BF16)], 1)
    pre0[...] = dot(x6, w0_ref[...])

    gain0 = gain_ref[0:1, :]
    shift0 = shift_ref[0:1, :]

    def step0(i, carry):
        at = pl.ds(pl.multiple_of(i * CH, CH), CH)
        for g in range(4):
            cols = pl.ds(g * channels, channels)
            x = pre0[at, cols]
            rstd = lax.rsqrt(jnp.mean(x * x, -1, keepdims=True) + EPS)
            z = x * rstd * gain0 + shift0
            cdf, _ = normal_cdf(z)
            act = z * cdf
            a0_ref[at, cols] = act.astype(BF16)
            if g == 0:
                ahead[at, :] = act
        return carry

    lax.fori_loop(0, count, step0, 0)

    tail_row = lax.broadcasted_iota(jnp.int32, (TAIL, channels), 0)
    drop = (tail_row == 0) & is_last

    def shifted(target, offset):
        ahead[groups:rows, :] = jnp.where(drop, 0.0, ahead[groups:rows, :])
        ahead[rows : rows + 1, :] = ahead[0:1, :]

        def move(i, carry):
            at = pl.multiple_of(i * CH, CH)
            block = ahead[pl.ds(at, CH + 8), :]
            target[pl.ds(at, CH), offset : offset + channels] = block[1 : CH + 1, :].astype(BF16)
            return carry

        lax.fori_loop(0, count, move, 0)

    shifted(a0_ref, 4 * channels)
    for g in range(3):
        cols = pl.ds(g * channels, channels)
        tail = a0_ref[groups:rows, cols].astype(F32)
        a0_ref[groups:rows, cols] = jnp.where(drop, 0.0, tail).astype(BF16)

    for h in range(2):
        pre1[h] = dot(a0_ref[:, 2 * h * channels : (2 * h + 3) * channels], k1_ref[...])
    bias1 = bias_ref[1:2, :]
    gain1 = gain_ref[1:2, :]
    shift1 = shift_ref[1:2, :]

    def step1(i, carry):
        at = pl.ds(pl.multiple_of(i * CH, CH), CH)
        for h in range(2):
            x = pre1[h, at, :] + bias1
            x = x - jnp.mean(x, -1, keepdims=True)
            rstd = lax.rsqrt(jnp.mean(x * x, -1, keepdims=True) + EPS)
            hat = x * rstd
            z = hat * gain1 + shift1
            cdf, bell = normal_cdf(z)
            act = z * cdf
            hat_ref[h, at, :] = hat
            slope_ref[h, at, :] = (cdf + z * bell * INV_SQRT_2PI) * gain1
            rstd_ref[h, at, :] = jnp.broadcast_to(rstd, (CH, 128))
            a1_ref[at, h * channels : (h + 1) * channels] = act.astype(BF16)
            if h == 0:
                ahead[at, :] = act
        return carry

    lax.fori_loop(0, count, step1, 0)
    shifted(a1_ref, 2 * channels)

    pre2[...] = dot(a1_ref[...], k2_ref[...])
    cotall[0:groups, :] = cot_ref[...].astype(F32)
    cotall[groups:rows, :] = jnp.where(
        tail_row == TAIL - 1, cotprev_ref[...].astype(F32), 0.0
    )
    bias2 = bias_ref[2:3, :]
    gain2 = gain_ref[2:3, :]
    shift2 = shift_ref[2:3, :]
    limit = length // 20

    def step2(i, carry):
        start = pl.multiple_of(i * CH, CH)
        at = pl.ds(start, CH)
        x = pre2[at, :] + bias2
        x = x - jnp.mean(x, -1, keepdims=True)
        rstd = lax.rsqrt(jnp.mean(x * x, -1, keepdims=True) + EPS)
        hat = x * rstd
        z = hat * gain2 + shift2
        cdf, bell = normal_cdf(z)
        place = start + lax.broadcasted_iota(jnp.int32, (CH, channels), 0)
        place = base + jnp.where(place == rows - 1, -1, place)
        valid = place < limit
        frames_all = jnp.where(valid, z * cdf, 0.0).astype(BF16)
        up = jnp.where(valid, cotall[at, :] * scale, 0.0)
        dhat = up * ((cdf + z * bell * INV_SQRT_2PI) * gain2)
        mean_d = jnp.mean(dhat, -1, keepdims=True)
        mean_dh = jnp.mean(dhat * hat, -1, keepdims=True)
        d2_ref[at, :] = (rstd * (dhat - mean_d - hat * mean_dh)).astype(BF16)

        @pl.when(i < groups // CH)
        def _():
            frames_ref[at, :] = frames_all

        return carry

    lax.fori_loop(0, count, step2, 0)
    d2own[...] = d2_ref[0:groups, :]
    chunk = keep_ref.shape[2]
    put_gradient(core, keep_ref, send_ref, [(a1_ref, 0, d2own)], chunk)


def forward(info, pieces, edges, w0, kernel1, kernel2, bias, gain, shift, cot, cotprev, scale, chunks):
    groups = cot.shape[0]
    channels = cot.shape[1]
    rows = groups + TAIL
    taps = kernel1.shape[0]
    grad = (2, chunks, taps // chunks, BC)
    return pl.pallas_call(
        functools.partial(forward_kernel, groups, scale),
        out_shape=[
            sds((groups, channels), BF16),
            sds(grad, F32),
            sds(grad, BF16),
            sds((rows, 5 * channels), BF16),
            sds((2, rows, channels), F32),
            sds((2, rows, channels), F32),
            sds((2, rows, 128), F32),
            sds((rows, channels), BF16),
        ],
        in_specs=[SM] + [VM] * 13,
        out_specs=[VM] * 8,
        scratch_shapes=[
            pltpu.VMEM((rows, 128), F32),
            pltpu.VMEM((rows, 4 * channels), F32),
            pltpu.VMEM((2, rows, channels), F32),
            pltpu.VMEM((rows, channels), F32),
            pltpu.VMEM((rows, 3 * channels), BF16),
            pltpu.VMEM((rows + 8, channels), F32),
            pltpu.VMEM((rows, channels), F32),
            pltpu.VMEM((groups, channels), BF16),
        ],
        compiler_params=params(),
        cost_estimate=cost(int(8e9), 10 << 20),
        name="forward",
    )(info, *pieces, edges, w0, kernel1, kernel2, bias, gain, shift, cot, cotprev)


def backward_kernel(
    groups,
    info,
    d2_ref,
    k2_ref,
    a0_ref,
    hat_ref,
    slope_ref,
    rstd_ref,
    keep_ref,
    send_ref,
    dwin,
    behind,
    d1,
):
    rows = groups + TAIL
    channels = d2_ref.shape[1]
    core = info[4]
    d2 = d2_ref[...]
    dwin[0] = dot_nt(d2[0:groups, :], k2_ref[0:channels, :])
    dwin[1] = dot_nt(d2[0:groups, :], k2_ref[channels : 2 * channels, :])
    third = dot_nt(d2, k2_ref[2 * channels : 3 * channels, :])
    behind[8 : 8 + groups, :] = third[0:groups, :]
    behind[7:8, :] = third[rows - 1 : rows, :]

    def step(i, carry):
        start = pl.multiple_of(i * CH, CH)
        at = pl.ds(start, CH)
        for h in range(2):
            d = dwin[h, at, :]
            if h == 0:
                d = d + behind[pl.ds(start, CH + 8), :][7 : 7 + CH, :]
            hat = hat_ref[h, at, :]
            dhat = d * slope_ref[h, at, :]
            mean_d = jnp.mean(dhat, -1, keepdims=True)
            mean_dh = jnp.mean(dhat * hat, -1, keepdims=True)
            rstd = rstd_ref[h, at, 0:1]
            d1[h, at, :] = (rstd * (dhat - mean_d - hat * mean_dh)).astype(BF16)
        return carry

    lax.fori_loop(0, groups // CH, step, 0)
    chunk = keep_ref.shape[2]
    put_gradient(
        core, keep_ref, send_ref, [(a0_ref, 0, d1.at[0]), (a0_ref, 2 * channels, d1.at[1])], chunk
    )


def backward(info, d2, kernel2, a0, hat, slope, rstd, chunks):
    rows, channels = d2.shape
    groups = rows - TAIL
    grad = (2, chunks, kernel2.shape[0] // chunks, BC)
    return pl.pallas_call(
        functools.partial(backward_kernel, groups),
        out_shape=[sds(grad, F32), sds(grad, BF16)],
        in_specs=[SM] + [VM] * 6,
        out_specs=[VM] * 2,
        scratch_shapes=[
            pltpu.VMEM((2, groups, channels), F32),
            pltpu.VMEM((groups + 8, channels), F32),
            pltpu.VMEM((2, groups, channels), BF16),
        ],
        compiler_params=params(),
        cost_estimate=cost(int(5e9), 10 << 20),
        name="backward",
    )(info, d2, kernel2, a0, hat, slope, rstd)


def plane_kernel(info, keep_ref, recv_ref, own_ref, tox_ref, toy_ref, tod_ref):
    x, y = info[5], info[6]
    for dx, dy, out in ((0, 0, own_ref), (1, 0, tox_ref), (0, 1, toy_ref), (1, 1, tod_ref)):
        for zz in range(2):
            at = (x ^ dx, 2 * zz + (y ^ dy))
            out[zz] = (keep_ref[at] + recv_ref[at].astype(F32)).astype(out.dtype)


def plane(info, keep, recv):
    shape = (2,) + keep.shape[2:]
    return pl.pallas_call(
        plane_kernel,
        out_shape=[sds(shape, F32)] + [sds(shape, BF16)] * 3,
        in_specs=[SM, VM, VM],
        out_specs=[VM] * 4,
        compiler_params=params(),
        cost_estimate=cost(1 << 20, 5 << 20),
        name="plane",
    )(info, keep, recv)


def column_kernel(info, *refs):
    ins, outs = refs[:8], refs[8:]
    z = info[7]
    for dz, out in enumerate(outs):
        zz = z ^ dz
        for layer in range(2):

            @pl.when(zz // 2 == layer)
            def _():
                own, rx, ry, rd = ins[4 * layer : 4 * layer + 4]
                at = zz % 2
                total = own[at] + rx[at].astype(F32) + ry[at].astype(F32) + rd[at].astype(F32)
                out[...] = total.astype(out.dtype)


def column(info, first, second):
    shape = first[0].shape[1:]
    return pl.pallas_call(
        column_kernel,
        out_shape=[sds(shape, F32)] + [sds(shape, BF16)] * 3,
        in_specs=[SM] + [VM] * 8,
        out_specs=[VM] * 4,
        compiler_params=params(),
        cost_estimate=cost(1 << 20, 3 << 20),
        name="column",
    )(info, *first, *second)


def final_kernel(own, a, b, c, out):
    total = own[...] + a[...].astype(F32) + b[...].astype(F32) + c[...].astype(F32)
    out[...] = total.astype(out.dtype)


def final(own, a, b, c):
    return pl.pallas_call(
        final_kernel,
        out_shape=sds(own.shape, BF16),
        in_specs=[VM] * 4,
        out_specs=VM,
        compiler_params=params(),
        cost_estimate=cost(1 << 18, 1 << 19),
        name="final",
    )(own, a, b, c)


def stats_kernel(info, own, other, pair, lprev, rprev, left, right):
    core, x = info[4], info[5]
    for piece, v in (
        (own, 2 * core + x),
        (other, 2 * core + 1 - x),
        (pair.at[0], 2 * (1 - core) + x),
        (pair.at[1], 2 * (1 - core) + 1 - x),
    ):
        for u in range(2):
            block = piece[u * BR : (u + 1) * BR, :]
            q = 4 * u + v
            left[q] = BETA * lprev[q] + (1.0 - BETA) * dot_nt(block, block)
            right[q] = BETA * rprev[q] + (1.0 - BETA) * dot_tn(block, block)


def stats(info, own, other, pair, lprev, rprev):
    return pl.pallas_call(
        stats_kernel,
        out_shape=[sds(lprev.shape, F32), sds(rprev.shape, F32)],
        in_specs=[SM] + [VM] * 5,
        out_specs=[VM] * 2,
        compiler_params=params(),
        cost_estimate=cost(int(2e8), 4 << 20),
        name="stats",
    )(info, own, other, pair, lprev, rprev)


def permute(value, route):
    return lax.ppermute(value, AXES, route)


def body(
    audio,
    lengths,
    kernel0,
    kernel1,
    kernel2,
    conv_bias,
    norm_gain,
    norm_shift,
    cotangent,
    left_prev,
    right_prev,
):
    tms, batches = lax.axis_size("tm"), lax.axis_size("batch")
    t, b = lax.axis_index("tm"), lax.axis_index("batch")
    recordings, samples_dev = audio.shape
    piece_rows = samples_dev // 20
    groups = piece_rows * batches
    total = groups * tms
    scale = 1.0 / math.sqrt(total)

    def route(move):
        pairs = []
        for tt in range(tms):
            for bb in range(batches):
                to = move(tt, bb)
                if 0 <= to[0] < tms:
                    pairs.append((tt * batches + bb, to[0] * batches + to[1]))
        return pairs

    info = jnp.stack(
        [
            lax.dynamic_index_in_dim(lengths, b, 0, False),
            t * groups,
            jnp.int32(total),
            b,
            b % 2,
            b // 2,
            t % 2,
            t // 2,
        ]
    ).astype(jnp.int32)

    grouped = audio.reshape(recordings, piece_rows, 20)
    pieces = []
    for k in range(batches):
        piece = lax.dynamic_index_in_dim(grouped, b ^ k, 0, False)
        if k:
            piece = permute(piece, route(lambda tt, bb: (tt, bb ^ k)))
        pieces.append(piece)

    def of_place(place, row):
        chosen = pieces[0][row]
        for k in range(1, batches):
            chosen = jnp.where((b ^ k) == place, pieces[k][row], chosen)
        return chosen[None]

    following = permute(of_place(0, 0), route(lambda tt, bb: (tt - 1, bb)))
    preceding = permute(of_place(batches - 1, piece_rows - 1), route(lambda tt, bb: (tt + 1, bb)))
    edges = jnp.concatenate([following, preceding], 0)
    cot = cotangent[0]
    cotprev = permute(cot[groups - 1 :], route(lambda tt, bb: (tt + 1, bb)))

    w0 = prep(kernel0, conv_bias)
    special = tms == 8 and batches == 4
    chunks = 4
    if not special:
        info = info.at[4].set(0)
    frames, keep2, send2, a0, hat, slope, rstd, d2 = forward(
        info,
        pieces,
        edges,
        w0,
        kernel1,
        kernel2,
        conv_bias,
        norm_gain,
        norm_shift,
        cot,
        cotprev,
        scale,
        chunks,
    )
    keep1, send1 = backward(info, d2, kernel2, a0, hat, slope, rstd, chunks)

    if not special:

        def blocks_of(keep, send):
            both = jnp.stack([keep, send.astype(F32)])
            both = both.reshape(2, 2, -1, BR, BC)
            return jnp.transpose(both, (2, 0, 1, 3, 4)).reshape(-1, BR, BC)

        stacked = jnp.concatenate([blocks_of(keep1, send1), blocks_of(keep2, send2)], 0)
        owned = lax.psum_scatter(stacked, "tm", scatter_dimension=0, tiled=True)
        owned = lax.psum(owned, "batch")
        left = BETA * left_prev + (1.0 - BETA) * jnp.einsum(
            "bik,bjk->bij", owned, owned, precision=lax.Precision.HIGHEST
        )
        right = BETA * right_prev + (1.0 - BETA) * jnp.einsum(
            "bki,bkj->bij", owned, owned, precision=lax.Precision.HIGHEST
        )
        return frames[None], left, right

    by_core = route(lambda tt, bb: (tt, bb ^ 1))
    by_x = route(lambda tt, bb: (tt, bb ^ 2))
    by_y = route(lambda tt, bb: (tt ^ 1, bb))
    by_xy = route(lambda tt, bb: (tt ^ 1, bb ^ 2))
    by_z = [route(lambda tt, bb: (tt ^ (2 * k), bb)) for k in range(1, 4)]

    def plane_sums(keep, send):
        own, tox, toy, tod = plane(info, keep, permute(send, by_core))
        return own, permute(tox, by_x), permute(toy, by_y), permute(tod, by_xy)

    second = plane_sums(keep2, send2)
    first = plane_sums(keep1, send1)
    own, *out = column(info, first, second)
    arrived = [permute(value, way) for value, way in zip(out, by_z)]
    owned = final(own, *arrived)
    other = permute(owned, by_x)
    pair = permute(jnp.stack([owned, other]), by_core)
    left, right = stats(info, owned, other, pair, left_prev, right_prev)
    return frames[None], left, right


def solution(mesh):
    return jax.shard_map(
        body,
        mesh=mesh,
        in_specs=(
            P(None, AXES),
            P(),
            P(),
            P(),
            P(),
            P(),
            P(),
            P(),
            P("batch", "tm", None),
            P("tm", None, None),
            P("tm", None, None),
        ),
        out_specs=(P("batch", "tm", None), P("tm", None, None), P("tm", None, None)),
        check_vma=False,
    )
```

time: 316 us -> 102 us (0.32)
  waiting for transfers between devices: 179 us -> 24.3 us
  local copies, waits for them, and re-layouts: 53.5 us -> 5.2 us
  Pallas kernels: 0 us -> 41.1 us
  other arithmetic: 38.9 us -> 0.05 us
  starting transfers between devices: 9.1 us -> 30.1 us
  matrix products: 20.2 us -> 0 us
  between operations: 14.3 us -> 0.94 us
    reduce_scatter x1 -> x0, waiting for transfers between devices: 124 us -> none  [body(): owned = lax.psum_scatter(stacked, 'tm', scatter_dimension=0, tiled=True)]
    pallas_call x0 -> x8, Pallas kernels: none -> 41.1 us  [the longest x1 27.7 us: forward(): pl.pallas_call(functools.partial(forward_kernel, groups, scale), out_shap...]
    psum x1 -> x0, waiting for transfers between devices: 33.6 us -> none  [body(): owned = lax.psum(owned.astype(jnp.bfloat16), 'batch').astype(jnp.float32)]
    ppermute x4 -> x19, waiting for transfers between devices: 2.07 us -> 24.3 us  [permute(): return lax.ppermute(value, AXES, route)]
    ppermute x4 -> x19, starting transfers between devices: 8.95 us -> 30.1 us  [permute(): return lax.ppermute(value, AXES, route)]
    reshape x10 -> x1, local copies, waits for them, and re-layouts: 21.5 us -> 1.01 us  [body(): grouped = audio.reshape(recordings, piece_rows, 20)]
    dot_general x8 -> x0, matrix products: 20.2 us -> none  [the longest x1 4.14 us: body(): jnp.einsum('rnk,rnc->kc', win_zero, dpre_one, preferred_element_type=jnp....]
    all_gather x2 -> x0, waiting for transfers between devices: 19 us -> none  [the longest x1 19 us: body(): pooled = lax.all_gather(local_frames, 'batch', axis=1, tiled=True)]
  transfers between devices with their start and end apart: 8 -> 19, of which waited for: 5 -> 10; matrix products, arithmetic and copies ran while one was open for 20% -> 3% of each run, Pallas kernels for 0% -> 10%
where the time goes in v1:
time: 102 us
  Pallas kernels  41.1 us (40%)
  starting transfers between devices  30.1 us (30%)
  waiting for transfers between devices  24.3 us (24%)
  local copies, waits for them, and re-layouts  5.2 us (5%)
    ppermute x19, starting transfers between devices, permute(): return lax.ppermute(value, AXES, route)  30.1 us
    pallas_call x1, Pallas kernels, forward(): pl.pallas_call(functools.partial(forward_kernel, groups, scale), out_shap...  27.7 us
    ppermute x19, waiting for transfers between devices, permute(): return lax.ppermute(value, AXES, route)  24.3 us
    pallas_call x1, Pallas kernels, backward(): pl.pallas_call(functools.partial(backward_kernel, groups), out_shape=[sds...  8.54 us
    pallas_call x1, Pallas kernels, stats(): pl.pallas_call(stats_kernel, out_shape=[sds(lprev.shape, F32), sds(rprev....  2.43 us
  transfers between devices with their start and end apart: 19, of which 10 were waited for; matrix products, arithmetic and copies ran while one was open for 3% of the time, Pallas kernels for 10%

profile of v1, /device:TPU:0, one launch (start us, length us, event | category | flops | bytes accessed | tf_op | source)
XLA Modules:
  0.0 101.6 jit_solution(15859745217320359037)
XLA Ops:
  0.7 1.0 reshape.16
  1.7 2.4 %collective-permute-start.2 = (f32[96,20]{1,0:T(8,128)S(1)}, f32[96,20]{1,0:T(8,128)S(1)}, u32[]{:S(2)}, u32[]{:S(2)}) collective-permute-start(f32[96,20]{1,0:T(8,128)S(1)} %get-tuple-element.53), channel_id=1, source_target_pairs={{0,3},{1,2},{2,1},{3,0},{4,7},{5,6},{6,5},{7,4},{8,11},{9,10},{10,... | collective-permute-start | bytes 23048 | tf_op jit(solution)/shard_map/ppermute | solution.py:487
  4.9 0.7 slice_bitcast_fusion
  5.6 3.7 %collective-permute-start.5 = (bf16[1,512]{1,0:T(2,128)(2,1)S(1)}, bf16[1,512]{1,0:T(2,128)(2,1)S(1)}, u32[]{:S(2)}, u32[]{:S(2)}) collective-permute-start(bf16[1,512]{1,0:T(2,128)(2,1)S(1)} %slice_bitcast_fusion), channel_id=1, source_target_pairs={{0,4},{1,5},{2,6},{3,7},{4,8},{5,9},{6,10},{7,11},{8,12},{9,13},{1... | collective-permute-start | bytes 3080 | tf_op jit(solution)/shard_map/ppermute | solution.py:487
  9.3 1.2 %dynamic_slice.17 = s32[1]{0:T(128)} dynamic-slice(s32[4]{0:T(128)} %param.12, s32[]{:T(128)S(6)} %select_n.77), dynamic_slice_sizes={1} | dynamic-slice | bytes 12 | tf_op jit(solution)/shard_map/jit(dynamic_index_in_dim)/dynamic_slice | solution.py:522
  10.5 0.7 stack.37.info
  11.3 0.8 copy-done.3
  12.0 0.7 copy-done.4
  13.0 1.3 %collective-permute-start.3 = (f32[1,20]{1,0:T(1,128)S(1)}, f32[1,20]{1,0:T(1,128)S(1)}, u32[]{:S(2)}, u32[]{:S(2)}) collective-permute-start(f32[1,20]{1,0:T(1,128)S(1)} %get-tuple-element.51), channel_id=1, source_target_pairs={{4,0},{5,1},{6,2},{7,3},{8,4},{9,5},{10,6},{11,7},{12,8},{13,9},{1... | collective-permute-start | bytes 248 | tf_op jit(solution)/shard_map/ppermute | solution.py:487
  14.3 4.5 %collective-permute-start.4 = (f32[1,20]{1,0:T(1,128)S(1)}, f32[1,20]{1,0:T(1,128)S(1)}, u32[]{:S(2)}, u32[]{:S(2)}) collective-permute-start(f32[1,20]{1,0:T(1,128)S(1)} %get-tuple-element.52), channel_id=1, source_target_pairs={{0,4},{1,5},{2,6},{3,7},{4,8},{5,9},{6,10},{7,11},{8,12},{9,13},{1... | collective-permute-start | bytes 248 | tf_op jit(solution)/shard_map/ppermute | solution.py:487
  18.8 1.3 %collective-permute-done.4 = f32[1,20]{1,0:T(1,128)S(1)} collective-permute-done((f32[1,20]{1,0:T(1,128)S(1)}, f32[1,20]{1,0:T(1,128)S(1)}, u32[]{:S(2)}, u32[]{:S(2)}) %collective-permute-start.4) | collective-permute-done | bytes 112 | tf_op jit(solution)/shard_map/ppermute | solution.py:487
  20.2 27.7 %forward.1 = (bf16[384,512]{1,0:T(8,128)(2,1)}, f32[2,4,384,128]{3,2,1,0:T(8,128)}, bf16[2,4,384,128]{3,2,1,0:T(8,128)(2,1)S(1)}, bf16[400,2560]{1,0:T(8,128)(2,...) custom-call(s32[8]{0:T(128)S(1)} %stack.37.info, ...), custom_call_target="tpu_custom_call" | custom-call | flops 8000000000 | bytes 10485760 | tf_op jit(solution)/shard_map/forward/pallas_call | solution.py:296
  47.9 8.5 %backward.1 = (f32[2,4,384,128]{3,2,1,0:T(8,128)S(1)}, bf16[2,4,384,128]{3,2,1,0:T(8,128)(2,1)S(1)}) custom-call(s32[8]{0:T(128)S(1)} %stack.37.info, bf16[400,512]{1,0:T(8,128)(2,1)S(1)} %get-tuple-element.28.d2_ref, bf16[1536,512]{1,0:T(8,128)(2,1)} %k2_ref.3, bf16[400,2560]{1,0:T(8,128)(2,1)} %get-tuple-element.29.a0_ref, ...), custom_call_target="tpu_custom_call" | custom-call | flops 5000000000 | bytes 10485760 | tf_op jit(solution)/shard_map/backward/pallas_call | solution.py:377
  57.0 0.7 plane.3
  57.7 1.6 %collective-permute-start.11 = (bf16[2,384,128]{2,1,0:T(8,128)(2,1)S(1)}, bf16[2,384,128]{2,1,0:T(8,128)(2,1)S(1)}, u32[]{:S(2)}, u32[]{:S(2)}) collective-permute-start(bf16[2,384,128]{2,1,0:T(8,128)(2,1)S(1)} %get-tuple-element.42), channel_id=1, source_target_pairs={{0,2},{1,3},{2,0},{3,1},{4,6},{5,7},{6,4},{7,5},{8,10},{9,11},{10,... | collective-permute-start | bytes 589832 | tf_op jit(solution)/shard_map/ppermute | solution.py:487
  59.3 2.4 %collective-permute-start.12 = (bf16[2,384,128]{2,1,0:T(8,128)(2,1)S(1)}, bf16[2,384,128]{2,1,0:T(8,128)(2,1)S(1)}, u32[]{:S(2)}, u32[]{:S(2)}) collective-permute-start(bf16[2,384,128]{2,1,0:T(8,128)(2,1)S(1)} %get-tuple-element.43), channel_id=1, source_target_pairs={{0,4},{1,5},{2,6},{3,7},{4,0},{5,1},{6,2},{7,3},{8,12},{9,13},{10,... | collective-permute-start | bytes 589832 | tf_op jit(solution)/shard_map/ppermute | solution.py:487
  61.7 0.7 plane.2
  62.4 1.5 %collective-permute-start.7 = (bf16[2,384,128]{2,1,0:T(8,128)(2,1)S(1)}, bf16[2,384,128]{2,1,0:T(8,128)(2,1)S(1)}, u32[]{:S(2)}, u32[]{:S(2)}) collective-permute-start(bf16[2,384,128]{2,1,0:T(8,128)(2,1)S(1)} %get-tuple-element.36), channel_id=1, source_target_pairs={{0,2},{1,3},{2,0},{3,1},{4,6},{5,7},{6,4},{7,5},{8,10},{9,11},{10,... | collective-permute-start | bytes 589832 | tf_op jit(solution)/shard_map/ppermute | solution.py:487
  63.9 2.0 %collective-permute-start.8 = (bf16[2,384,128]{2,1,0:T(8,128)(2,1)S(1)}, bf16[2,384,128]{2,1,0:T(8,128)(2,1)S(1)}, u32[]{:S(2)}, u32[]{:S(2)}) collective-permute-start(bf16[2,384,128]{2,1,0:T(8,128)(2,1)S(1)} %get-tuple-element.37), channel_id=1, source_target_pairs={{0,4},{1,5},{2,6},{3,7},{4,0},{5,1},{6,2},{7,3},{8,12},{9,13},{10,... | collective-permute-start | bytes 589832 | tf_op jit(solution)/shard_map/ppermute | solution.py:487
  65.9 2.9 %collective-permute-start.9 = (bf16[2,384,128]{2,1,0:T(8,128)(2,1)S(1)}, bf16[2,384,128]{2,1,0:T(8,128)(2,1)S(1)}, u32[]{:S(2)}, u32[]{:S(2)}) collective-permute-start(bf16[2,384,128]{2,1,0:T(8,128)(2,1)S(1)} %get-tuple-element.38), channel_id=1, source_target_pairs={{0,6},{1,7},{2,4},{3,5},{4,2},{5,3},{6,0},{7,1},{8,14},{9,15},{10,... | collective-permute-start | bytes 589832 | tf_op jit(solution)/shard_map/ppermute | solution.py:487
  68.9 2.5 %collective-permute-done.12.refs_6_ = bf16[2,384,128]{2,1,0:T(8,128)(2,1)S(1)} collective-permute-done((bf16[2,384,128]{2,1,0:T(8,128)(2,1)S(1)}, bf16[2,384,128]{2,1,0:T(8,128)(2,1)S(1)}, u32[]{:S(2)}, u32[]{:S(2)}) %collective-permute-start.12) | collective-permute-done | bytes 196640 | tf_op jit(solution)/shard_map/ppermute | solution.py:487
  71.6 2.4 %collective-permute-done.7.refs_1_ = bf16[2,384,128]{2,1,0:T(8,128)(2,1)S(1)} collective-permute-done((bf16[2,384,128]{2,1,0:T(8,128)(2,1)S(1)}, bf16[2,384,128]{2,1,0:T(8,128)(2,1)S(1)}, u32[]{:S(2)}, u32[]{:S(2)}) %collective-permute-start.7) | collective-permute-done | bytes 196640 | tf_op jit(solution)/shard_map/ppermute | solution.py:487
  74.0 4.4 %collective-permute-done.8.refs_2_ = bf16[2,384,128]{2,1,0:T(8,128)(2,1)S(1)} collective-permute-done((bf16[2,384,128]{2,1,0:T(8,128)(2,1)S(1)}, bf16[2,384,128]{2,1,0:T(8,128)(2,1)S(1)}, u32[]{:S(2)}, u32[]{:S(2)}) %collective-permute-start.8) | collective-permute-done | bytes 196640 | tf_op jit(solution)/shard_map/ppermute | solution.py:487
  78.4 0.8 collective-permute-done.9.refs_3_
  79.1 0.8 column.1
  79.9 3.5 %collective-permute-start.14 = (bf16[384,128]{1,0:T(8,128)(2,1)S(1)}, bf16[384,128]{1,0:T(8,128)(2,1)S(1)}, u32[]{:S(2)}, u32[]{:S(2)}) collective-permute-start(bf16[384,128]{1,0:T(8,128)(2,1)S(1)} %get-tuple-element.46), channel_id=1, source_target_pairs={{0,8},{1,9},{2,10},{3,11},{4,12},{5,13},{6,14},{7,15},{8,0},{9,1},... | collective-permute-start | bytes 294920 | tf_op jit(solution)/shard_map/ppermute | solution.py:487
  83.4 2.6 %collective-permute-start.15 = (bf16[384,128]{1,0:T(8,128)(2,1)S(1)}, bf16[384,128]{1,0:T(8,128)(2,1)S(1)}, u32[]{:S(2)}, u32[]{:S(2)}) collective-permute-start(bf16[384,128]{1,0:T(8,128)(2,1)S(1)} %get-tuple-element.47), channel_id=1, source_target_pairs={{0,16},{1,17},{2,18},{3,19},{4,20},{5,21},{6,22},{7,23},{8,24},{9,... | collective-permute-start | bytes 294920 | tf_op jit(solution)/shard_map/ppermute | solution.py:487
  86.0 1.0 collective-permute-done.14.a
  87.0 5.9 %collective-permute-done.15.b = bf16[384,128]{1,0:T(8,128)(2,1)S(1)} collective-permute-done((bf16[384,128]{1,0:T(8,128)(2,1)S(1)}, bf16[384,128]{1,0:T(8,128)(2,1)S(1)}, u32[]{:S(2)}, u32[]{:S(2)}) %collective-permute-start.15) | collective-permute-done | bytes 98336 | tf_op jit(solution)/shard_map/ppermute | solution.py:487
  93.2 4.4 %collective-permute-done.17.other = bf16[384,128]{1,0:T(8,128)(2,1)S(1)} collective-permute-done((bf16[384,128]{1,0:T(8,128)(2,1)S(1)}, bf16[384,128]{1,0:T(8,128)(2,1)S(1)}, u32[]{:S(2)}, u32[]{:S(2)}) %collective-permute-start.17) | collective-permute-done | bytes 98336 | tf_op jit(solution)/shard_map/ppermute | solution.py:487
  97.7 1.4 %collective-permute-done.18.pair = bf16[2,384,128]{2,1,0:T(8,128)(2,1)S(1)} collective-permute-done((bf16[2,384,128]{2,1,0:T(8,128)(2,1)S(1)}, bf16[2,384,128]{2,1,0:T(8,128)(2,1)S(1)}, u32[]{:S(2)}, u32[]{:S(2)}) %collective-permute-start.18) | collective-permute-done | bytes 196640 | tf_op jit(solution)/shard_map/ppermute | solution.py:487
  99.1 2.4 %stats.1 = (f32[8,192,192]{2,1,0:T(8,128)}, f32[8,128,128]{2,1,0:T(8,128)}) custom-call(s32[8]{0:T(128)S(1)} %stack.37.info, bf16[384,128]{1,0:T(8,128)(2,1)S(1)} %final.1.own, bf16[384,128]{1,0:T(8,128)(2,1)S(1)} %collective-permute-done.17.other, bf16[2,384,128]{2,1,0:T(8,128)(2,1)S(1)} %collective-permute-done.18.pair, f32[8,192,192]{2,1,0:T(8,128)S(1)} %copy-done.1, ...), custom_call_target="tpu_custom_call" | custom-call | flops 200000000 | bytes 4194304 | tf_op jit(solution)/shard_map/stats/pallas_call | solution.py:475
  (38 shorter events, 2.2 us)
Async XLA Ops:
  0.6 19.5 %copy-start.5 = (bf16[1,384,512]{2,1,0:T(8,128)(2,1)S(1)}, bf16[1,384,512]{2,1,0:T(8,128)(2,1)}, u32[]{:S(2)}) copy-start(bf16[1,384,512]{2,1,0:T(8,128)(2,1)} %param.19) | copy-start | bytes 1179652
  0.6 19.5 %copy-start.7 = (f32[3,512]{1,0:T(4,128)S(1)}, f32[3,512]{1,0:T(4,128)}, u32[]{:S(2)}) copy-start(f32[3,512]{1,0:T(4,128)} %shift_ref.1) | copy-start | bytes 18436
  0.7 19.5 %copy-start.6 = (f32[3,512]{1,0:T(4,128)S(1)}, f32[3,512]{1,0:T(4,128)}, u32[]{:S(2)}) copy-start(f32[3,512]{1,0:T(4,128)} %gain_ref.1) | copy-start | bytes 18436
  1.7 11.2 %collective-permute-start.2 = (f32[96,20]{1,0:T(8,128)S(1)}, f32[96,20]{1,0:T(8,128)S(1)}, u32[]{:S(2)}, u32[]{:S(2)}) collective-permute-start(f32[96,20]{1,0:T(8,128)S(1)} %get-tuple-element.53), channel_id=1, source_target_pairs={{0,3},{1,2},{2,1},{3,0},{4,7},{5,6},{6,5},{7,4},{8,11},{9,10},{10,... | collective-permute-start | bytes 23048 | tf_op jit(solution)/shard_map/ppermute | solution.py:487
  4.2 8.7 %collective-permute-start.1 = (f32[96,20]{1,0:T(8,128)S(1)}, f32[96,20]{1,0:T(8,128)S(1)}, u32[]{:S(2)}, u32[]{:S(2)}) collective-permute-start(f32[96,20]{1,0:T(8,128)S(1)} %get-tuple-element.54), channel_id=1, source_target_pairs={{0,2},{1,3},{2,0},{3,1},{4,6},{5,7},{6,4},{7,5},{8,10},{9,11},{10,... | collective-permute-start | bytes 23048 | tf_op jit(solution)/shard_map/ppermute | solution.py:487
  4.8 8.1 %collective-permute-start = (f32[96,20]{1,0:T(8,128)S(1)}, f32[96,20]{1,0:T(8,128)S(1)}, u32[]{:S(2)}, u32[]{:S(2)}) collective-permute-start(f32[96,20]{1,0:T(8,128)S(1)} %get-tuple-element.55), channel_id=1, source_target_pairs={{0,1},{1,0},{2,3},{3,2},{4,5},{5,4},{6,7},{7,6},{8,9},{9,8},{10,11... | collective-permute-start | bytes 23048 | tf_op jit(solution)/shard_map/ppermute | solution.py:487
  5.6 14.5 %collective-permute-start.5 = (bf16[1,512]{1,0:T(2,128)(2,1)S(1)}, bf16[1,512]{1,0:T(2,128)(2,1)S(1)}, u32[]{:S(2)}, u32[]{:S(2)}) collective-permute-start(bf16[1,512]{1,0:T(2,128)(2,1)S(1)} %slice_bitcast_fusion), channel_id=1, source_target_pairs={{0,4},{1,5},{2,6},{3,7},{4,8},{5,9},{6,10},{7,11},{8,12},{9,13},{1... | collective-permute-start | bytes 3080 | tf_op jit(solution)/shard_map/ppermute | solution.py:487
  11.3 0.8 copy-start.3
  12.0 0.7 copy-start.4
  13.0 5.9 %collective-permute-start.3 = (f32[1,20]{1,0:T(1,128)S(1)}, f32[1,20]{1,0:T(1,128)S(1)}, u32[]{:S(2)}, u32[]{:S(2)}) collective-permute-start(f32[1,20]{1,0:T(1,128)S(1)} %get-tuple-element.51), channel_id=1, source_target_pairs={{4,0},{5,1},{6,2},{7,3},{8,4},{9,5},{10,6},{11,7},{12,8},{13,9},{1... | collective-permute-start | bytes 248 | tf_op jit(solution)/shard_map/ppermute | solution.py:487
  14.3 5.8 %collective-permute-start.4 = (f32[1,20]{1,0:T(1,128)S(1)}, f32[1,20]{1,0:T(1,128)S(1)}, u32[]{:S(2)}, u32[]{:S(2)}) collective-permute-start(f32[1,20]{1,0:T(1,128)S(1)} %get-tuple-element.52), channel_id=1, source_target_pairs={{0,4},{1,5},{2,6},{3,7},{4,8},{5,9},{6,10},{7,11},{8,12},{9,13},{1... | collective-permute-start | bytes 248 | tf_op jit(solution)/shard_map/ppermute | solution.py:487
  47.9 9.1 %collective-permute-start.10 = (bf16[2,4,384,128]{3,2,1,0:T(8,128)(2,1)S(1)}, bf16[2,4,384,128]{3,2,1,0:T(8,128)(2,1)S(1)}, u32[]{:S(2)}, u32[]{:S(2)}) collective-permute-start(bf16[2,4,384,128]{3,2,1,0:T(8,128)(2,1)S(1)} %get-tuple-element.40), channel_id=1, source_target_pairs={{0,1},{1,0},{2,3},{3,2},{4,5},{5,4},{6,7},{7,6},{8,9},{9,8},{10,11... | collective-permute-start | bytes 2359304 | tf_op jit(solution)/shard_map/ppermute | solution.py:487
  47.9 9.1 %copy-start = (f32[2,4,384,128]{3,2,1,0:T(8,128)S(1)}, f32[2,4,384,128]{3,2,1,0:T(8,128)}, u32[]{:S(2)}) copy-start(f32[2,4,384,128]{3,2,1,0:T(8,128)} %get-tuple-element.39.keep_ref) | copy-start | bytes 4718596
  56.4 5.2 %collective-permute-start.6 = (bf16[2,4,384,128]{3,2,1,0:T(8,128)(2,1)S(1)}, bf16[2,4,384,128]{3,2,1,0:T(8,128)(2,1)S(1)}, u32[]{:S(2)}, u32[]{:S(2)}) collective-permute-start(bf16[2,4,384,128]{3,2,1,0:T(8,128)(2,1)S(1)} %get-tuple-element.34), channel_id=1, source_target_pairs={{0,1},{1,0},{2,3},{3,2},{4,5},{5,4},{6,7},{7,6},{8,9},{9,8},{10,11... | collective-permute-start | bytes 2359304 | tf_op jit(solution)/shard_map/ppermute | solution.py:487
  57.7 8.2 %collective-permute-start.11 = (bf16[2,384,128]{2,1,0:T(8,128)(2,1)S(1)}, bf16[2,384,128]{2,1,0:T(8,128)(2,1)S(1)}, u32[]{:S(2)}, u32[]{:S(2)}) collective-permute-start(bf16[2,384,128]{2,1,0:T(8,128)(2,1)S(1)} %get-tuple-element.42), channel_id=1, source_target_pairs={{0,2},{1,3},{2,0},{3,1},{4,6},{5,7},{6,4},{7,5},{8,10},{9,11},{10,... | collective-permute-start | bytes 589832 | tf_op jit(solution)/shard_map/ppermute | solution.py:487
  59.3 12.1 %collective-permute-start.12 = (bf16[2,384,128]{2,1,0:T(8,128)(2,1)S(1)}, bf16[2,384,128]{2,1,0:T(8,128)(2,1)S(1)}, u32[]{:S(2)}, u32[]{:S(2)}) collective-permute-start(bf16[2,384,128]{2,1,0:T(8,128)(2,1)S(1)} %get-tuple-element.43), channel_id=1, source_target_pairs={{0,4},{1,5},{2,6},{3,7},{4,0},{5,1},{6,2},{7,3},{8,12},{9,13},{10,... | collective-permute-start | bytes 589832 | tf_op jit(solution)/shard_map/ppermute | solution.py:487
  61.7 10.0 %collective-permute-start.13 = (bf16[2,384,128]{2,1,0:T(8,128)(2,1)S(1)}, bf16[2,384,128]{2,1,0:T(8,128)(2,1)S(1)}, u32[]{:S(2)}, u32[]{:S(2)}) collective-permute-start(bf16[2,384,128]{2,1,0:T(8,128)(2,1)S(1)} %get-tuple-element.44), channel_id=1, source_target_pairs={{0,6},{1,7},{2,4},{3,5},{4,2},{5,3},{6,0},{7,1},{8,14},{9,15},{10,... | collective-permute-start | bytes 589832 | tf_op jit(solution)/shard_map/ppermute | solution.py:487
  62.4 36.8 %copy-start.1 = (f32[8,192,192]{2,1,0:T(8,128)S(1)}, f32[8,192,192]{2,1,0:T(8,128)}, u32[]{:S(2)}) copy-start(f32[8,192,192]{2,1,0:T(8,128)} %lprev.1) | copy-start | bytes 3538948
  62.4 36.8 %copy-start.2 = (f32[8,128,128]{2,1,0:T(8,128)S(1)}, f32[8,128,128]{2,1,0:T(8,128)}, u32[]{:S(2)}) copy-start(f32[8,128,128]{2,1,0:T(8,128)} %rprev.1) | copy-start | bytes 1572868
  62.4 11.6 %collective-permute-start.7 = (bf16[2,384,128]{2,1,0:T(8,128)(2,1)S(1)}, bf16[2,384,128]{2,1,0:T(8,128)(2,1)S(1)}, u32[]{:S(2)}, u32[]{:S(2)}) collective-permute-start(bf16[2,384,128]{2,1,0:T(8,128)(2,1)S(1)} %get-tuple-element.36), channel_id=1, source_target_pairs={{0,2},{1,3},{2,0},{3,1},{4,6},{5,7},{6,4},{7,5},{8,10},{9,11},{10,... | collective-permute-start | bytes 589832 | tf_op jit(solution)/shard_map/ppermute | solution.py:487
  63.9 14.5 %collective-permute-start.8 = (bf16[2,384,128]{2,1,0:T(8,128)(2,1)S(1)}, bf16[2,384,128]{2,1,0:T(8,128)(2,1)S(1)}, u32[]{:S(2)}, u32[]{:S(2)}) collective-permute-start(bf16[2,384,128]{2,1,0:T(8,128)(2,1)S(1)} %get-tuple-element.37), channel_id=1, source_target_pairs={{0,4},{1,5},{2,6},{3,7},{4,0},{5,1},{6,2},{7,3},{8,12},{9,13},{10,... | collective-permute-start | bytes 589832 | tf_op jit(solution)/shard_map/ppermute | solution.py:487
  65.9 13.2 %collective-permute-start.9 = (bf16[2,384,128]{2,1,0:T(8,128)(2,1)S(1)}, bf16[2,384,128]{2,1,0:T(8,128)(2,1)S(1)}, u32[]{:S(2)}, u32[]{:S(2)}) collective-permute-start(bf16[2,384,128]{2,1,0:T(8,128)(2,1)S(1)} %get-tuple-element.38), channel_id=1, source_target_pairs={{0,6},{1,7},{2,4},{3,5},{4,2},{5,3},{6,0},{7,1},{8,14},{9,15},{10,... | collective-permute-start | bytes 589832 | tf_op jit(solution)/shard_map/ppermute | solution.py:487
  79.9 7.1 %collective-permute-start.14 = (bf16[384,128]{1,0:T(8,128)(2,1)S(1)}, bf16[384,128]{1,0:T(8,128)(2,1)S(1)}, u32[]{:S(2)}, u32[]{:S(2)}) collective-permute-start(bf16[384,128]{1,0:T(8,128)(2,1)S(1)} %get-tuple-element.46), channel_id=1, source_target_pairs={{0,8},{1,9},{2,10},{3,11},{4,12},{5,13},{6,14},{7,15},{8,0},{9,1},... | collective-permute-start | bytes 294920 | tf_op jit(solution)/shard_map/ppermute | solution.py:487
  83.4 9.5 %collective-permute-start.15 = (bf16[384,128]{1,0:T(8,128)(2,1)S(1)}, bf16[384,128]{1,0:T(8,128)(2,1)S(1)}, u32[]{:S(2)}, u32[]{:S(2)}) collective-permute-start(bf16[384,128]{1,0:T(8,128)(2,1)S(1)} %get-tuple-element.47), channel_id=1, source_target_pairs={{0,16},{1,17},{2,18},{3,19},{4,20},{5,21},{6,22},{7,23},{8,24},{9,... | collective-permute-start | bytes 294920 | tf_op jit(solution)/shard_map/ppermute | solution.py:487
  86.0 6.9 %collective-permute-start.16 = (bf16[384,128]{1,0:T(8,128)(2,1)S(1)}, bf16[384,128]{1,0:T(8,128)(2,1)S(1)}, u32[]{:S(2)}, u32[]{:S(2)}) collective-permute-start(bf16[384,128]{1,0:T(8,128)(2,1)S(1)} %get-tuple-element.48), channel_id=1, source_target_pairs={{0,24},{1,25},{2,26},{3,27},{4,28},{5,29},{6,30},{7,31},{8,16},{9,... | collective-permute-start | bytes 294920 | tf_op jit(solution)/shard_map/ppermute | solution.py:487
  92.9 4.7 %collective-permute-start.17 = (bf16[384,128]{1,0:T(8,128)(2,1)S(1)}, bf16[384,128]{1,0:T(8,128)(2,1)S(1)}, u32[]{:S(2)}, u32[]{:S(2)}) collective-permute-start(bf16[384,128]{1,0:T(8,128)(2,1)S(1)} %final.1.own), channel_id=1, source_target_pairs={{0,2},{1,3},{2,0},{3,1},{4,6},{5,7},{6,4},{7,5},{8,10},{9,11},{10,... | collective-permute-start | bytes 294920 | tf_op jit(solution)/shard_map/ppermute | solution.py:487
  97.6 1.5 %collective-permute-start.18 = (bf16[2,384,128]{2,1,0:T(8,128)(2,1)S(1)}, bf16[2,384,128]{2,1,0:T(8,128)(2,1)S(1)}, u32[]{:S(2)}, u32[]{:S(2)}) collective-permute-start(bf16[2,384,128]{2,1,0:T(8,128)(2,1)S(1)} %pad_maximum_fusion), channel_id=1, source_target_pairs={{0,1},{1,0},{2,3},{3,2},{4,5},{5,4},{6,7},{7,6},{8,9},{9,8},{10,11... | collective-permute-start | bytes 589832 | tf_op jit(solution)/shard_map/ppermute | solution.py:487

commit v2 on v1

v2 whole, which is shorter than its diff:
```python
import functools
import math

import jax
import jax.numpy as jnp
from jax import lax
from jax.experimental import pallas as pl
from jax.experimental.pallas import tpu as pltpu
from jax.sharding import PartitionSpec as P

BR = 192
BC = 128
EPS = 1e-05
BETA = 0.95
AXES = ("tm", "batch")
F32 = jnp.float32
BF16 = jnp.bfloat16
MIB = 1024 * 1024
CH = 16
CH0, CH1, CH2, CH3 = 16,16,16,16
UN0, UN1, UN2, UN3 = 4,25,6,6
TAIL = 16

VM = pl.BlockSpec(memory_space=pltpu.VMEM)
SM = pl.BlockSpec(memory_space=pltpu.SMEM)


def params(mib=12):
    return pltpu.CompilerParams(vmem_limit_bytes=mib * MIB)


def cost(flops, nbytes, trans=0):
    return pl.CostEstimate(flops=flops, bytes_accessed=nbytes, transcendentals=trans)


def sds(shape, dtype):
    return jax.ShapeDtypeStruct(shape, dtype)


def normal_cdf(z):
    bell = jnp.exp(z * z * -0.5)
    t = 1.0 / (1.0 + jnp.abs(z) * (0.3275911 / math.sqrt(2.0)))
    poly = t * (0.5 * 1.061405429) + (0.5 * -1.453152027)
    poly = poly * t + (0.5 * 1.421413741)
    poly = poly * t + (0.5 * -0.284496736)
    poly = poly * t + (0.5 * 0.254829592)
    q = poly * t * bell
    return jnp.where(z < 0.0, q, 1.0 - q), bell


INV_SQRT_2PI = 1.0 / math.sqrt(2.0 * math.pi)


def split3(x):
    hi = x.astype(BF16).astype(F32)
    rest = x - hi
    mid = rest.astype(BF16).astype(F32)
    return hi, mid, rest - mid


def prep_kernel(k0_ref, bias_ref, w_ref, wide):
    channels = k0_ref.shape[1]
    k0 = k0_ref[...]
    k0 = k0 - jnp.mean(k0, -1, keepdims=True)
    bias = bias_ref[0:1, :]
    bias = bias - jnp.mean(bias, -1, keepdims=True)
    parts = split3(k0)
    bparts = split3(bias)
    wide[...] = jnp.zeros_like(wide)
    for block, part in enumerate((0, 1, 2, 0, 1, 0)):
        for g in range(4):
            cols = pl.ds(g * channels, channels)
            wide[pl.ds(block * 32 + 5 * g, 10), cols] = parts[part]
            if block < 3:
                wide[pl.ds(block * 32 + 31, 1), cols] = bparts[part]
    w_ref[...] = wide[...].astype(BF16)


def prep(kernel0, conv_bias):
    channels = kernel0.shape[1]
    return pl.pallas_call(
        prep_kernel,
        out_shape=sds((256, 4 * channels), BF16),
        in_specs=[VM, VM],
        out_specs=VM,
        scratch_shapes=[pltpu.VMEM((256, 4 * channels), F32)],
        compiler_params=params(),
        cost_estimate=cost(4 * 256 * 2048, 1 << 20),
        name="prep",
    )(kernel0, conv_bias)


def dot(a, b):
    return lax.dot_general(a, b, (((1,), (0,)), ((), ())), preferred_element_type=F32)


def dot_tn(a, b):
    return lax.dot_general(a, b, (((0,), (0,)), ((), ())), preferred_element_type=F32)


def dot_nt(a, b):
    return lax.dot_general(a, b, (((1,), (1,)), ((), ())), preferred_element_type=F32)


def put_gradient(core, keep_ref, send_ref, pairs, chunk):
    half = keep_ref.shape[-1] * 2
    width = keep_ref.shape[-1]
    for which, out in ((core, keep_ref), (1 - core, send_ref)):
        start = pl.multiple_of(which * half, half)
        for row in range(keep_ref.shape[1]):
            total = None
            for a_ref, offset, d_ref in pairs:
                groups = d_ref.shape[0]
                a = a_ref[0:groups, offset + row * chunk : offset + (row + 1) * chunk]
                piece = dot_tn(a, d_ref[:, pl.ds(start, half)])
                total = piece if total is None else total + piece
            out[0, row] = total[:, :width].astype(out.dtype)
            out[1, row] = total[:, width:].astype(out.dtype)


class Place:
    def __init__(self, special):
        t, b = lax.axis_index("tm"), lax.axis_index("batch")
        self.t, self.b = t, b
        self.core = lax.rem(b, 2) if special else 0
        self.x, self.y, self.z = lax.div(b, 2), lax.rem(t, 2), lax.div(t, 2)


def layer_zero(pre, at, gain0, shift0, channels, g):
    x = pre[at, pl.ds(g * channels, channels)]
    rstd = lax.rsqrt(jnp.mean(x * x, -1, keepdims=True) + EPS)
    z = x * rstd * gain0 + shift0
    cdf, _ = normal_cdf(z)
    return z * cdf


def taps(block, after):
    lane = lax.broadcasted_iota(jnp.int32, block.shape, 1)
    after = pltpu.roll(after, 20, 1)
    s = jnp.where(
        lane < 20, block, jnp.where(lane < 25, after, jnp.where(lane == 31, 1.0, 0.0))
    )
    hi, mid, low = split3(s)
    first = hi + pltpu.roll(hi, 32, 1) + pltpu.roll(hi, 64, 1) + pltpu.roll(mid, 96, 1)
    second = mid + pltpu.roll(low, 32, 1)
    return jnp.concatenate([first.astype(BF16), second.astype(BF16)], 1)


def move_up(source, target, offset, rows):
    channels = source.shape[1]

    def move(i, carry):
        at = pl.multiple_of(i * CH, CH)
        block = source[pl.ds(at, CH + 8), :]
        target[pl.ds(at, CH), offset : offset + channels] = block[1 : CH + 1, :].astype(BF16)
        return carry

    lax.fori_loop(0, rows // CH, move, 0, unroll=2)


def audio_kernel(
    special, lengths, p0, p1, p2, p3, w0_ref, gain_ref, shift_ref, a0_ref, head_ref, keep, samples, pre0, ahead
):
    here = Place(special)
    piece_rows = p0.shape[0]
    groups = 4 * piece_rows
    channels = gain_ref.shape[1]
    length = lengths[here.b]
    base = here.t * groups
    samples[...] = jnp.zeros_like(samples)
    for k, piece in enumerate((p0, p1, p2, p3)):
        place = pl.multiple_of((here.b ^ k) * piece_rows, 8)
        samples[pl.ds(place, piece_rows), 0:20] = piece[...]
    row = lax.broadcasted_iota(jnp.int32, (groups, 128), 0)
    lane = lax.broadcasted_iota(jnp.int32, (groups, 128), 1)
    s = jnp.where(((base + row) * 20 + lane < length) & (lane < 20), samples[...], 0.0)
    keep[0:8, :] = s[0:8]
    keep[8 : 8 + TAIL, :] = s[groups - TAIL :]
    pre0[...] = dot(taps(s, pltpu.roll(s, groups - 1, 0)), w0_ref[...])
    gain0 = gain_ref[0:1, :]
    shift0 = shift_ref[0:1, :]

    def step(i, carry):
        at = pl.ds(pl.multiple_of(i * CH0, CH0), CH0)
        for g in range(4):
            act = layer_zero(pre0, at, gain0, shift0, channels, g)
            a0_ref[at, pl.ds(g * channels, channels)] = act.astype(BF16)
            if g == 0:
                ahead[at, :] = act
        return carry

    lax.fori_loop(0, groups // CH0, step, 0, unroll=UN0)
    head_ref[...] = ahead[0:8, :]
    move_up(ahead, a0_ref, 4 * channels, groups)


def audio_layer(lengths, pieces, w0, gain, shift, special):
    groups = 4 * pieces[0].shape[0]
    channels = gain.shape[1]
    return pl.pallas_call(
        functools.partial(audio_kernel, special),
        out_shape=[
            sds((groups, 5 * channels), BF16),
            sds((8, channels), F32),
            sds((8 + TAIL, 128), F32),
        ],
        in_specs=[SM] + [VM] * 7,
        out_specs=[VM] * 3,
        scratch_shapes=[
            pltpu.VMEM((groups, 128), F32),
            pltpu.VMEM((groups, 4 * channels), F32),
            pltpu.VMEM((groups + 8, channels), F32),
        ],
        compiler_params=params(16),
        cost_estimate=cost(int(3e9), 5 << 20),
        name="audio_layer",
    )(lengths, *pieces, w0, gain, shift)


def forward_kernel(
    special,
    groups,
    scale,
    lengths,
    a0_in,
    head_in,
    kept,
    edge_a,
    edge_b,
    w0_ref,
    k1_ref,
    k2_ref,
    bias_ref,
    gain_ref,
    shift_ref,
    cot_ref,
    a0_ref,
    frames_ref,
    keep_ref,
    send_ref,
    hat_ref,
    slope_ref,
    rstd_ref,
    d2_ref,
    pre0,
    pre1,
    pre2,
    a1_ref,
    ahead,
    d2own,
):
    here = Place(special)
    rows = groups + TAIL
    channels = k1_ref.shape[1]
    length = lengths[here.b]
    base = here.t * groups
    total = groups * lax.axis_size("tm")
    is_last = base + groups >= total
    odd = lax.rem(here.t, 2) == 1

    following = jnp.where(odd, edge_b[...], edge_a[...])
    preceding = jnp.where(odd, edge_a[...], edge_b[...])
    row = lax.broadcasted_iota(jnp.int32, (TAIL, 128), 0)
    lane = lax.broadcasted_iota(jnp.int32, (TAIL, 128), 1)
    group = base + jnp.where(row == TAIL - 1, -1, groups + row)
    tail = jnp.where(row == 0, following[:, :128], jnp.where(row == TAIL - 1, preceding[:, :128], 0.0))
    tail = jnp.where((group * 20 + lane < length) & (lane < 20), tail, 0.0)
    block = jnp.concatenate([kept[8 : 8 + TAIL, :], tail], 0)
    row = lax.broadcasted_iota(jnp.int32, (2 * TAIL, 128), 0)
    after = jnp.where(row == 2 * TAIL - 1, kept[0:1, :], pltpu.roll(block, 2 * TAIL - 1, 0))
    pre0[...] = dot(taps(block, after), w0_ref[...])
    tail_row = lax.broadcasted_iota(jnp.int32, (TAIL, channels), 0)
    drop = (tail_row == 0) & is_last
    gain0 = gain_ref[0:1, :]
    shift0 = shift_ref[0:1, :]
    a0_ref[0:groups, :] = a0_in[...]
    for g in range(4):
        cols = pl.ds(g * channels, channels)
        start = TAIL if g in (1, 2) else 0
        act = layer_zero(pre0, pl.ds(start, 2 * TAIL - start), gain0, shift0, channels, g)
        behind, act = act[: TAIL - start], act[TAIL - start :]
        act = jnp.where(drop, 0.0, act)
        a0_ref[groups:rows, cols] = act.astype(BF16)
        if g == 3:
            a0_ref[groups - TAIL : groups, cols] = behind.astype(BF16)
        if g == 0:
            both = jnp.concatenate([behind, act], 0)
            up_row = lax.broadcasted_iota(jnp.int32, both.shape, 0)
            up = jnp.where(
                up_row == 2 * TAIL - 1, head_in[0:1, :], pltpu.roll(both, 2 * TAIL - 1, 0)
            )
            a0_ref[groups - TAIL : rows, 4 * channels : 5 * channels] = up.astype(BF16)

    for h in range(2):
        pre1[h] = dot(a0_ref[:, 2 * h * channels : (2 * h + 3) * channels], k1_ref[...])
    bias1 = bias_ref[1:2, :]
    gain1 = gain_ref[1:2, :]
    shift1 = shift_ref[1:2, :]

    def step1(i, carry):
        at = pl.ds(pl.multiple_of(i * CH1, CH1), CH1)
        for h in range(2):
            x = pre1[h, at, :] + bias1
            x = x - jnp.mean(x, -1, keepdims=True)
            rstd = lax.rsqrt(jnp.mean(x * x, -1, keepdims=True) + EPS)
            hat = x * rstd
            z = hat * gain1 + shift1
            cdf, bell = normal_cdf(z)
            act = z * cdf
            hat_ref[h, at, :] = hat
            slope_ref[h, at, :] = (cdf + z * bell * INV_SQRT_2PI) * gain1
            rstd_ref[h, at, :] = jnp.broadcast_to(rstd, (CH1, 128))
            a1_ref[at, h * channels : (h + 1) * channels] = act.astype(BF16)
            if h == 0:
                ahead[at, :] = act
        return carry

    lax.fori_loop(0, rows // CH1, step1, 0, unroll=UN1)
    ahead[groups:rows, :] = jnp.where(drop, 0.0, ahead[groups:rows, :])
    ahead[rows : rows + 1, :] = ahead[0:1, :]
    move_up(ahead, a1_ref, 2 * channels, rows)

    pre2[...] = dot(a1_ref[...], k2_ref[...])
    bias2 = bias_ref[2:3, :]
    gain2 = gain_ref[2:3, :]
    shift2 = shift_ref[2:3, :]
    limit = length // 20

    def layer_two(at, place, cot):
        x = pre2[at, :] + bias2
        x = x - jnp.mean(x, -1, keepdims=True)
        rstd = lax.rsqrt(jnp.mean(x * x, -1, keepdims=True) + EPS)
        hat = x * rstd
        z = hat * gain2 + shift2
        cdf, bell = normal_cdf(z)
        valid = place < limit
        up = jnp.where(valid, cot * scale, 0.0)
        dhat = up * ((cdf + z * bell * INV_SQRT_2PI) * gain2)
        mean_d = jnp.mean(dhat, -1, keepdims=True)
        mean_dh = jnp.mean(dhat * hat, -1, keepdims=True)
        d2 = rstd * (dhat - mean_d - hat * mean_dh)
        return jnp.where(valid, z * cdf, 0.0).astype(BF16), d2.astype(BF16)

    def step2(i, carry):
        start = pl.multiple_of(i * CH2, CH2)
        at = pl.ds(start, CH2)
        place = base + start + lax.broadcasted_iota(jnp.int32, (CH2, channels), 0)
        frames, d2 = layer_two(at, place, cot_ref[at, :].astype(F32))
        frames_ref[at, :] = frames
        d2_ref[at, :] = d2
        d2own[at, :] = d2
        return carry

    lax.fori_loop(0, groups // CH2, step2, 0, unroll=UN2)
    cot_tail = jnp.where(tail_row == TAIL - 1, preceding[:, 128:], 0.0)
    place = base + jnp.where(tail_row == TAIL - 1, -1, groups + tail_row)
    _, d2_ref[groups:rows, :] = layer_two(pl.ds(groups, TAIL), place, cot_tail)
    put_gradient(here.core, keep_ref, send_ref, [(a1_ref, 0, d2own)], keep_ref.shape[2])


def forward(
    lengths, a0, head, kept, edges, w0, kernel1, kernel2, bias, gain, shift, cot, scale, chunks, special
):
    groups = cot.shape[0]
    channels = cot.shape[1]
    rows = groups + TAIL
    taps_all = kernel1.shape[0]
    grad = (2, chunks, taps_all // chunks, BC)
    return pl.pallas_call(
        functools.partial(forward_kernel, special, groups, scale),
        out_shape=[
            sds((rows, 5 * channels), BF16),
            sds((groups, channels), BF16),
            sds(grad, F32),
            sds(grad, BF16),
            sds((2, rows, channels), F32),
            sds((2, rows, channels), F32),
            sds((2, rows, 128), F32),
            sds((rows, channels), BF16),
        ],
        in_specs=[SM] + [VM] * 12,
        out_specs=[VM] * 8,
        scratch_shapes=[
            pltpu.VMEM((2 * TAIL, 4 * channels), F32),
            pltpu.VMEM((2, rows, channels), F32),
            pltpu.VMEM((rows, channels), F32),
            pltpu.VMEM((rows, 3 * channels), BF16),
            pltpu.VMEM((rows + 8, channels), F32),
            pltpu.VMEM((groups, channels), BF16),
        ],
        compiler_params=params(26),
        cost_estimate=cost(int(8e9), 10 << 20),
        name="forward",
    )(lengths, a0, head, kept, *edges, w0, kernel1, kernel2, bias, gain, shift, cot)


def window_kernel(d2_ref, k2_ref, dwin, behind):
    groups, channels = dwin.shape[1:]
    rows = groups + TAIL
    d2 = d2_ref[...]
    third = dot_nt(d2, k2_ref[2 * channels : 3 * channels, :])
    behind[8 : 8 + groups, :] = third[0:groups, :]
    behind[7:8, :] = third[rows - 1 : rows, :]
    dwin[0] = dot_nt(d2[0:groups, :], k2_ref[0:channels, :])
    dwin[1] = dot_nt(d2[0:groups, :], k2_ref[channels : 2 * channels, :])


def window(d2, kernel2):
    rows, channels = d2.shape
    groups = rows - TAIL
    return pl.pallas_call(
        window_kernel,
        out_shape=[sds((2, groups, channels), F32), sds((groups + 8, channels), F32)],
        in_specs=[VM] * 2,
        out_specs=[VM] * 2,
        compiler_params=params(),
        cost_estimate=cost(int(1.5e9), 3 << 20),
        name="window",
    )(d2, kernel2)


def backward_kernel(
    special, behind, dwin, a0_ref, hat_ref, slope_ref, rstd_ref, order_ref, keep_ref, send_ref, d1
):
    here = Place(special)
    groups, channels = dwin.shape[1:]

    def step(i, carry):
        start = pl.multiple_of(i * CH3, CH3)
        at = pl.ds(start, CH3)
        for h in range(2):
            d = dwin[h, at, :]
            if h == 0:
                d = d + behind[pl.ds(start, CH3 + 8), :][7 : 7 + CH3, :]
            hat = hat_ref[h, at, :]
            dhat = d * slope_ref[h, at, :]
            mean_d = jnp.mean(dhat, -1, keepdims=True)
            mean_dh = jnp.mean(dhat * hat, -1, keepdims=True)
            rstd = rstd_ref[h, at, 0:1]
            d1[h, at, :] = (rstd * (dhat - mean_d - hat * mean_dh)).astype(BF16)
        return carry

    lax.fori_loop(0, groups // CH3, step, 0, unroll=UN3)
    put_gradient(
        here.core,
        keep_ref,
        send_ref,
        [(a0_ref, 0, d1.at[0]), (a0_ref, 2 * channels, d1.at[1])],
        keep_ref.shape[2],
    )


def backward(behind, dwin, a0, hat, slope, rstd, order, taps_all, chunks, special):
    groups, channels = dwin.shape[1:]
    grad = (2, chunks, taps_all // chunks, BC)
    return pl.pallas_call(
        functools.partial(backward_kernel, special),
        out_shape=[sds(grad, F32), sds(grad, BF16)],
        in_specs=[VM] * 6 + [pl.BlockSpec(memory_space=pl.ANY)],
        out_specs=[VM] * 2,
        scratch_shapes=[
            pltpu.VMEM((2, groups, channels), BF16),
        ],
        compiler_params=params(20),
        cost_estimate=cost(int(4e9), 10 << 20),
        name="backward",
    )(behind, dwin, a0, hat, slope, rstd, order)


def plane_kernel(keep_ref, recv_ref, *outs):
    here = Place(True)
    x, y = here.x, here.y
    for (dx, dy), out in zip(((0, 0), (1, 0), (0, 1), (1, 1)), outs):
        for zz in range(2):
            at = (x ^ dx, 2 * zz + (y ^ dy))
            out[zz] = (keep_ref[at] + recv_ref[at].astype(F32)).astype(out.dtype)


def plane(keep, recv, order):
    shape = (2,) + keep.shape[2:]
    return pl.pallas_call(
        lambda keep_ref, recv_ref, order_ref, *outs: plane_kernel(keep_ref, recv_ref, *outs),
        out_shape=[sds(shape, F32)] + [sds(shape, BF16)] * 3,
        in_specs=[VM] * 2 + [pl.BlockSpec(memory_space=pl.ANY)],
        out_specs=[VM] * 4,
        compiler_params=params(),
        cost_estimate=cost(1 << 20, 5 << 20),
        name="plane",
    )(keep, recv, order)


def collect_kernel(own, rx, ry, rd, out):
    out[...] = own[...] + rx[...].astype(F32) + ry[...].astype(F32) + rd[...].astype(F32)


def collect(own, rx, ry, rd):
    return pl.pallas_call(
        collect_kernel,
        out_shape=sds(own.shape, F32),
        in_specs=[VM] * 4,
        out_specs=VM,
        compiler_params=params(),
        cost_estimate=cost(1 << 20, 8 << 20),
        name="collect",
    )(own, rx, ry, rd)


def column_kernel(own, rx, ry, rd, second, *outs):
    z = Place(True).z
    for dz, out in enumerate(outs):
        zz = z ^ dz
        at = lax.rem(zz, 2)

        @pl.when(zz < 2)
        def _():
            total = own[at] + rx[at].astype(F32) + ry[at].astype(F32) + rd[at].astype(F32)
            out[...] = total.astype(out.dtype)

        @pl.when(zz >= 2)
        def _():
            out[...] = second[at].astype(out.dtype)


def column(first, second):
    shape = second.shape[1:]
    return pl.pallas_call(
        column_kernel,
        out_shape=[sds(shape, F32)] + [sds(shape, BF16)] * 3,
        in_specs=[VM] * 5,
        out_specs=[VM] * 4,
        compiler_params=params(),
        cost_estimate=cost(1 << 20, 3 << 20),
        name="column",
    )(*first, second)


def final_kernel(own, a, b, c, out):
    total = own[...] + a[...].astype(F32) + b[...].astype(F32) + c[...].astype(F32)
    out[...] = total.astype(out.dtype)


def final(own, a, b, c):
    return pl.pallas_call(
        final_kernel,
        out_shape=sds(own.shape, BF16),
        in_specs=[VM] * 4,
        out_specs=VM,
        compiler_params=params(),
        cost_estimate=cost(1 << 18, 1 << 19),
        name="final",
    )(own, a, b, c)


def stats_kernel(own, other, pair, lprev, rprev, left, right):
    here = Place(True)
    core, x = here.core, here.x
    for piece, v in (
        (own, 2 * core + x),
        (other, 2 * core + 1 - x),
        (pair.at[0], 2 * (1 - core) + x),
        (pair.at[1], 2 * (1 - core) + 1 - x),
    ):
        for u in range(2):
            block = piece[u * BR : (u + 1) * BR, :]
            q = 4 * u + v
            left[q] = BETA * lprev[q] + (1.0 - BETA) * dot_nt(block, block)
            right[q] = BETA * rprev[q] + (1.0 - BETA) * dot_tn(block, block)


def stats(own, other, pair, lprev, rprev):
    return pl.pallas_call(
        stats_kernel,
        out_shape=[sds(lprev.shape, F32), sds(rprev.shape, F32)],
        in_specs=[VM] * 5,
        out_specs=[VM] * 2,
        compiler_params=params(),
        cost_estimate=cost(int(2e8), 4 << 20),
        name="stats",
    )(own, other, pair, lprev, rprev)


def permute(value, route):
    return lax.ppermute(value, AXES, route)


def body(
    audio,
    lengths,
    kernel0,
    kernel1,
    kernel2,
    conv_bias,
    norm_gain,
    norm_shift,
    cotangent,
    left_prev,
    right_prev,
):
    tms, batches = lax.axis_size("tm"), lax.axis_size("batch")
    t, b = lax.axis_index("tm"), lax.axis_index("batch")
    recordings, samples_dev = audio.shape
    piece_rows = samples_dev // 20
    groups = piece_rows * batches
    total = groups * tms
    scale = 1.0 / math.sqrt(total)

    def route(move):
        pairs = []
        for tt in range(tms):
            for bb in range(batches):
                to = move(tt, bb)
                if 0 <= to[0] < tms:
                    pairs.append((tt * batches + bb, to[0] * batches + to[1]))
        return pairs

    grouped = audio.reshape(recordings, piece_rows, 20)
    pieces = []
    for k in range(batches):
        piece = lax.dynamic_index_in_dim(grouped, b ^ k, 0, False)
        if k:
            piece = permute(piece, route(lambda tt, bb: (tt, bb ^ k)))
        pieces.append(piece)

    def of_place(place, row):
        chosen = pieces[0][row]
        for k in range(1, batches):
            chosen = jnp.where((b ^ k) == place, pieces[k][row], chosen)
        return chosen[None]

    cot = cotangent[0]
    first_group = jnp.pad(of_place(0, 0), ((0, 0), (0, 108 + cot.shape[1])))
    last_group = jnp.concatenate(
        [
            jnp.pad(of_place(batches - 1, piece_rows - 1), ((0, 0), (0, 108))),
            cot[groups - 1 :].astype(F32),
        ],
        1,
    )
    odd = t % 2 == 1
    edge_a = permute(jnp.where(odd, first_group, last_group), route(lambda tt, bb: (tt ^ 1, bb)))
    edge_b = permute(
        jnp.where(odd, last_group, first_group), route(lambda tt, bb: (tt + 2 * (tt % 2) - 1, bb))
    )

    w0 = prep(kernel0, conv_bias)
    special = tms == 8 and batches == 4
    chunks = 4
    a0, head, kept = audio_layer(lengths, pieces, w0, norm_gain, norm_shift, special)
    a0, frames, keep2, send2, hat, slope, rstd, d2 = forward(
        lengths,
        a0,
        head,
        kept,
        (edge_a, edge_b),
        w0,
        kernel1,
        kernel2,
        conv_bias,
        norm_gain,
        norm_shift,
        cot,
        scale,
        chunks,
        special,
    )
    dwin, behind = window(d2, kernel2)

    def gradient_one(order):
        return backward(behind, dwin, a0, hat, slope, rstd, order, kernel1.shape[0], chunks, special)

    if not special:
        keep1, send1 = gradient_one(keep2)

        def blocks_of(keep, send):
            both = jnp.stack([keep, send.astype(F32)])
            both = both.reshape(2, 2, -1, BR, BC)
            return jnp.transpose(both, (2, 0, 1, 3, 4)).reshape(-1, BR, BC)

        stacked = jnp.concatenate([blocks_of(keep1, send1), blocks_of(keep2, send2)], 0)
        owned = lax.psum_scatter(stacked, "tm", scatter_dimension=0, tiled=True)
        owned = lax.psum(owned, "batch")
        left = BETA * left_prev + (1.0 - BETA) * jnp.einsum(
            "bik,bjk->bij", owned, owned, precision=lax.Precision.HIGHEST
        )
        right = BETA * right_prev + (1.0 - BETA) * jnp.einsum(
            "bki,bkj->bij", owned, owned, precision=lax.Precision.HIGHEST
        )
        return frames[None], left, right

    by_core = route(lambda tt, bb: (tt, bb ^ 1))
    by_x = route(lambda tt, bb: (tt, bb ^ 2))
    by_y = route(lambda tt, bb: (tt ^ 1, bb))
    by_xy = route(lambda tt, bb: (tt ^ 1, bb ^ 2))
    by_z = [route(lambda tt, bb: (tt ^ (2 * k), bb)) for k in range(1, 4)]

    def to_plane(tox, toy, tod):
        return permute(tox, by_x), permute(toy, by_y), permute(tod, by_xy)

    own2, *out = plane(keep2, permute(send2, by_core), keep2)
    second = collect(own2, *to_plane(*out))
    keep1, send1 = gradient_one(own2)
    own1, *out = plane(keep1, permute(send1, by_core), second)
    own, *out = column((own1, *to_plane(*out)), second)
    arrived = [permute(value, way) for value, way in zip(out, by_z)]
    owned = final(own, *arrived)
    other = permute(owned, by_x)
    pair = permute(jnp.stack([owned, other]), by_core)
    left, right = stats(owned, other, pair, left_prev, right_prev)
    return frames[None], left, right


def solution(mesh):
    return jax.shard_map(
        body,
        mesh=mesh,
        in_specs=(
            P(None, AXES),
            P(),
            P(),
            P(),
            P(),
            P(),
            P(),
            P(),
            P("batch", "tm", None),
            P("tm", None, None),
            P("tm", None, None),
        ),
        out_specs=(P("batch", "tm", None), P("tm", None, None), P("tm", None, None)),
        check_vma=False,
    )
```

time: 102 us -> 74.8 us (0.73)
  Pallas kernels: 41.1 us -> 19.1 us
  starting transfers between devices: 30.1 us -> 21.4 us
  waiting for transfers between devices: 24.3 us -> 29.8 us
  local copies, waits for them, and re-layouts: 5.2 us -> 2.49 us
    pallas_call x4 -> x7, Pallas kernels: 37.6 us -> 16.9 us  [the longest x1 8.15 us: forward(): pl.pallas_call(functools.partial(forward_kernel, special, groups, scale),...]
    ppermute x19 -> x18, starting transfers between devices: 30.1 us -> 21.4 us  [permute(): return lax.ppermute(value, AXES, route)]
    ppermute x19 -> x18, waiting for transfers between devices: 24.3 us -> 29.8 us  [permute(): return lax.ppermute(value, AXES, route)]
    dynamic_slice x1 -> x0, local copies, waits for them, and re-layouts: 1.24 us -> none  [body(): lax.dynamic_index_in_dim(lengths, b, 0, False)]
  transfers between devices with their start and end apart: 19 -> 18, of which waited for: 10 -> 10; matrix products, arithmetic and copies ran while one was open for 3% -> 1% of each run, Pallas kernels for 10% -> 8%
where the time goes in v2:
time: 74.8 us; the launch traced here: 74.4 us
  waiting for transfers between devices  29.8 us (40%)
  starting transfers between devices  21.4 us (29%)
  Pallas kernels  19.1 us (26%)
  local copies, waits for them, and re-layouts  2.49 us (3%)
  between operations  0.91 us (1%)
    ppermute x18, waiting for transfers between devices, permute(): return lax.ppermute(value, AXES, route)  29.8 us
    ppermute x18, starting transfers between devices, permute(): return lax.ppermute(value, AXES, route)  21.4 us
    pallas_call x1, Pallas kernels, forward(): pl.pallas_call(functools.partial(forward_kernel, special, groups, scale),...  8.15 us
    pallas_call x1, Pallas kernels, audio_layer(): pl.pallas_call(functools.partial(audio_kernel, special), out_shape=[sds((...  4.78 us
    pallas_call x1, Pallas kernels, backward(): pl.pallas_call(functools.partial(backward_kernel, special), out_shape=[sd...  2.76 us
    pallas_call x1, Pallas kernels, stats(): pl.pallas_call(stats_kernel, out_shape=[sds(lprev.shape, F32), sds(rprev....  1.87 us
  transfers between devices with their start and end apart: 18, of which 10 were waited for; matrix products, arithmetic and copies ran while one was open for 1% of the time, Pallas kernels for 8%

profile of v2, /device:TPU:0, one launch (start us, length us, event | category | flops | bytes accessed | tf_op | source)
XLA Modules:
  0.0 74.4 jit_solution(6696674682617502260)
XLA Ops:
  0.7 1.0 %reshape.30 = f32[4,96,20]{2,1,0:T(8,128)S(1)} reshape(f32[4,1920]{1,0:T(4,128)} %param.11) | data formatting | bytes 61440 | tf_op jit(solution)/shard_map/reshape | solution.py:616
  1.7 2.4 %collective-permute-start.2 = (f32[96,20]{1,0:T(8,128)S(1)}, f32[96,20]{1,0:T(8,128)S(1)}, u32[]{:S(2)}, u32[]{:S(2)}) collective-permute-start(f32[96,20]{1,0:T(8,128)S(1)} %get-tuple-element.63), channel_id=1, source_target_pairs={{0,3},{1,2},{2,1},{3,0},{4,7},{5,6},{6,5},{7,4},{8,11},{9,10},{10,... | collective-permute-start | bytes 23048 | tf_op jit(solution)/shard_map/ppermute | solution.py:583
  4.1 0.6 collective-permute-start.1
  4.8 0.7 bitcast_convert_fusion
  5.5 0.8 %copy-done.2 = f32[10,512]{1,0:T(8,128)S(1)} copy-done((f32[10,512]{1,0:T(8,128)S(1)}, f32[10,512]{1,0:T(8,128)}, u32[]{:S(2)}) %copy-start.2) | copy-done | bytes 20504
  6.3 0.7 copy-done.3
  7.2 1.3 %collective-permute-done.1.p2 = f32[96,20]{1,0:T(8,128)S(1)} collective-permute-done((f32[96,20]{1,0:T(8,128)S(1)}, f32[96,20]{1,0:T(8,128)S(1)}, u32[]{:S(2)}, u32[]{:S(2)}) %collective-permute-start.1) | collective-permute-done | bytes 7712 | tf_op jit(solution)/shard_map/ppermute | solution.py:583
  8.5 0.7 collective-permute-start.4
  9.2 4.4 %collective-permute-start.3 = (f32[1,640]{1,0:T(1,128)S(1)}, f32[1,640]{1,0:T(1,128)S(1)}, u32[]{:S(2)}, u32[]{:S(2)}) collective-permute-start(f32[1,640]{1,0:T(1,128)S(1)} %get-tuple-element.68), channel_id=1, source_target_pairs={{0,4},{1,5},{2,6},{3,7},{4,0},{5,1},{6,2},{7,3},{8,12},{9,13},{10,... | collective-permute-start | bytes 7688 | tf_op jit(solution)/shard_map/ppermute | solution.py:583
  13.6 4.8 %audio_layer.1 = (bf16[384,2560]{1,0:T(8,128)(2,1)S(1)}, f32[8,512]{1,0:T(8,128)S(1)}, f32[24,128]{1,0:T(8,128)S(1)}) custom-call(s32[4]{0:T(128)S(1)} %copy-done.9, f32[96,20]{1,0:T(8,128)S(1)} %get-tuple-element.66.p0, f32[96,20]{1,0:T(8,128)S(1)} %collective-permute-done.p1, f32[96,20]{1,0:T(8,128)S(1)} %collective-permute-done.1.p2, ...), custom_call_target="tpu_custom_call" | custom-call | flops 3000000000 | bytes 5242880 | tf_op jit(solution)/shard_map/audio_layer/pallas_call | solution.py:200
  18.4 8.2 %forward.1 = (bf16[400,2560]{1,0:T(8,128)(2,1)S(1)}, bf16[384,512]{1,0:T(8,128)(2,1)}, f32[2,4,384,128]{3,2,1,0:T(8,128)S(1)}, bf16[2,4,384,128]{3,2,1,0:T(8,128...) custom-call(s32[4]{0:T(128)S(1)} %copy-done.9, ...), custom_call_target="tpu_custom_call" | custom-call | flops 8000000000 | bytes 10485760 | tf_op jit(solution)/shard_map/forward/pallas_call | solution.py:369
  26.6 0.8 %window.1 = (f32[2,384,512]{2,1,0:T(8,128)S(1)}, f32[392,512]{1,0:T(8,128)S(1)}) custom-call(bf16[400,512]{1,0:T(8,128)(2,1)S(1)} %get-tuple-element.36.d2_ref, bf16[1536,512]{1,0:T(8,128)(2,1)S(1)} %copy-done.6), custom_call_target="tpu_custom_call" | custom-call | flops 1500000000 | bytes 3145728 | tf_op jit(solution)/shard_map/window/pallas_call | solution.py:411
  27.4 1.5 %collective-permute-done.5.recv_ref = bf16[2,4,384,128]{3,2,1,0:T(8,128)(2,1)S(1)} collective-permute-done((bf16[2,4,384,128]{3,2,1,0:T(8,128)(2,1)S(1)}, bf16[2,4,384,128]{3,2,1,0:T(8,128)(2,1)S(1)}, u32[]{:S(2)}, u32[]{:S(2)}) %collective-permute-start.5) | collective-permute-done | bytes 786464 | tf_op jit(solution)/shard_map/ppermute | solution.py:583
  29.0 2.8 %backward.1 = (f32[2,4,384,128]{3,2,1,0:T(8,128)S(1)}, bf16[2,4,384,128]{3,2,1,0:T(8,128)(2,1)S(1)}) custom-call(f32[392,512]{1,0:T(8,128)S(1)} %get-tuple-element.37.behind, f32[2,384,512]{2,1,0:T(8,128)S(1)} %get-tuple-element.38.dwin, bf16[400,2560]{1,0:T(8,128)(2,1)S(1)} %get-tuple-element.39.a0_ref, f32[2,400,512]{2,1,0:T(8,128)S(1)} %get-tuple-element.40.hat_ref, ...), custom_call_target="tpu_custom_call" | custom-call | flops 4000000000 | bytes 10485760 | tf_op jit(solution)/shard_map/backward/pallas_call | solution.py:456
  32.0 1.4 %collective-permute-start.7 = (bf16[2,384,128]{2,1,0:T(8,128)(2,1)S(1)}, bf16[2,384,128]{2,1,0:T(8,128)(2,1)S(1)}, u32[]{:S(2)}, u32[]{:S(2)}) collective-permute-start(bf16[2,384,128]{2,1,0:T(8,128)(2,1)S(1)} %get-tuple-element.48), channel_id=1, source_target_pairs={{0,2},{1,3},{2,0},{3,1},{4,6},{5,7},{6,4},{7,5},{8,10},{9,11},{10,... | collective-permute-start | bytes 589832 | tf_op jit(solution)/shard_map/ppermute | solution.py:583
  33.4 2.1 %collective-permute-start.9 = (bf16[2,384,128]{2,1,0:T(8,128)(2,1)S(1)}, bf16[2,384,128]{2,1,0:T(8,128)(2,1)S(1)}, u32[]{:S(2)}, u32[]{:S(2)}) collective-permute-start(bf16[2,384,128]{2,1,0:T(8,128)(2,1)S(1)} %get-tuple-element.50), channel_id=1, source_target_pairs={{0,6},{1,7},{2,4},{3,5},{4,2},{5,3},{6,0},{7,1},{8,14},{9,15},{10,... | collective-permute-start | bytes 589832 | tf_op jit(solution)/shard_map/ppermute | solution.py:583
  35.5 4.2 %collective-permute-done.7.rx = bf16[2,384,128]{2,1,0:T(8,128)(2,1)S(1)} collective-permute-done((bf16[2,384,128]{2,1,0:T(8,128)(2,1)S(1)}, bf16[2,384,128]{2,1,0:T(8,128)(2,1)S(1)}, u32[]{:S(2)}, u32[]{:S(2)}) %collective-permute-start.7) | collective-permute-done | bytes 196640 | tf_op jit(solution)/shard_map/ppermute | solution.py:583
  39.7 4.7 %collective-permute-done.8.ry = bf16[2,384,128]{2,1,0:T(8,128)(2,1)S(1)} collective-permute-done((bf16[2,384,128]{2,1,0:T(8,128)(2,1)S(1)}, bf16[2,384,128]{2,1,0:T(8,128)(2,1)S(1)}, u32[]{:S(2)}, u32[]{:S(2)}) %collective-permute-start.8) | collective-permute-done | bytes 196640 | tf_op jit(solution)/shard_map/ppermute | solution.py:583
  44.7 0.8 %collective-permute-start.10 = (bf16[2,384,128]{2,1,0:T(8,128)(2,1)S(1)}, bf16[2,384,128]{2,1,0:T(8,128)(2,1)S(1)}, u32[]{:S(2)}, u32[]{:S(2)}) collective-permute-start(bf16[2,384,128]{2,1,0:T(8,128)(2,1)S(1)} %get-tuple-element.52), channel_id=1, source_target_pairs={{0,2},{1,3},{2,0},{3,1},{4,6},{5,7},{6,4},{7,5},{8,10},{9,11},{10,... | collective-permute-start | bytes 589832 | tf_op jit(solution)/shard_map/ppermute | solution.py:583
  45.5 1.1 %collective-permute-start.11 = (bf16[2,384,128]{2,1,0:T(8,128)(2,1)S(1)}, bf16[2,384,128]{2,1,0:T(8,128)(2,1)S(1)}, u32[]{:S(2)}, u32[]{:S(2)}) collective-permute-start(bf16[2,384,128]{2,1,0:T(8,128)(2,1)S(1)} %get-tuple-element.53), channel_id=1, source_target_pairs={{0,4},{1,5},{2,6},{3,7},{4,0},{5,1},{6,2},{7,3},{8,12},{9,13},{10,... | collective-permute-start | bytes 589832 | tf_op jit(solution)/shard_map/ppermute | solution.py:583
  46.5 1.8 %collective-permute-start.12 = (bf16[2,384,128]{2,1,0:T(8,128)(2,1)S(1)}, bf16[2,384,128]{2,1,0:T(8,128)(2,1)S(1)}, u32[]{:S(2)}, u32[]{:S(2)}) collective-permute-start(bf16[2,384,128]{2,1,0:T(8,128)(2,1)S(1)} %get-tuple-element.54), channel_id=1, source_target_pairs={{0,6},{1,7},{2,4},{3,5},{4,2},{5,3},{6,0},{7,1},{8,14},{9,15},{10,... | collective-permute-start | bytes 589832 | tf_op jit(solution)/shard_map/ppermute | solution.py:583
  48.3 4.3 %collective-permute-done.10.rx = bf16[2,384,128]{2,1,0:T(8,128)(2,1)S(1)} collective-permute-done((bf16[2,384,128]{2,1,0:T(8,128)(2,1)S(1)}, bf16[2,384,128]{2,1,0:T(8,128)(2,1)S(1)}, u32[]{:S(2)}, u32[]{:S(2)}) %collective-permute-start.10) | collective-permute-done | bytes 196640 | tf_op jit(solution)/shard_map/ppermute | solution.py:583
  52.6 2.7 %collective-permute-done.11.ry = bf16[2,384,128]{2,1,0:T(8,128)(2,1)S(1)} collective-permute-done((bf16[2,384,128]{2,1,0:T(8,128)(2,1)S(1)}, bf16[2,384,128]{2,1,0:T(8,128)(2,1)S(1)}, u32[]{:S(2)}, u32[]{:S(2)}) %collective-permute-start.11) | collective-permute-done | bytes 196640 | tf_op jit(solution)/shard_map/ppermute | solution.py:583
  55.5 1.6 %collective-permute-start.13 = (bf16[384,128]{1,0:T(8,128)(2,1)S(1)}, bf16[384,128]{1,0:T(8,128)(2,1)S(1)}, u32[]{:S(2)}, u32[]{:S(2)}) collective-permute-start(bf16[384,128]{1,0:T(8,128)(2,1)S(1)} %get-tuple-element.56), channel_id=1, source_target_pairs={{0,8},{1,9},{2,10},{3,11},{4,12},{5,13},{6,14},{7,15},{8,0},{9,1},... | collective-permute-start | bytes 294920 | tf_op jit(solution)/shard_map/ppermute | solution.py:583
  57.1 2.4 %collective-permute-start.14 = (bf16[384,128]{1,0:T(8,128)(2,1)S(1)}, bf16[384,128]{1,0:T(8,128)(2,1)S(1)}, u32[]{:S(2)}, u32[]{:S(2)}) collective-permute-start(bf16[384,128]{1,0:T(8,128)(2,1)S(1)} %get-tuple-element.57), channel_id=1, source_target_pairs={{0,16},{1,17},{2,18},{3,19},{4,20},{5,21},{6,22},{7,23},{8,24},{9,... | collective-permute-start | bytes 294920 | tf_op jit(solution)/shard_map/ppermute | solution.py:583
  59.6 0.4 collective-permute-start.15
  60.0 1.0 %collective-permute-done.13.a = bf16[384,128]{1,0:T(8,128)(2,1)S(1)} collective-permute-done((bf16[384,128]{1,0:T(8,128)(2,1)S(1)}, bf16[384,128]{1,0:T(8,128)(2,1)S(1)}, u32[]{:S(2)}, u32[]{:S(2)}) %collective-permute-start.13) | collective-permute-done | bytes 98336 | tf_op jit(solution)/shard_map/ppermute | solution.py:583
  60.9 5.3 %collective-permute-done.14.b = bf16[384,128]{1,0:T(8,128)(2,1)S(1)} collective-permute-done((bf16[384,128]{1,0:T(8,128)(2,1)S(1)}, bf16[384,128]{1,0:T(8,128)(2,1)S(1)}, u32[]{:S(2)}, u32[]{:S(2)}) %collective-permute-start.14) | collective-permute-done | bytes 98336 | tf_op jit(solution)/shard_map/ppermute | solution.py:583
  66.3 1.4 %collective-permute-start.16 = (bf16[384,128]{1,0:T(8,128)(2,1)S(1)}, bf16[384,128]{1,0:T(8,128)(2,1)S(1)}, u32[]{:S(2)}, u32[]{:S(2)}) collective-permute-start(bf16[384,128]{1,0:T(8,128)(2,1)S(1)} %final.1.own), channel_id=1, source_target_pairs={{0,2},{1,3},{2,0},{3,1},{4,6},{5,7},{6,4},{7,5},{8,10},{9,11},{10,... | collective-permute-start | bytes 294920 | tf_op jit(solution)/shard_map/ppermute | solution.py:583
  67.7 3.3 %collective-permute-done.16.other = bf16[384,128]{1,0:T(8,128)(2,1)S(1)} collective-permute-done((bf16[384,128]{1,0:T(8,128)(2,1)S(1)}, bf16[384,128]{1,0:T(8,128)(2,1)S(1)}, u32[]{:S(2)}, u32[]{:S(2)}) %collective-permute-start.16) | collective-permute-done | bytes 98336 | tf_op jit(solution)/shard_map/ppermute | solution.py:583
  71.1 1.4 %collective-permute-done.17.pair = bf16[2,384,128]{2,1,0:T(8,128)(2,1)S(1)} collective-permute-done((bf16[2,384,128]{2,1,0:T(8,128)(2,1)S(1)}, bf16[2,384,128]{2,1,0:T(8,128)(2,1)S(1)}, u32[]{:S(2)}, u32[]{:S(2)}) %collective-permute-start.17) | collective-permute-done | bytes 196640 | tf_op jit(solution)/shard_map/ppermute | solution.py:583
  72.5 1.9 %stats.1 = (f32[8,192,192]{2,1,0:T(8,128)}, f32[8,128,128]{2,1,0:T(8,128)}) custom-call(bf16[384,128]{1,0:T(8,128)(2,1)S(1)} %final.1.own, bf16[384,128]{1,0:T(8,128)(2,1)S(1)} %collective-permute-done.16.other, bf16[2,384,128]{2,1,0:T(8,128)(2,1)S(1)} %collective-permute-done.17.pair, f32[8,192,192]{2,1,0:T(8,128)S(1)} %copy-done, f32[8,128,128]{2,1,0:T(8,128)S(1)} %copy-done.1), custom_call_target="tpu_custom_call" | custom-call | flops 200000000 | bytes 4194304 | tf_op jit(solution)/shard_map/stats/pallas_call | solution.py:571
  (41 shorter events, 1.2 us)
Async XLA Ops:
  0.6 12.9 %copy-start.8 = (f32[3,512]{1,0:T(4,128)S(1)}, f32[3,512]{1,0:T(4,128)}, u32[]{:S(2)}) copy-start(f32[3,512]{1,0:T(4,128)} %shift_ref.3) | copy-start | bytes 18436
  0.6 12.9 %copy-start.7 = (f32[3,512]{1,0:T(4,128)S(1)}, f32[3,512]{1,0:T(4,128)}, u32[]{:S(2)}) copy-start(f32[3,512]{1,0:T(4,128)} %gain_ref.3) | copy-start | bytes 18436
  0.7 12.9 %copy-start.9 = (s32[4]{0:T(128)S(1)}, s32[4]{0:T(128)}, u32[]{:S(2)}) copy-start(s32[4]{0:T(128)} %lengths.3) | copy-start | bytes 52
  1.7 5.5 %collective-permute-start.2 = (f32[96,20]{1,0:T(8,128)S(1)}, f32[96,20]{1,0:T(8,128)S(1)}, u32[]{:S(2)}, u32[]{:S(2)}) collective-permute-start(f32[96,20]{1,0:T(8,128)S(1)} %get-tuple-element.63), channel_id=1, source_target_pairs={{0,3},{1,2},{2,1},{3,0},{4,7},{5,6},{6,5},{7,4},{8,11},{9,10},{10,... | collective-permute-start | bytes 23048 | tf_op jit(solution)/shard_map/ppermute | solution.py:583
  4.1 4.3 %collective-permute-start.1 = (f32[96,20]{1,0:T(8,128)S(1)}, f32[96,20]{1,0:T(8,128)S(1)}, u32[]{:S(2)}, u32[]{:S(2)}) collective-permute-start(f32[96,20]{1,0:T(8,128)S(1)} %get-tuple-element.64), channel_id=1, source_target_pairs={{0,2},{1,3},{2,0},{3,1},{4,6},{5,7},{6,4},{7,5},{8,10},{9,11},{10,... | collective-permute-start | bytes 23048 | tf_op jit(solution)/shard_map/ppermute | solution.py:583
  4.8 3.7 %collective-permute-start = (f32[96,20]{1,0:T(8,128)S(1)}, f32[96,20]{1,0:T(8,128)S(1)}, u32[]{:S(2)}, u32[]{:S(2)}) collective-permute-start(f32[96,20]{1,0:T(8,128)S(1)} %get-tuple-element.65), channel_id=1, source_target_pairs={{0,1},{1,0},{2,3},{3,2},{4,5},{5,4},{6,7},{7,6},{8,9},{9,8},{10,11... | collective-permute-start | bytes 23048 | tf_op jit(solution)/shard_map/ppermute | solution.py:583
  5.5 0.8 %copy-start.2 = (f32[10,512]{1,0:T(8,128)S(1)}, f32[10,512]{1,0:T(8,128)}, u32[]{:S(2)}) copy-start(f32[10,512]{1,0:T(8,128)} %k0_ref.1) | copy-start | bytes 61444
  6.3 0.7 copy-start.3
  8.5 9.9 %collective-permute-start.4 = (f32[1,640]{1,0:T(1,128)S(1)}, f32[1,640]{1,0:T(1,128)S(1)}, u32[]{:S(2)}, u32[]{:S(2)}) collective-permute-start(f32[1,640]{1,0:T(1,128)S(1)} %get-tuple-element.67), channel_id=1, source_target_pairs={{4,8},{5,9},{6,10},{7,11},{8,4},{9,5},{10,6},{11,7},{12,16},{13,17... | collective-permute-start | bytes 7688 | tf_op jit(solution)/shard_map/ppermute | solution.py:583
  9.2 9.2 %collective-permute-start.3 = (f32[1,640]{1,0:T(1,128)S(1)}, f32[1,640]{1,0:T(1,128)S(1)}, u32[]{:S(2)}, u32[]{:S(2)}) collective-permute-start(f32[1,640]{1,0:T(1,128)S(1)} %get-tuple-element.68), channel_id=1, source_target_pairs={{0,4},{1,5},{2,6},{3,7},{4,0},{5,1},{6,2},{7,3},{8,12},{9,13},{10,... | collective-permute-start | bytes 7688 | tf_op jit(solution)/shard_map/ppermute | solution.py:583
  13.5 4.8 %copy-start.4 = (bf16[1,384,512]{2,1,0:T(8,128)(2,1)S(1)}, bf16[1,384,512]{2,1,0:T(8,128)(2,1)}, u32[]{:S(2)}) copy-start(bf16[1,384,512]{2,1,0:T(8,128)(2,1)} %param.19) | copy-start | bytes 1179652
  13.5 4.8 %copy-start.5 = (bf16[1536,512]{1,0:T(8,128)(2,1)S(1)}, bf16[1536,512]{1,0:T(8,128)(2,1)}, u32[]{:S(2)}) copy-start(bf16[1536,512]{1,0:T(8,128)(2,1)} %k1_ref.1) | copy-start | bytes 4718596
  13.6 4.8 %copy-start.6 = (bf16[1536,512]{1,0:T(8,128)(2,1)S(1)}, bf16[1536,512]{1,0:T(8,128)(2,1)}, u32[]{:S(2)}) copy-start(bf16[1536,512]{1,0:T(8,128)(2,1)} %k2_ref.3) | copy-start | bytes 4718596
  26.6 2.3 %collective-permute-start.5 = (bf16[2,4,384,128]{3,2,1,0:T(8,128)(2,1)S(1)}, bf16[2,4,384,128]{3,2,1,0:T(8,128)(2,1)S(1)}, u32[]{:S(2)}, u32[]{:S(2)}) collective-permute-start(bf16[2,4,384,128]{3,2,1,0:T(8,128)(2,1)S(1)} %get-tuple-element.44), channel_id=1, source_target_pairs={{0,1},{1,0},{2,3},{3,2},{4,5},{5,4},{6,7},{7,6},{8,9},{9,8},{10,11... | collective-permute-start | bytes 2359304 | tf_op jit(solution)/shard_map/ppermute | solution.py:583
  31.8 12.7 %collective-permute-start.6 = (bf16[2,4,384,128]{3,2,1,0:T(8,128)(2,1)S(1)}, bf16[2,4,384,128]{3,2,1,0:T(8,128)(2,1)S(1)}, u32[]{:S(2)}, u32[]{:S(2)}) collective-permute-start(bf16[2,4,384,128]{3,2,1,0:T(8,128)(2,1)S(1)} %get-tuple-element.47), channel_id=1, source_target_pairs={{0,1},{1,0},{2,3},{3,2},{4,5},{5,4},{6,7},{7,6},{8,9},{9,8},{10,11... | collective-permute-start | bytes 2359304 | tf_op jit(solution)/shard_map/ppermute | solution.py:583
  32.0 7.7 %collective-permute-start.7 = (bf16[2,384,128]{2,1,0:T(8,128)(2,1)S(1)}, bf16[2,384,128]{2,1,0:T(8,128)(2,1)S(1)}, u32[]{:S(2)}, u32[]{:S(2)}) collective-permute-start(bf16[2,384,128]{2,1,0:T(8,128)(2,1)S(1)} %get-tuple-element.48), channel_id=1, source_target_pairs={{0,2},{1,3},{2,0},{3,1},{4,6},{5,7},{6,4},{7,5},{8,10},{9,11},{10,... | collective-permute-start | bytes 589832 | tf_op jit(solution)/shard_map/ppermute | solution.py:583
  33.3 11.1 %collective-permute-start.8 = (bf16[2,384,128]{2,1,0:T(8,128)(2,1)S(1)}, bf16[2,384,128]{2,1,0:T(8,128)(2,1)S(1)}, u32[]{:S(2)}, u32[]{:S(2)}) collective-permute-start(bf16[2,384,128]{2,1,0:T(8,128)(2,1)S(1)} %get-tuple-element.49), channel_id=1, source_target_pairs={{0,4},{1,5},{2,6},{3,7},{4,0},{5,1},{6,2},{7,3},{8,12},{9,13},{10,... | collective-permute-start | bytes 589832 | tf_op jit(solution)/shard_map/ppermute | solution.py:583
  33.4 11.1 %collective-permute-start.9 = (bf16[2,384,128]{2,1,0:T(8,128)(2,1)S(1)}, bf16[2,384,128]{2,1,0:T(8,128)(2,1)S(1)}, u32[]{:S(2)}, u32[]{:S(2)}) collective-permute-start(bf16[2,384,128]{2,1,0:T(8,128)(2,1)S(1)} %get-tuple-element.50), channel_id=1, source_target_pairs={{0,6},{1,7},{2,4},{3,5},{4,2},{5,3},{6,0},{7,1},{8,14},{9,15},{10,... | collective-permute-start | bytes 589832 | tf_op jit(solution)/shard_map/ppermute | solution.py:583
  44.7 27.8 %copy-start = (f32[8,192,192]{2,1,0:T(8,128)S(1)}, f32[8,192,192]{2,1,0:T(8,128)}, u32[]{:S(2)}) copy-start(f32[8,192,192]{2,1,0:T(8,128)} %lprev.1) | copy-start | bytes 3538948
  44.7 27.8 %copy-start.1 = (f32[8,128,128]{2,1,0:T(8,128)S(1)}, f32[8,128,128]{2,1,0:T(8,128)}, u32[]{:S(2)}) copy-start(f32[8,128,128]{2,1,0:T(8,128)} %rprev.1) | copy-start | bytes 1572868
  44.7 7.9 %collective-permute-start.10 = (bf16[2,384,128]{2,1,0:T(8,128)(2,1)S(1)}, bf16[2,384,128]{2,1,0:T(8,128)(2,1)S(1)}, u32[]{:S(2)}, u32[]{:S(2)}) collective-permute-start(bf16[2,384,128]{2,1,0:T(8,128)(2,1)S(1)} %get-tuple-element.52), channel_id=1, source_target_pairs={{0,2},{1,3},{2,0},{3,1},{4,6},{5,7},{6,4},{7,5},{8,10},{9,11},{10,... | collective-permute-start | bytes 589832 | tf_op jit(solution)/shard_map/ppermute | solution.py:583
  45.5 9.9 %collective-permute-start.11 = (bf16[2,384,128]{2,1,0:T(8,128)(2,1)S(1)}, bf16[2,384,128]{2,1,0:T(8,128)(2,1)S(1)}, u32[]{:S(2)}, u32[]{:S(2)}) collective-permute-start(bf16[2,384,128]{2,1,0:T(8,128)(2,1)S(1)} %get-tuple-element.53), channel_id=1, source_target_pairs={{0,4},{1,5},{2,6},{3,7},{4,0},{5,1},{6,2},{7,3},{8,12},{9,13},{10,... | collective-permute-start | bytes 589832 | tf_op jit(solution)/shard_map/ppermute | solution.py:583
  46.5 8.8 %collective-permute-start.12 = (bf16[2,384,128]{2,1,0:T(8,128)(2,1)S(1)}, bf16[2,384,128]{2,1,0:T(8,128)(2,1)S(1)}, u32[]{:S(2)}, u32[]{:S(2)}) collective-permute-start(bf16[2,384,128]{2,1,0:T(8,128)(2,1)S(1)} %get-tuple-element.54), channel_id=1, source_target_pairs={{0,6},{1,7},{2,4},{3,5},{4,2},{5,3},{6,0},{7,1},{8,14},{9,15},{10,... | collective-permute-start | bytes 589832 | tf_op jit(solution)/shard_map/ppermute | solution.py:583
  55.5 5.4 %collective-permute-start.13 = (bf16[384,128]{1,0:T(8,128)(2,1)S(1)}, bf16[384,128]{1,0:T(8,128)(2,1)S(1)}, u32[]{:S(2)}, u32[]{:S(2)}) collective-permute-start(bf16[384,128]{1,0:T(8,128)(2,1)S(1)} %get-tuple-element.56), channel_id=1, source_target_pairs={{0,8},{1,9},{2,10},{3,11},{4,12},{5,13},{6,14},{7,15},{8,0},{9,1},... | collective-permute-start | bytes 294920 | tf_op jit(solution)/shard_map/ppermute | solution.py:583
  57.1 9.1 %collective-permute-start.14 = (bf16[384,128]{1,0:T(8,128)(2,1)S(1)}, bf16[384,128]{1,0:T(8,128)(2,1)S(1)}, u32[]{:S(2)}, u32[]{:S(2)}) collective-permute-start(bf16[384,128]{1,0:T(8,128)(2,1)S(1)} %get-tuple-element.57), channel_id=1, source_target_pairs={{0,16},{1,17},{2,18},{3,19},{4,20},{5,21},{6,22},{7,23},{8,24},{9,... | collective-permute-start | bytes 294920 | tf_op jit(solution)/shard_map/ppermute | solution.py:583
  59.6 6.7 %collective-permute-start.15 = (bf16[384,128]{1,0:T(8,128)(2,1)S(1)}, bf16[384,128]{1,0:T(8,128)(2,1)S(1)}, u32[]{:S(2)}, u32[]{:S(2)}) collective-permute-start(bf16[384,128]{1,0:T(8,128)(2,1)S(1)} %get-tuple-element.58), channel_id=1, source_target_pairs={{0,24},{1,25},{2,26},{3,27},{4,28},{5,29},{6,30},{7,31},{8,16},{9,... | collective-permute-start | bytes 294920 | tf_op jit(solution)/shard_map/ppermute | solution.py:583
  66.3 4.7 %collective-permute-start.16 = (bf16[384,128]{1,0:T(8,128)(2,1)S(1)}, bf16[384,128]{1,0:T(8,128)(2,1)S(1)}, u32[]{:S(2)}, u32[]{:S(2)}) collective-permute-start(bf16[384,128]{1,0:T(8,128)(2,1)S(1)} %final.1.own), channel_id=1, source_target_pairs={{0,2},{1,3},{2,0},{3,1},{4,6},{5,7},{6,4},{7,5},{8,10},{9,11},{10,... | collective-permute-start | bytes 294920 | tf_op jit(solution)/shard_map/ppermute | solution.py:583
  71.0 1.5 %collective-permute-start.17 = (bf16[2,384,128]{2,1,0:T(8,128)(2,1)S(1)}, bf16[2,384,128]{2,1,0:T(8,128)(2,1)S(1)}, u32[]{:S(2)}, u32[]{:S(2)}) collective-permute-start(bf16[2,384,128]{2,1,0:T(8,128)(2,1)S(1)} %pad_maximum_fusion), channel_id=1, source_target_pairs={{0,1},{1,0},{2,3},{3,2},{4,5},{5,4},{6,7},{7,6},{8,9},{9,8},{10,11... | collective-permute-start | bytes 589832 | tf_op jit(solution)/shard_map/ppermute | solution.py:583

commit v3 on v2

--- a/solution.py
+++ b/solution.py
@@ -17,6 +17,7 @@
 BF16 = jnp.bfloat16
 MIB = 1024 * 1024
 CH = 16
+PACK = 6
 CH0, CH1, CH2, CH3 = 16,16,16,16
 UN0, UN1, UN2, UN3 = 4,25,6,6
 TAIL = 16
@@ -158,19 +159,49 @@
     lax.fori_loop(0, rows // CH, move, 0, unroll=2)
 
 
+def pack_kernel(grouped, *outs):
+    b = lax.axis_index("batch")
+    piece_rows = grouped.shape[1]
+    part = piece_rows // PACK
+    lane = lax.broadcasted_iota(jnp.int32, (part, 128), 1)
+    for k, out in enumerate(outs):
+        total = None
+        for q in range(PACK):
+            block = grouped[b ^ k, q * part : (q + 1) * part, :]
+            block = jnp.concatenate([block, jnp.zeros((part, 108), F32)], 1)
+            block = pltpu.roll(block, 20 * q, 1) if q else block
+            total = block if total is None else total + block
+        out[...] = total
+
+
+def pack(grouped):
+    recordings, piece_rows, _ = grouped.shape
+    return pl.pallas_call(
+        pack_kernel,
+        out_shape=[sds((piece_rows // PACK, 128), F32)] * recordings,
+        in_specs=[VM],
+        out_specs=[VM] * recordings,
+        compiler_params=params(),
+        cost_estimate=cost(1 << 16, 1 << 17),
+        name="pack",
+    )(grouped)
+
+
 def audio_kernel(
     special, lengths, p0, p1, p2, p3, w0_ref, gain_ref, shift_ref, a0_ref, head_ref, keep, samples, pre0, ahead
 ):
     here = Place(special)
-    piece_rows = p0.shape[0]
+    part = p0.shape[0]
+    piece_rows = PACK * part
     groups = 4 * piece_rows
     channels = gain_ref.shape[1]
     length = lengths[here.b]
     base = here.t * groups
-    samples[...] = jnp.zeros_like(samples)
     for k, piece in enumerate((p0, p1, p2, p3)):
-        place = pl.multiple_of((here.b ^ k) * piece_rows, 8)
-        samples[pl.ds(place, piece_rows), 0:20] = piece[...]
+        for q in range(PACK):
+            place = pl.multiple_of((here.b ^ k) * piece_rows + q * part, 8)
+            block = piece[...]
+            samples[pl.ds(place, part), :] = pltpu.roll(block, 128 - 20 * q, 1) if q else block
     row = lax.broadcasted_iota(jnp.int32, (groups, 128), 0)
     lane = lax.broadcasted_iota(jnp.int32, (groups, 128), 1)
     s = jnp.where(((base + row) * 20 + lane < length) & (lane < 20), samples[...], 0.0)
@@ -195,7 +226,7 @@
 
 
 def audio_layer(lengths, pieces, w0, gain, shift, special):
-    groups = 4 * pieces[0].shape[0]
+    groups = 4 * PACK * pieces[0].shape[0]
     channels = gain.shape[1]
     return pl.pallas_call(
         functools.partial(audio_kernel, special),
@@ -394,7 +425,7 @@
     )(lengths, a0, head, kept, *edges, w0, kernel1, kernel2, bias, gain, shift, cot)
 
 
-def window_kernel(d2_ref, k2_ref, dwin, behind):
+def window_kernel(d2_ref, k2_ref, hat_ref, slope_ref, rstd_ref, d1, dwin, behind):
     groups, channels = dwin.shape[1:]
     rows = groups + TAIL
     d2 = d2_ref[...]
@@ -403,27 +434,6 @@
     behind[7:8, :] = third[rows - 1 : rows, :]
     dwin[0] = dot_nt(d2[0:groups, :], k2_ref[0:channels, :])
     dwin[1] = dot_nt(d2[0:groups, :], k2_ref[channels : 2 * channels, :])
-
-
-def window(d2, kernel2):
-    rows, channels = d2.shape
-    groups = rows - TAIL
-    return pl.pallas_call(
-        window_kernel,
-        out_shape=[sds((2, groups, channels), F32), sds((groups + 8, channels), F32)],
-        in_specs=[VM] * 2,
-        out_specs=[VM] * 2,
-        compiler_params=params(),
-        cost_estimate=cost(int(1.5e9), 3 << 20),
-        name="window",
-    )(d2, kernel2)
-
-
-def backward_kernel(
-    special, behind, dwin, a0_ref, hat_ref, slope_ref, rstd_ref, order_ref, keep_ref, send_ref, d1
-):
-    here = Place(special)
-    groups, channels = dwin.shape[1:]
 
     def step(i, carry):
         start = pl.multiple_of(i * CH3, CH3)
@@ -441,6 +451,29 @@
         return carry
 
     lax.fori_loop(0, groups // CH3, step, 0, unroll=UN3)
+
+
+def window(d2, kernel2, hat, slope, rstd):
+    rows, channels = d2.shape
+    groups = rows - TAIL
+    return pl.pallas_call(
+        window_kernel,
+        out_shape=sds((2, groups, channels), BF16),
+        in_specs=[VM] * 5,
+        out_specs=VM,
+        scratch_shapes=[
+            pltpu.VMEM((2, groups, channels), F32),
+            pltpu.VMEM((groups + 8, channels), F32),
+        ],
+        compiler_params=params(16),
+        cost_estimate=cost(int(1.5e9), 3 << 20),
+        name="window",
+    )(d2, kernel2, hat, slope, rstd)
+
+
+def backward_kernel(special, d1, a0_ref, order_ref, keep_ref, send_ref):
+    here = Place(special)
+    channels = d1.shape[2]
     put_gradient(
         here.core,
         keep_ref,
@@ -450,21 +483,17 @@
     )
 
 
-def backward(behind, dwin, a0, hat, slope, rstd, order, taps_all, chunks, special):
-    groups, channels = dwin.shape[1:]
+def backward(d1, a0, order, taps_all, chunks, special):
     grad = (2, chunks, taps_all // chunks, BC)
     return pl.pallas_call(
         functools.partial(backward_kernel, special),
         out_shape=[sds(grad, F32), sds(grad, BF16)],
-        in_specs=[VM] * 6 + [pl.BlockSpec(memory_space=pl.ANY)],
+        in_specs=[VM] * 2 + [pl.BlockSpec(memory_space=pl.ANY)],
         out_specs=[VM] * 2,
-        scratch_shapes=[
-            pltpu.VMEM((2, groups, channels), BF16),
-        ],
-        compiler_params=params(20),
+        compiler_params=params(16),
         cost_estimate=cost(int(4e9), 10 << 20),
         name="backward",
-    )(behind, dwin, a0, hat, slope, rstd, order)
+    )(d1, a0, order)
 
 
 def plane_kernel(keep_ref, recv_ref, *outs):
@@ -500,7 +529,7 @@
         in_specs=[VM] * 4,
         out_specs=VM,
         compiler_params=params(),
-        cost_estimate=cost(1 << 20, 8 << 20),
+        cost_estimate=cost(int(1e10), 8 << 20),
         name="collect",
     )(own, rx, ry, rd)
 
@@ -613,25 +642,21 @@
                     pairs.append((tt * batches + bb, to[0] * batches + to[1]))
         return pairs
 
-    grouped = audio.reshape(recordings, piece_rows, 20)
-    pieces = []
-    for k in range(batches):
-        piece = lax.dynamic_index_in_dim(grouped, b ^ k, 0, False)
-        if k:
-            piece = permute(piece, route(lambda tt, bb: (tt, bb ^ k)))
-        pieces.append(piece)
-
-    def of_place(place, row):
-        chosen = pieces[0][row]
+    pieces = list(pack(audio.reshape(recordings, piece_rows, 20)))
+    for k in range(1, batches):
+        pieces[k] = permute(pieces[k], route(lambda tt, bb: (tt, bb ^ k)))
+
+    def of_place(place, row, lane):
+        chosen = pieces[0][row, lane : lane + 20]
         for k in range(1, batches):
-            chosen = jnp.where((b ^ k) == place, pieces[k][row], chosen)
+            chosen = jnp.where((b ^ k) == place, pieces[k][row, lane : lane + 20], chosen)
         return chosen[None]
 
     cot = cotangent[0]
-    first_group = jnp.pad(of_place(0, 0), ((0, 0), (0, 108 + cot.shape[1])))
+    first_group = jnp.pad(of_place(0, 0, 0), ((0, 0), (0, 108 + cot.shape[1])))
     last_group = jnp.concatenate(
         [
-            jnp.pad(of_place(batches - 1, piece_rows - 1), ((0, 0), (0, 108))),
+            jnp.pad(of_place(batches - 1, -1, 20 * (PACK - 1)), ((0, 0), (0, 108))),
             cot[groups - 1 :].astype(F32),
         ],
         1,
@@ -663,10 +688,10 @@
         chunks,
         special,
     )
-    dwin, behind = window(d2, kernel2)
+    d1 = window(d2, kernel2, hat, slope, rstd)
 
     def gradient_one(order):
-        return backward(behind, dwin, a0, hat, slope, rstd, order, kernel1.shape[0], chunks, special)
+        return backward(d1, a0, order, kernel1.shape[0], chunks, special)
 
     if not special:
         keep1, send1 = gradient_one(keep2)

time: 74.8 us -> 70.7 us (0.945)
  waiting for transfers between devices: 29.8 us -> 25.8 us
    ppermute x18, waiting for transfers between devices: 29.8 us -> 25.8 us  [permute(): return lax.ppermute(value, AXES, route)]
    pallas_call x1 -> x2, Pallas kernels: 0.81 us -> 1.82 us  [the longest x1 1.71 us: window(): pl.pallas_call(window_kernel, out_shape=sds((2, groups, channels), BF16),...]
    pallas_call x1, Pallas kernels: 2.76 us -> 1.84 us  [backward(): pl.pallas_call(functools.partial(backward_kernel, special), out_shape=[sd...]
    unnamed x20 -> x22, local copies, waits for them, and re-layouts: 1.5 us -> 1.5 us
  transfers between devices with their start and end apart: 18 -> 18, of which waited for: 10 -> 10; matrix products, arithmetic and copies ran while one was open for 1% -> 1% of each run, Pallas kernels for 8% -> 12%
where the time goes in v3:
time: 70.7 us; the launch traced here: 70.4 us
  waiting for transfers between devices  25.8 us (36%)
  starting transfers between devices  21.1 us (30%)
  Pallas kernels  19.3 us (27%)
  local copies, waits for them, and re-layouts  2.49 us (4%)
  between operations  0.9 us (1%)
  other arithmetic  0.8 us (1%)
    ppermute x18, waiting for transfers between devices, permute(): return lax.ppermute(value, AXES, route)  25.8 us
    ppermute x18, starting transfers between devices, permute(): return lax.ppermute(value, AXES, route)  21.1 us
    pallas_call x1, Pallas kernels, forward(): pl.pallas_call(functools.partial(forward_kernel, special, groups, scale),...  8.16 us
    pallas_call x1, Pallas kernels, audio_layer(): pl.pallas_call(functools.partial(audio_kernel, special), out_shape=[sds((...  4.87 us
    pallas_call x1, Pallas kernels, stats(): pl.pallas_call(stats_kernel, out_shape=[sds(lprev.shape, F32), sds(rprev....  1.89 us
    pallas_call x1, Pallas kernels, backward(): pl.pallas_call(functools.partial(backward_kernel, special), out_shape=[sd...  1.84 us
    pallas_call x1, Pallas kernels, window(): pl.pallas_call(window_kernel, out_shape=sds((2, groups, channels), BF16),...  1.71 us
    unnamed x22, local copies, waits for them, and re-layouts  1.5 us
  transfers between devices with their start and end apart: 18, of which 10 were waited for; matrix products, arithmetic and copies ran while one was open for 1% of the time, Pallas kernels for 12%

profile of v3, /device:TPU:0, one launch (start us, length us, event | category | flops | bytes accessed | tf_op | source)
XLA Modules:
  0.0 70.4 jit_solution(938569632034792859)
XLA Ops:
  0.7 1.0 %reshape.24.grouped = f32[4,96,20]{2,1,0:T(8,128)S(1)} reshape(f32[4,1920]{1,0:T(4,128)} %param.11) | data formatting | bytes 61440 | tf_op jit(solution)/shard_map/reshape | solution.py:645
  1.8 0.5 collective-permute-start
  2.3 2.6 %collective-permute-start.1 = (f32[16,128]{1,0:T(8,128)S(1)}, f32[16,128]{1,0:T(8,128)S(1)}, u32[]{:S(2)}, u32[]{:S(2)}) collective-permute-start(f32[16,128]{1,0:T(8,128)S(1)} %get-tuple-element.36), channel_id=1, source_target_pairs={{0,2},{1,3},{2,0},{3,1},{4,6},{5,7},{6,4},{7,5},{8,10},{9,11},{10,... | collective-permute-start | bytes 24584 | tf_op jit(solution)/shard_map/ppermute | solution.py:612
  4.9 0.7 bitcast_convert_fusion
  5.6 0.8 %copy-done.3 = f32[10,512]{1,0:T(8,128)S(1)} copy-done((f32[10,512]{1,0:T(8,128)S(1)}, f32[10,512]{1,0:T(8,128)}, u32[]{:S(2)}) %copy-start.3) | copy-done | bytes 20504
  6.4 0.7 copy-done.4
  7.3 0.6 collective-permute-done.2.p3
  8.0 0.7 collective-permute-start.4
  8.7 4.4 %collective-permute-start.3 = (f32[1,640]{1,0:T(1,128)S(1)}, f32[1,640]{1,0:T(1,128)S(1)}, u32[]{:S(2)}, u32[]{:S(2)}) collective-permute-start(f32[1,640]{1,0:T(1,128)S(1)} %get-tuple-element.68), channel_id=1, source_target_pairs={{0,4},{1,5},{2,6},{3,7},{4,0},{5,1},{6,2},{7,3},{8,12},{9,13},{10,... | collective-permute-start | bytes 7688 | tf_op jit(solution)/shard_map/ppermute | solution.py:612
  13.1 4.9 %audio_layer.1 = (bf16[384,2560]{1,0:T(8,128)(2,1)S(1)}, f32[8,512]{1,0:T(8,128)S(1)}, f32[24,128]{1,0:T(8,128)S(1)}) custom-call(s32[4]{0:T(128)S(1)} %copy-done.10, f32[16,128]{1,0:T(8,128)S(1)} %get-tuple-element.34.p0, f32[16,128]{1,0:T(8,128)S(1)} %collective-permute-done.p1, f32[16,128]{1,0:T(8,128)S(1)} %collective-permute-done.1.p2, ...), custom_call_target="tpu_custom_call" | custom-call | flops 3000000000 | bytes 5242880 | tf_op jit(solution)/shard_map/audio_layer/pallas_call | solution.py:231
  18.0 8.2 %forward.1 = (bf16[400,2560]{1,0:T(8,128)(2,1)S(1)}, bf16[384,512]{1,0:T(8,128)(2,1)}, f32[2,4,384,128]{3,2,1,0:T(8,128)S(1)}, bf16[2,4,384,128]{3,2,1,0:T(8,128...) custom-call(s32[4]{0:T(128)S(1)} %copy-done.10, ...), custom_call_target="tpu_custom_call" | custom-call | flops 8000000000 | bytes 10485760 | tf_op jit(solution)/shard_map/forward/pallas_call | solution.py:400
  26.2 1.7 %window.1.d1 = bf16[2,384,512]{2,1,0:T(8,128)(2,1)S(1)} custom-call(bf16[400,512]{1,0:T(8,128)(2,1)S(1)} %get-tuple-element.42.d2_ref, bf16[1536,512]{1,0:T(8,128)(2,1)S(1)} %copy-done.1, f32[2,400,512]{2,1,0:T(8,128)S(1)} %get-tuple-element.43.hat_ref, f32[2,400,512]{2,1,0:T(8,128)S(1)} %get-tuple-element.44.slope_ref, ...), custom_call_target="tpu_custom_call" | custom-call | flops 1500000000 | bytes 3145728 | tf_op jit(solution)/shard_map/window/pallas_call | solution.py:459
  28.0 0.6 collective-permute-done.5.recv_ref
  28.6 1.2 %collective-permute-start.7 = (bf16[2,384,128]{2,1,0:T(8,128)(2,1)S(1)}, bf16[2,384,128]{2,1,0:T(8,128)(2,1)S(1)}, u32[]{:S(2)}, u32[]{:S(2)}) collective-permute-start(bf16[2,384,128]{2,1,0:T(8,128)(2,1)S(1)} %get-tuple-element.52), channel_id=1, source_target_pairs={{0,2},{1,3},{2,0},{3,1},{4,6},{5,7},{6,4},{7,5},{8,10},{9,11},{10,... | collective-permute-start | bytes 589832 | tf_op jit(solution)/shard_map/ppermute | solution.py:612
  29.8 2.4 %collective-permute-start.9 = (bf16[2,384,128]{2,1,0:T(8,128)(2,1)S(1)}, bf16[2,384,128]{2,1,0:T(8,128)(2,1)S(1)}, u32[]{:S(2)}, u32[]{:S(2)}) collective-permute-start(bf16[2,384,128]{2,1,0:T(8,128)(2,1)S(1)} %get-tuple-element.54), channel_id=1, source_target_pairs={{0,6},{1,7},{2,4},{3,5},{4,2},{5,3},{6,0},{7,1},{8,14},{9,15},{10,... | collective-permute-start | bytes 589832 | tf_op jit(solution)/shard_map/ppermute | solution.py:612
  32.2 1.8 %backward.1 = (f32[2,4,384,128]{3,2,1,0:T(8,128)S(1)}, bf16[2,4,384,128]{3,2,1,0:T(8,128)(2,1)S(1)}) custom-call(bf16[2,384,512]{2,1,0:T(8,128)(2,1)S(1)} %window.1.d1, bf16[400,2560]{1,0:T(8,128)(2,1)S(1)} %get-tuple-element.46.a0_ref, f32[2,384,128]{2,1,0:T(8,128)S(1)} %get-tuple-element.49.order_ref.own), custom_call_target="tpu_custom_call" | custom-call | flops 4000000000 | bytes 10485760 | tf_op jit(solution)/shard_map/backward/pallas_call | solution.py:488
  34.1 2.3 %collective-permute-done.7.rx = bf16[2,384,128]{2,1,0:T(8,128)(2,1)S(1)} collective-permute-done((bf16[2,384,128]{2,1,0:T(8,128)(2,1)S(1)}, bf16[2,384,128]{2,1,0:T(8,128)(2,1)S(1)}, u32[]{:S(2)}, u32[]{:S(2)}) %collective-permute-start.7) | collective-permute-done | bytes 196640 | tf_op jit(solution)/shard_map/ppermute | solution.py:612
  36.5 4.2 %collective-permute-done.8.ry = bf16[2,384,128]{2,1,0:T(8,128)(2,1)S(1)} collective-permute-done((bf16[2,384,128]{2,1,0:T(8,128)(2,1)S(1)}, bf16[2,384,128]{2,1,0:T(8,128)(2,1)S(1)}, u32[]{:S(2)}, u32[]{:S(2)}) %collective-permute-start.8) | collective-permute-done | bytes 196640 | tf_op jit(solution)/shard_map/ppermute | solution.py:612
  41.0 1.0 %collective-permute-start.10 = (bf16[2,384,128]{2,1,0:T(8,128)(2,1)S(1)}, bf16[2,384,128]{2,1,0:T(8,128)(2,1)S(1)}, u32[]{:S(2)}, u32[]{:S(2)}) collective-permute-start(bf16[2,384,128]{2,1,0:T(8,128)(2,1)S(1)} %get-tuple-element.56), channel_id=1, source_target_pairs={{0,2},{1,3},{2,0},{3,1},{4,6},{5,7},{6,4},{7,5},{8,10},{9,11},{10,... | collective-permute-start | bytes 589832 | tf_op jit(solution)/shard_map/ppermute | solution.py:612
  42.0 0.8 %collective-permute-start.11 = (bf16[2,384,128]{2,1,0:T(8,128)(2,1)S(1)}, bf16[2,384,128]{2,1,0:T(8,128)(2,1)S(1)}, u32[]{:S(2)}, u32[]{:S(2)}) collective-permute-start(bf16[2,384,128]{2,1,0:T(8,128)(2,1)S(1)} %get-tuple-element.57), channel_id=1, source_target_pairs={{0,4},{1,5},{2,6},{3,7},{4,0},{5,1},{6,2},{7,3},{8,12},{9,13},{10,... | collective-permute-start | bytes 589832 | tf_op jit(solution)/shard_map/ppermute | solution.py:612
  42.8 1.8 %collective-permute-start.12 = (bf16[2,384,128]{2,1,0:T(8,128)(2,1)S(1)}, bf16[2,384,128]{2,1,0:T(8,128)(2,1)S(1)}, u32[]{:S(2)}, u32[]{:S(2)}) collective-permute-start(bf16[2,384,128]{2,1,0:T(8,128)(2,1)S(1)} %get-tuple-element.58), channel_id=1, source_target_pairs={{0,6},{1,7},{2,4},{3,5},{4,2},{5,3},{6,0},{7,1},{8,14},{9,15},{10,... | collective-permute-start | bytes 589832 | tf_op jit(solution)/shard_map/ppermute | solution.py:612
  44.5 4.3 %collective-permute-done.10.rx = bf16[2,384,128]{2,1,0:T(8,128)(2,1)S(1)} collective-permute-done((bf16[2,384,128]{2,1,0:T(8,128)(2,1)S(1)}, bf16[2,384,128]{2,1,0:T(8,128)(2,1)S(1)}, u32[]{:S(2)}, u32[]{:S(2)}) %collective-permute-start.10) | collective-permute-done | bytes 196640 | tf_op jit(solution)/shard_map/ppermute | solution.py:612
  48.9 3.0 %collective-permute-done.11.ry = bf16[2,384,128]{2,1,0:T(8,128)(2,1)S(1)} collective-permute-done((bf16[2,384,128]{2,1,0:T(8,128)(2,1)S(1)}, bf16[2,384,128]{2,1,0:T(8,128)(2,1)S(1)}, u32[]{:S(2)}, u32[]{:S(2)}) %collective-permute-start.11) | collective-permute-done | bytes 196640 | tf_op jit(solution)/shard_map/ppermute | solution.py:612
  52.0 1.6 %collective-permute-start.13 = (bf16[384,128]{1,0:T(8,128)(2,1)S(1)}, bf16[384,128]{1,0:T(8,128)(2,1)S(1)}, u32[]{:S(2)}, u32[]{:S(2)}) collective-permute-start(bf16[384,128]{1,0:T(8,128)(2,1)S(1)} %get-tuple-element.60), channel_id=1, source_target_pairs={{0,8},{1,9},{2,10},{3,11},{4,12},{5,13},{6,14},{7,15},{8,0},{9,1},... | collective-permute-start | bytes 294920 | tf_op jit(solution)/shard_map/ppermute | solution.py:612
  53.6 2.0 %collective-permute-start.14 = (bf16[384,128]{1,0:T(8,128)(2,1)S(1)}, bf16[384,128]{1,0:T(8,128)(2,1)S(1)}, u32[]{:S(2)}, u32[]{:S(2)}) collective-permute-start(bf16[384,128]{1,0:T(8,128)(2,1)S(1)} %get-tuple-element.61), channel_id=1, source_target_pairs={{0,16},{1,17},{2,18},{3,19},{4,20},{5,21},{6,22},{7,23},{8,24},{9,... | collective-permute-start | bytes 294920 | tf_op jit(solution)/shard_map/ppermute | solution.py:612
  55.6 0.8 %collective-permute-start.15 = (bf16[384,128]{1,0:T(8,128)(2,1)S(1)}, bf16[384,128]{1,0:T(8,128)(2,1)S(1)}, u32[]{:S(2)}, u32[]{:S(2)}) collective-permute-start(bf16[384,128]{1,0:T(8,128)(2,1)S(1)} %get-tuple-element.62), channel_id=1, source_target_pairs={{0,24},{1,25},{2,26},{3,27},{4,28},{5,29},{6,30},{7,31},{8,16},{9,... | collective-permute-start | bytes 294920 | tf_op jit(solution)/shard_map/ppermute | solution.py:612
  56.4 0.4 collective-permute-done.13.a
  56.9 5.3 %collective-permute-done.14.b = bf16[384,128]{1,0:T(8,128)(2,1)S(1)} collective-permute-done((bf16[384,128]{1,0:T(8,128)(2,1)S(1)}, bf16[384,128]{1,0:T(8,128)(2,1)S(1)}, u32[]{:S(2)}, u32[]{:S(2)}) %collective-permute-start.14) | collective-permute-done | bytes 98336 | tf_op jit(solution)/shard_map/ppermute | solution.py:612
  62.2 1.2 %collective-permute-start.16 = (bf16[384,128]{1,0:T(8,128)(2,1)S(1)}, bf16[384,128]{1,0:T(8,128)(2,1)S(1)}, u32[]{:S(2)}, u32[]{:S(2)}) collective-permute-start(bf16[384,128]{1,0:T(8,128)(2,1)S(1)} %final.1.own), channel_id=1, source_target_pairs={{0,2},{1,3},{2,0},{3,1},{4,6},{5,7},{6,4},{7,5},{8,10},{9,11},{10,... | collective-permute-start | bytes 294920 | tf_op jit(solution)/shard_map/ppermute | solution.py:612
  63.4 3.5 %collective-permute-done.16.other = bf16[384,128]{1,0:T(8,128)(2,1)S(1)} collective-permute-done((bf16[384,128]{1,0:T(8,128)(2,1)S(1)}, bf16[384,128]{1,0:T(8,128)(2,1)S(1)}, u32[]{:S(2)}, u32[]{:S(2)}) %collective-permute-start.16) | collective-permute-done | bytes 98336 | tf_op jit(solution)/shard_map/ppermute | solution.py:612
  67.0 1.4 %collective-permute-done.17.pair = bf16[2,384,128]{2,1,0:T(8,128)(2,1)S(1)} collective-permute-done((bf16[2,384,128]{2,1,0:T(8,128)(2,1)S(1)}, bf16[2,384,128]{2,1,0:T(8,128)(2,1)S(1)}, u32[]{:S(2)}, u32[]{:S(2)}) %collective-permute-start.17) | collective-permute-done | bytes 196640 | tf_op jit(solution)/shard_map/ppermute | solution.py:612
  68.5 1.9 %stats.1 = (f32[8,192,192]{2,1,0:T(8,128)}, f32[8,128,128]{2,1,0:T(8,128)}) custom-call(bf16[384,128]{1,0:T(8,128)(2,1)S(1)} %final.1.own, bf16[384,128]{1,0:T(8,128)(2,1)S(1)} %collective-permute-done.16.other, bf16[2,384,128]{2,1,0:T(8,128)(2,1)S(1)} %collective-permute-done.17.pair, f32[8,192,192]{2,1,0:T(8,128)S(1)} %copy-done, f32[8,128,128]{2,1,0:T(8,128)S(1)} %copy-done.2), custom_call_target="tpu_custom_call" | custom-call | flops 200000000 | bytes 4194304 | tf_op jit(solution)/shard_map/stats/pallas_call | solution.py:600
  (43 shorter events, 1.3 us)
Async XLA Ops:
  0.6 12.5 %copy-start.9 = (f32[3,512]{1,0:T(4,128)S(1)}, f32[3,512]{1,0:T(4,128)}, u32[]{:S(2)}) copy-start(f32[3,512]{1,0:T(4,128)} %shift_ref.3) | copy-start | bytes 18436
  0.6 12.5 %copy-start.8 = (f32[3,512]{1,0:T(4,128)S(1)}, f32[3,512]{1,0:T(4,128)}, u32[]{:S(2)}) copy-start(f32[3,512]{1,0:T(4,128)} %gain_ref.3) | copy-start | bytes 18436
  0.7 12.4 %copy-start.10 = (s32[4]{0:T(128)S(1)}, s32[4]{0:T(128)}, u32[]{:S(2)}) copy-start(s32[4]{0:T(128)} %lengths.3) | copy-start | bytes 52
  1.8 5.5 %collective-permute-start = (f32[16,128]{1,0:T(8,128)S(1)}, f32[16,128]{1,0:T(8,128)S(1)}, u32[]{:S(2)}, u32[]{:S(2)}) collective-permute-start(f32[16,128]{1,0:T(8,128)S(1)} %get-tuple-element.35), channel_id=1, source_target_pairs={{0,1},{1,0},{2,3},{3,2},{4,5},{5,4},{6,7},{7,6},{8,9},{9,8},{10,11... | collective-permute-start | bytes 24584 | tf_op jit(solution)/shard_map/ppermute | solution.py:612
  2.3 5.0 %collective-permute-start.1 = (f32[16,128]{1,0:T(8,128)S(1)}, f32[16,128]{1,0:T(8,128)S(1)}, u32[]{:S(2)}, u32[]{:S(2)}) collective-permute-start(f32[16,128]{1,0:T(8,128)S(1)} %get-tuple-element.36), channel_id=1, source_target_pairs={{0,2},{1,3},{2,0},{3,1},{4,6},{5,7},{6,4},{7,5},{8,10},{9,11},{10,... | collective-permute-start | bytes 24584 | tf_op jit(solution)/shard_map/ppermute | solution.py:612
  4.9 3.1 %collective-permute-start.2 = (f32[16,128]{1,0:T(8,128)S(1)}, f32[16,128]{1,0:T(8,128)S(1)}, u32[]{:S(2)}, u32[]{:S(2)}) collective-permute-start(f32[16,128]{1,0:T(8,128)S(1)} %get-tuple-element.37), channel_id=1, source_target_pairs={{0,3},{1,2},{2,1},{3,0},{4,7},{5,6},{6,5},{7,4},{8,11},{9,10},{10,... | collective-permute-start | bytes 24584 | tf_op jit(solution)/shard_map/ppermute | solution.py:612
  5.6 0.8 %copy-start.3 = (f32[10,512]{1,0:T(8,128)S(1)}, f32[10,512]{1,0:T(8,128)}, u32[]{:S(2)}) copy-start(f32[10,512]{1,0:T(8,128)} %k0_ref.1) | copy-start | bytes 61444
  6.4 0.7 copy-start.4
  8.0 10.0 %collective-permute-start.4 = (f32[1,640]{1,0:T(1,128)S(1)}, f32[1,640]{1,0:T(1,128)S(1)}, u32[]{:S(2)}, u32[]{:S(2)}) collective-permute-start(f32[1,640]{1,0:T(1,128)S(1)} %get-tuple-element.67), channel_id=1, source_target_pairs={{4,8},{5,9},{6,10},{7,11},{8,4},{9,5},{10,6},{11,7},{12,16},{13,17... | collective-permute-start | bytes 7688 | tf_op jit(solution)/shard_map/ppermute | solution.py:612
  8.7 9.3 %copy-start.1 = (bf16[1536,512]{1,0:T(8,128)(2,1)S(1)}, bf16[1536,512]{1,0:T(8,128)(2,1)}, u32[]{:S(2)}) copy-start(bf16[1536,512]{1,0:T(8,128)(2,1)} %k2_ref.3) | copy-start | bytes 4718596
  8.7 9.3 %copy-start.5 = (f32[3,512]{1,0:T(4,128)S(1)}, f32[3,512]{1,0:T(4,128)}, u32[]{:S(2)}) copy-start(f32[3,512]{1,0:T(4,128)} %bias_ref.3) | copy-start | bytes 18436
  8.7 9.3 %copy-start.6 = (bf16[1,384,512]{2,1,0:T(8,128)(2,1)S(1)}, bf16[1,384,512]{2,1,0:T(8,128)(2,1)}, u32[]{:S(2)}) copy-start(bf16[1,384,512]{2,1,0:T(8,128)(2,1)} %param.19) | copy-start | bytes 1179652
  8.7 9.3 %copy-start.7 = (bf16[1536,512]{1,0:T(8,128)(2,1)S(1)}, bf16[1536,512]{1,0:T(8,128)(2,1)}, u32[]{:S(2)}) copy-start(bf16[1536,512]{1,0:T(8,128)(2,1)} %k1_ref.1) | copy-start | bytes 4718596
  8.7 9.3 %collective-permute-start.3 = (f32[1,640]{1,0:T(1,128)S(1)}, f32[1,640]{1,0:T(1,128)S(1)}, u32[]{:S(2)}, u32[]{:S(2)}) collective-permute-start(f32[1,640]{1,0:T(1,128)S(1)} %get-tuple-element.68), channel_id=1, source_target_pairs={{0,4},{1,5},{2,6},{3,7},{4,0},{5,1},{6,2},{7,3},{8,12},{9,13},{10,... | collective-permute-start | bytes 7688 | tf_op jit(solution)/shard_map/ppermute | solution.py:612
  26.2 2.3 %collective-permute-start.5 = (bf16[2,4,384,128]{3,2,1,0:T(8,128)(2,1)S(1)}, bf16[2,4,384,128]{3,2,1,0:T(8,128)(2,1)S(1)}, u32[]{:S(2)}, u32[]{:S(2)}) collective-permute-start(bf16[2,4,384,128]{3,2,1,0:T(8,128)(2,1)S(1)} %get-tuple-element.48), channel_id=1, source_target_pairs={{0,1},{1,0},{2,3},{3,2},{4,5},{5,4},{6,7},{7,6},{8,9},{9,8},{10,11... | collective-permute-start | bytes 2359304 | tf_op jit(solution)/shard_map/ppermute | solution.py:612
  28.6 7.8 %collective-permute-start.7 = (bf16[2,384,128]{2,1,0:T(8,128)(2,1)S(1)}, bf16[2,384,128]{2,1,0:T(8,128)(2,1)S(1)}, u32[]{:S(2)}, u32[]{:S(2)}) collective-permute-start(bf16[2,384,128]{2,1,0:T(8,128)(2,1)S(1)} %get-tuple-element.52), channel_id=1, source_target_pairs={{0,2},{1,3},{2,0},{3,1},{4,6},{5,7},{6,4},{7,5},{8,10},{9,11},{10,... | collective-permute-start | bytes 589832 | tf_op jit(solution)/shard_map/ppermute | solution.py:612
  29.8 10.9 %collective-permute-start.8 = (bf16[2,384,128]{2,1,0:T(8,128)(2,1)S(1)}, bf16[2,384,128]{2,1,0:T(8,128)(2,1)S(1)}, u32[]{:S(2)}, u32[]{:S(2)}) collective-permute-start(bf16[2,384,128]{2,1,0:T(8,128)(2,1)S(1)} %get-tuple-element.53), channel_id=1, source_target_pairs={{0,4},{1,5},{2,6},{3,7},{4,0},{5,1},{6,2},{7,3},{8,12},{9,13},{10,... | collective-permute-start | bytes 589832 | tf_op jit(solution)/shard_map/ppermute | solution.py:612
  29.8 10.8 %collective-permute-start.9 = (bf16[2,384,128]{2,1,0:T(8,128)(2,1)S(1)}, bf16[2,384,128]{2,1,0:T(8,128)(2,1)S(1)}, u32[]{:S(2)}, u32[]{:S(2)}) collective-permute-start(bf16[2,384,128]{2,1,0:T(8,128)(2,1)S(1)} %get-tuple-element.54), channel_id=1, source_target_pairs={{0,6},{1,7},{2,4},{3,5},{4,2},{5,3},{6,0},{7,1},{8,14},{9,15},{10,... | collective-permute-start | bytes 589832 | tf_op jit(solution)/shard_map/ppermute | solution.py:612
  34.0 6.7 %collective-permute-start.6 = (bf16[2,4,384,128]{3,2,1,0:T(8,128)(2,1)S(1)}, bf16[2,4,384,128]{3,2,1,0:T(8,128)(2,1)S(1)}, u32[]{:S(2)}, u32[]{:S(2)}) collective-permute-start(bf16[2,4,384,128]{3,2,1,0:T(8,128)(2,1)S(1)} %get-tuple-element.51), channel_id=1, source_target_pairs={{0,1},{1,0},{2,3},{3,2},{4,5},{5,4},{6,7},{7,6},{8,9},{9,8},{10,11... | collective-permute-start | bytes 2359304 | tf_op jit(solution)/shard_map/ppermute | solution.py:612
  40.9 27.5 %copy-start = (f32[8,192,192]{2,1,0:T(8,128)S(1)}, f32[8,192,192]{2,1,0:T(8,128)}, u32[]{:S(2)}) copy-start(f32[8,192,192]{2,1,0:T(8,128)} %lprev.1) | copy-start | bytes 3538948
  40.9 27.5 %copy-start.2 = (f32[8,128,128]{2,1,0:T(8,128)S(1)}, f32[8,128,128]{2,1,0:T(8,128)}, u32[]{:S(2)}) copy-start(f32[8,128,128]{2,1,0:T(8,128)} %rprev.1) | copy-start | bytes 1572868
  41.0 7.9 %collective-permute-start.10 = (bf16[2,384,128]{2,1,0:T(8,128)(2,1)S(1)}, bf16[2,384,128]{2,1,0:T(8,128)(2,1)S(1)}, u32[]{:S(2)}, u32[]{:S(2)}) collective-permute-start(bf16[2,384,128]{2,1,0:T(8,128)(2,1)S(1)} %get-tuple-element.56), channel_id=1, source_target_pairs={{0,2},{1,3},{2,0},{3,1},{4,6},{5,7},{6,4},{7,5},{8,10},{9,11},{10,... | collective-permute-start | bytes 589832 | tf_op jit(solution)/shard_map/ppermute | solution.py:612
  42.0 9.9 %collective-permute-start.11 = (bf16[2,384,128]{2,1,0:T(8,128)(2,1)S(1)}, bf16[2,384,128]{2,1,0:T(8,128)(2,1)S(1)}, u32[]{:S(2)}, u32[]{:S(2)}) collective-permute-start(bf16[2,384,128]{2,1,0:T(8,128)(2,1)S(1)} %get-tuple-element.57), channel_id=1, source_target_pairs={{0,4},{1,5},{2,6},{3,7},{4,0},{5,1},{6,2},{7,3},{8,12},{9,13},{10,... | collective-permute-start | bytes 589832 | tf_op jit(solution)/shard_map/ppermute | solution.py:612
  42.8 9.1 %collective-permute-start.12 = (bf16[2,384,128]{2,1,0:T(8,128)(2,1)S(1)}, bf16[2,384,128]{2,1,0:T(8,128)(2,1)S(1)}, u32[]{:S(2)}, u32[]{:S(2)}) collective-permute-start(bf16[2,384,128]{2,1,0:T(8,128)(2,1)S(1)} %get-tuple-element.58), channel_id=1, source_target_pairs={{0,6},{1,7},{2,4},{3,5},{4,2},{5,3},{6,0},{7,1},{8,14},{9,15},{10,... | collective-permute-start | bytes 589832 | tf_op jit(solution)/shard_map/ppermute | solution.py:612
  52.0 4.9 %collective-permute-start.13 = (bf16[384,128]{1,0:T(8,128)(2,1)S(1)}, bf16[384,128]{1,0:T(8,128)(2,1)S(1)}, u32[]{:S(2)}, u32[]{:S(2)}) collective-permute-start(bf16[384,128]{1,0:T(8,128)(2,1)S(1)} %get-tuple-element.60), channel_id=1, source_target_pairs={{0,8},{1,9},{2,10},{3,11},{4,12},{5,13},{6,14},{7,15},{8,0},{9,1},... | collective-permute-start | bytes 294920 | tf_op jit(solution)/shard_map/ppermute | solution.py:612
  53.6 8.6 %collective-permute-start.14 = (bf16[384,128]{1,0:T(8,128)(2,1)S(1)}, bf16[384,128]{1,0:T(8,128)(2,1)S(1)}, u32[]{:S(2)}, u32[]{:S(2)}) collective-permute-start(bf16[384,128]{1,0:T(8,128)(2,1)S(1)} %get-tuple-element.61), channel_id=1, source_target_pairs={{0,16},{1,17},{2,18},{3,19},{4,20},{5,21},{6,22},{7,23},{8,24},{9,... | collective-permute-start | bytes 294920 | tf_op jit(solution)/shard_map/ppermute | solution.py:612
  55.6 6.6 %collective-permute-start.15 = (bf16[384,128]{1,0:T(8,128)(2,1)S(1)}, bf16[384,128]{1,0:T(8,128)(2,1)S(1)}, u32[]{:S(2)}, u32[]{:S(2)}) collective-permute-start(bf16[384,128]{1,0:T(8,128)(2,1)S(1)} %get-tuple-element.62), channel_id=1, source_target_pairs={{0,24},{1,25},{2,26},{3,27},{4,28},{5,29},{6,30},{7,31},{8,16},{9,... | collective-permute-start | bytes 294920 | tf_op jit(solution)/shard_map/ppermute | solution.py:612
  62.2 4.7 %collective-permute-start.16 = (bf16[384,128]{1,0:T(8,128)(2,1)S(1)}, bf16[384,128]{1,0:T(8,128)(2,1)S(1)}, u32[]{:S(2)}, u32[]{:S(2)}) collective-permute-start(bf16[384,128]{1,0:T(8,128)(2,1)S(1)} %final.1.own), channel_id=1, source_target_pairs={{0,2},{1,3},{2,0},{3,1},{4,6},{5,7},{6,4},{7,5},{8,10},{9,11},{10,... | collective-permute-start | bytes 294920 | tf_op jit(solution)/shard_map/ppermute | solution.py:612
  67.0 1.5 %collective-permute-start.17 = (bf16[2,384,128]{2,1,0:T(8,128)(2,1)S(1)}, bf16[2,384,128]{2,1,0:T(8,128)(2,1)S(1)}, u32[]{:S(2)}, u32[]{:S(2)}) collective-permute-start(bf16[2,384,128]{2,1,0:T(8,128)(2,1)S(1)} %pad_maximum_fusion), channel_id=1, source_target_pairs={{0,1},{1,0},{2,3},{3,2},{4,5},{5,4},{6,7},{7,6},{8,9},{9,8},{10,11... | collective-permute-start | bytes 589832 | tf_op jit(solution)/shard_map/ppermute | solution.py:612

commit v4 on v3

--- a/solution.py
+++ b/solution.py
@@ -19,7 +19,7 @@
 CH = 16
 PACK = 6
 CH0, CH1, CH2, CH3 = 16,16,16,16
-UN0, UN1, UN2, UN3 = 4,25,6,6
+UN0, UN1, UN2, UN3 = 12, 25, 24, 24
 TAIL = 16
 
 VM = pl.BlockSpec(memory_space=pltpu.VMEM)
@@ -39,14 +39,8 @@
 
 
 def normal_cdf(z):
-    bell = jnp.exp(z * z * -0.5)
-    t = 1.0 / (1.0 + jnp.abs(z) * (0.3275911 / math.sqrt(2.0)))
-    poly = t * (0.5 * 1.061405429) + (0.5 * -1.453152027)
-    poly = poly * t + (0.5 * 1.421413741)
-    poly = poly * t + (0.5 * -0.284496736)
-    poly = poly * t + (0.5 * 0.254829592)
-    q = poly * t * bell
-    return jnp.where(z < 0.0, q, 1.0 - q), bell
+    bell = jnp.exp2(z * z * (-0.5 * math.log2(math.e)))
+    return 0.5 + 0.5 * lax.erf(z * math.sqrt(0.5)), bell
 
 
 INV_SQRT_2PI = 1.0 / math.sqrt(2.0 * math.pi)
@@ -59,15 +53,21 @@
     return hi, mid, rest - mid
 
 
-def prep_kernel(k0_ref, bias_ref, w_ref, wide):
-    channels = k0_ref.shape[1]
-    k0 = k0_ref[...]
+def prep_kernel(table_ref, w_ref, meta_ref, wide):
+    channels = table_ref.shape[1]
+    b = lax.axis_index("batch")
+    lane = lax.broadcasted_iota(jnp.int32, (1, channels), 1)
+    length = jnp.sum(jnp.where(lane == b, table_ref[20:21, :], 0.0), -1, keepdims=True)
+    length = jnp.broadcast_to(length.astype(jnp.int32), meta_ref.shape)
+    meta_row = lax.broadcasted_iota(jnp.int32, meta_ref.shape, 0)
+    meta_ref[...] = jnp.where(meta_row == 0, length, lax.div(length, 20))
+    wide[...] = jnp.zeros_like(wide)
+    k0 = table_ref[0:10, :]
     k0 = k0 - jnp.mean(k0, -1, keepdims=True)
-    bias = bias_ref[0:1, :]
+    bias = table_ref[10:11, :]
     bias = bias - jnp.mean(bias, -1, keepdims=True)
     parts = split3(k0)
     bparts = split3(bias)
-    wide[...] = jnp.zeros_like(wide)
     for block, part in enumerate((0, 1, 2, 0, 1, 0)):
         for g in range(4):
             cols = pl.ds(g * channels, channels)
@@ -77,18 +77,18 @@
     w_ref[...] = wide[...].astype(BF16)
 
 
-def prep(kernel0, conv_bias):
-    channels = kernel0.shape[1]
+def prep(table):
+    channels = table.shape[1]
     return pl.pallas_call(
         prep_kernel,
-        out_shape=sds((256, 4 * channels), BF16),
-        in_specs=[VM, VM],
-        out_specs=VM,
+        out_shape=[sds((256, 4 * channels), BF16), sds((8, channels), jnp.int32)],
+        in_specs=[VM],
+        out_specs=[VM] * 2,
         scratch_shapes=[pltpu.VMEM((256, 4 * channels), F32)],
         compiler_params=params(),
         cost_estimate=cost(4 * 256 * 2048, 1 << 20),
         name="prep",
-    )(kernel0, conv_bias)
+    )(table)
 
 
 def dot(a, b):
@@ -159,43 +159,48 @@
     lax.fori_loop(0, rows // CH, move, 0, unroll=2)
 
 
-def pack_kernel(grouped, *outs):
+def pack_kernel(audio, *refs):
+    outs, (local, packed) = refs[:-2], refs[-2:]
     b = lax.axis_index("batch")
-    piece_rows = grouped.shape[1]
-    part = piece_rows // PACK
-    lane = lax.broadcasted_iota(jnp.int32, (part, 128), 1)
+    recordings, samples = audio.shape
+    part = samples // 20 // PACK
+    pltpu.sync_copy(audio, local)
+    x = local[...]
+    blank = jnp.zeros((recordings, 128 - 20 * PACK), F32)
+    for r in range(part):
+        starts = [20 * (part * q + r) for q in range(PACK)]
+        packed[:, r, :] = jnp.concatenate([x[:, at : at + 20] for at in starts] + [blank], 1)
     for k, out in enumerate(outs):
-        total = None
-        for q in range(PACK):
-            block = grouped[b ^ k, q * part : (q + 1) * part, :]
-            block = jnp.concatenate([block, jnp.zeros((part, 108), F32)], 1)
-            block = pltpu.roll(block, 20 * q, 1) if q else block
-            total = block if total is None else total + block
-        out[...] = total
-
-
-def pack(grouped):
-    recordings, piece_rows, _ = grouped.shape
+        out[...] = packed[b ^ k]
+
+
+def pack(audio):
+    recordings, samples = audio.shape
+    part = samples // 20 // PACK
     return pl.pallas_call(
         pack_kernel,
-        out_shape=[sds((piece_rows // PACK, 128), F32)] * recordings,
-        in_specs=[VM],
+        out_shape=[sds((part, 128), F32)] * recordings,
+        in_specs=[pl.BlockSpec(memory_space=pltpu.HBM)],
         out_specs=[VM] * recordings,
+        scratch_shapes=[
+            pltpu.VMEM(audio.shape, F32),
+            pltpu.VMEM((recordings, part, 128), F32),
+        ],
         compiler_params=params(),
         cost_estimate=cost(1 << 16, 1 << 17),
         name="pack",
-    )(grouped)
+    )(audio)
 
 
 def audio_kernel(
-    special, lengths, p0, p1, p2, p3, w0_ref, gain_ref, shift_ref, a0_ref, head_ref, keep, samples, pre0, ahead
+    special, p0, p1, p2, p3, w0_ref, rows_ref, meta_ref, a0_ref, head_ref, keep, samples, pre0, ahead
 ):
     here = Place(special)
     part = p0.shape[0]
     piece_rows = PACK * part
     groups = 4 * piece_rows
-    channels = gain_ref.shape[1]
-    length = lengths[here.b]
+    channels = rows_ref.shape[1]
+    length = meta_ref[0:1, 0:128]
     base = here.t * groups
     for k, piece in enumerate((p0, p1, p2, p3)):
         for q in range(PACK):
@@ -208,8 +213,8 @@
     keep[0:8, :] = s[0:8]
     keep[8 : 8 + TAIL, :] = s[groups - TAIL :]
     pre0[...] = dot(taps(s, pltpu.roll(s, groups - 1, 0)), w0_ref[...])
-    gain0 = gain_ref[0:1, :]
-    shift0 = shift_ref[0:1, :]
+    gain0 = rows_ref[13:14, :]
+    shift0 = rows_ref[16:17, :]
 
     def step(i, carry):
         at = pl.ds(pl.multiple_of(i * CH0, CH0), CH0)
@@ -225,9 +230,9 @@
     move_up(ahead, a0_ref, 4 * channels, groups)
 
 
-def audio_layer(lengths, pieces, w0, gain, shift, special):
+def audio_layer(pieces, w0, table, meta, special):
     groups = 4 * PACK * pieces[0].shape[0]
-    channels = gain.shape[1]
+    channels = table.shape[1]
     return pl.pallas_call(
         functools.partial(audio_kernel, special),
         out_shape=[
@@ -235,7 +240,7 @@
             sds((8, channels), F32),
             sds((8 + TAIL, 128), F32),
         ],
-        in_specs=[SM] + [VM] * 7,
+        in_specs=[VM] * 7,
         out_specs=[VM] * 3,
         scratch_shapes=[
             pltpu.VMEM((groups, 128), F32),
@@ -245,14 +250,13 @@
         compiler_params=params(16),
         cost_estimate=cost(int(3e9), 5 << 20),
         name="audio_layer",
-    )(lengths, *pieces, w0, gain, shift)
+    )(*pieces, w0, table, meta)
 
 
 def forward_kernel(
     special,
     groups,
     scale,
-    lengths,
     a0_in,
     head_in,
     kept,
@@ -261,9 +265,8 @@
     w0_ref,
     k1_ref,
     k2_ref,
-    bias_ref,
-    gain_ref,
-    shift_ref,
+    rows_ref,
+    meta_ref,
     cot_ref,
     a0_ref,
     frames_ref,
@@ -283,7 +286,7 @@
     here = Place(special)
     rows = groups + TAIL
     channels = k1_ref.shape[1]
-    length = lengths[here.b]
+    length = meta_ref[0:1, 0:128]
     base = here.t * groups
     total = groups * lax.axis_size("tm")
     is_last = base + groups >= total
@@ -302,8 +305,8 @@
     pre0[...] = dot(taps(block, after), w0_ref[...])
     tail_row = lax.broadcasted_iota(jnp.int32, (TAIL, channels), 0)
     drop = (tail_row == 0) & is_last
-    gain0 = gain_ref[0:1, :]
-    shift0 = shift_ref[0:1, :]
+    gain0 = rows_ref[13:14, :]
+    shift0 = rows_ref[16:17, :]
     a0_ref[0:groups, :] = a0_in[...]
     for g in range(4):
         cols = pl.ds(g * channels, channels)
@@ -324,9 +327,9 @@
 
     for h in range(2):
         pre1[h] = dot(a0_ref[:, 2 * h * channels : (2 * h + 3) * channels], k1_ref[...])
-    bias1 = bias_ref[1:2, :]
-    gain1 = gain_ref[1:2, :]
-    shift1 = shift_ref[1:2, :]
+    bias1 = rows_ref[11:12, :]
+    gain1 = rows_ref[14:15, :]
+    shift1 = rows_ref[17:18, :]
 
     def step1(i, carry):
         at = pl.ds(pl.multiple_of(i * CH1, CH1), CH1)
@@ -352,10 +355,10 @@
     move_up(ahead, a1_ref, 2 * channels, rows)
 
     pre2[...] = dot(a1_ref[...], k2_ref[...])
-    bias2 = bias_ref[2:3, :]
-    gain2 = gain_ref[2:3, :]
-    shift2 = shift_ref[2:3, :]
-    limit = length // 20
+    bias2 = rows_ref[12:13, :]
+    gain2 = rows_ref[15:16, :]
+    shift2 = rows_ref[18:19, :]
+    limit = meta_ref[1:2, :]
 
     def layer_two(at, place, cot):
         x = pre2[at, :] + bias2
@@ -390,7 +393,7 @@
 
 
 def forward(
-    lengths, a0, head, kept, edges, w0, kernel1, kernel2, bias, gain, shift, cot, scale, chunks, special
+    a0, head, kept, edges, w0, kernel1, kernel2, table, meta, cot, scale, chunks, special
 ):
     groups = cot.shape[0]
     channels = cot.shape[1]
@@ -409,7 +412,7 @@
             sds((2, rows, 128), F32),
             sds((rows, channels), BF16),
         ],
-        in_specs=[SM] + [VM] * 12,
+        in_specs=[VM] * 11,
         out_specs=[VM] * 8,
         scratch_shapes=[
             pltpu.VMEM((2 * TAIL, 4 * channels), F32),
@@ -422,7 +425,7 @@
         compiler_params=params(26),
         cost_estimate=cost(int(8e9), 10 << 20),
         name="forward",
-    )(lengths, a0, head, kept, *edges, w0, kernel1, kernel2, bias, gain, shift, cot)
+    )(a0, head, kept, *edges, w0, kernel1, kernel2, table, meta, cot)
 
 
 def window_kernel(d2_ref, k2_ref, hat_ref, slope_ref, rstd_ref, d1, dwin, behind):
@@ -471,7 +474,7 @@
     )(d2, kernel2, hat, slope, rstd)
 
 
-def backward_kernel(special, d1, a0_ref, order_ref, keep_ref, send_ref):
+def backward_kernel(special, d1, a0_ref, keep_ref, send_ref):
     here = Place(special)
     channels = d1.shape[2]
     put_gradient(
@@ -483,17 +486,17 @@
     )
 
 
-def backward(d1, a0, order, taps_all, chunks, special):
+def backward(d1, a0, taps_all, chunks, special):
     grad = (2, chunks, taps_all // chunks, BC)
     return pl.pallas_call(
         functools.partial(backward_kernel, special),
         out_shape=[sds(grad, F32), sds(grad, BF16)],
-        in_specs=[VM] * 2 + [pl.BlockSpec(memory_space=pl.ANY)],
+        in_specs=[VM] * 2,
         out_specs=[VM] * 2,
         compiler_params=params(16),
         cost_estimate=cost(int(4e9), 10 << 20),
         name="backward",
-    )(d1, a0, order)
+    )(d1, a0)
 
 
 def plane_kernel(keep_ref, recv_ref, *outs):
@@ -505,62 +508,44 @@
             out[zz] = (keep_ref[at] + recv_ref[at].astype(F32)).astype(out.dtype)
 
 
-def plane(keep, recv, order):
+def plane(keep, recv, flops=1 << 20):
     shape = (2,) + keep.shape[2:]
     return pl.pallas_call(
-        lambda keep_ref, recv_ref, order_ref, *outs: plane_kernel(keep_ref, recv_ref, *outs),
+        plane_kernel,
         out_shape=[sds(shape, F32)] + [sds(shape, BF16)] * 3,
-        in_specs=[VM] * 2 + [pl.BlockSpec(memory_space=pl.ANY)],
+        in_specs=[VM] * 2,
         out_specs=[VM] * 4,
         compiler_params=params(),
-        cost_estimate=cost(1 << 20, 5 << 20),
+        cost_estimate=cost(flops, 5 << 20),
         name="plane",
-    )(keep, recv, order)
-
-
-def collect_kernel(own, rx, ry, rd, out):
-    out[...] = own[...] + rx[...].astype(F32) + ry[...].astype(F32) + rd[...].astype(F32)
-
-
-def collect(own, rx, ry, rd):
-    return pl.pallas_call(
-        collect_kernel,
-        out_shape=sds(own.shape, F32),
-        in_specs=[VM] * 4,
-        out_specs=VM,
-        compiler_params=params(),
-        cost_estimate=cost(int(1e10), 8 << 20),
-        name="collect",
-    )(own, rx, ry, rd)
-
-
-def column_kernel(own, rx, ry, rd, second, *outs):
+    )(keep, recv)
+
+
+def column_kernel(*refs):
+    layers, outs = (refs[0:4], refs[4:8]), refs[8:]
     z = Place(True).z
     for dz, out in enumerate(outs):
         zz = z ^ dz
         at = lax.rem(zz, 2)
-
-        @pl.when(zz < 2)
-        def _():
-            total = own[at] + rx[at].astype(F32) + ry[at].astype(F32) + rd[at].astype(F32)
-            out[...] = total.astype(out.dtype)
-
-        @pl.when(zz >= 2)
-        def _():
-            out[...] = second[at].astype(out.dtype)
+        for layer, (own, rx, ry, rd) in enumerate(layers):
+
+            @pl.when(lax.div(zz, 2) == layer)
+            def _():
+                total = own[at] + rx[at].astype(F32) + ry[at].astype(F32) + rd[at].astype(F32)
+                out[...] = total.astype(out.dtype)
 
 
 def column(first, second):
-    shape = second.shape[1:]
+    shape = first[0].shape[1:]
     return pl.pallas_call(
         column_kernel,
         out_shape=[sds(shape, F32)] + [sds(shape, BF16)] * 3,
-        in_specs=[VM] * 5,
+        in_specs=[VM] * 8,
         out_specs=[VM] * 4,
         compiler_params=params(),
         cost_estimate=cost(1 << 20, 3 << 20),
         name="column",
-    )(*first, second)
+    )(*first, *second)
 
 
 def final_kernel(own, a, b, c, out):
@@ -580,32 +565,45 @@
     )(own, a, b, c)
 
 
-def stats_kernel(own, other, pair, lprev, rprev, left, right):
+def stats_kernel(flips, count, *refs):
+    pieces, (lprev, rprev), (left, right, lbuf, rbuf, sems) = refs[:count], refs[count : count + 2], refs[-5:]
     here = Place(True)
-    core, x = here.core, here.x
-    for piece, v in (
-        (own, 2 * core + x),
-        (other, 2 * core + 1 - x),
-        (pair.at[0], 2 * (1 - core) + x),
-        (pair.at[1], 2 * (1 - core) + 1 - x),
-    ):
+    copies = []
+    for i, (piece, (dcore, dx)) in enumerate(zip(pieces, flips)):
+        v = 2 * (here.core ^ dcore) + (here.x ^ dx)
         for u in range(2):
+            slot = 2 * i + u
+            q = 4 * u + v
             block = piece[u * BR : (u + 1) * BR, :]
-            q = 4 * u + v
-            left[q] = BETA * lprev[q] + (1.0 - BETA) * dot_nt(block, block)
-            right[q] = BETA * rprev[q] + (1.0 - BETA) * dot_tn(block, block)
-
-
-def stats(own, other, pair, lprev, rprev):
-    return pl.pallas_call(
-        stats_kernel,
+            lbuf[slot] = BETA * lprev[q] + (1.0 - BETA) * dot_nt(block, block)
+            rbuf[slot] = BETA * rprev[q] + (1.0 - BETA) * dot_tn(block, block)
+            for buf, out, which in ((lbuf, left, 0), (rbuf, right, 1)):
+                copy = pltpu.make_async_copy(buf.at[slot], out.at[q], sems.at[which, slot])
+                copy.start()
+                copies.append(copy)
+    for copy in copies:
+        copy.wait()
+
+
+def stats(pieces, flips, lprev, rprev, begun=()):
+    count = len(pieces)
+    slots = 2 * count
+    hbm = pl.BlockSpec(memory_space=pl.ANY)
+    return pl.pallas_call(
+        functools.partial(stats_kernel, flips, count),
         out_shape=[sds(lprev.shape, F32), sds(rprev.shape, F32)],
-        in_specs=[VM] * 5,
-        out_specs=[VM] * 2,
+        in_specs=[VM] * (count + 2) + [hbm] * len(begun),
+        out_specs=[hbm] * 2,
+        input_output_aliases={count + 2 + i: i for i in range(len(begun))},
+        scratch_shapes=[
+            pltpu.VMEM((slots,) + lprev.shape[1:], F32),
+            pltpu.VMEM((slots,) + rprev.shape[1:], F32),
+            pltpu.SemaphoreType.DMA((2, slots)),
+        ],
         compiler_params=params(),
-        cost_estimate=cost(int(2e8), 4 << 20),
+        cost_estimate=cost(slots * int(2e7), slots << 18),
         name="stats",
-    )(own, other, pair, lprev, rprev)
+    )(*pieces, lprev, rprev, *begun)
 
 
 def permute(value, route):
@@ -642,7 +640,7 @@
                     pairs.append((tt * batches + bb, to[0] * batches + to[1]))
         return pairs
 
-    pieces = list(pack(audio.reshape(recordings, piece_rows, 20)))
+    pieces = list(pack(audio))
     for k in range(1, batches):
         pieces[k] = permute(pieces[k], route(lambda tt, bb: (tt, bb ^ k)))
 
@@ -653,11 +651,18 @@
         return chosen[None]
 
     cot = cotangent[0]
+    last_row = cot[groups - 1 :].astype(F32)
+    lengths_row = jnp.pad(lengths.astype(F32), (0, cot.shape[1] - recordings))[None]
+    table, at = 0.0, 0
+    for part in (kernel0, conv_bias, norm_gain, norm_shift, last_row, lengths_row):
+        table += jnp.pad(part, ((at, 24 - at - part.shape[0]), (0, 0)))
+        at += part.shape[0]
+    w0, meta = prep(table)
     first_group = jnp.pad(of_place(0, 0, 0), ((0, 0), (0, 108 + cot.shape[1])))
     last_group = jnp.concatenate(
         [
             jnp.pad(of_place(batches - 1, -1, 20 * (PACK - 1)), ((0, 0), (0, 108))),
-            cot[groups - 1 :].astype(F32),
+            table[19:20],
         ],
         1,
     )
@@ -667,12 +672,10 @@
         jnp.where(odd, last_group, first_group), route(lambda tt, bb: (tt + 2 * (tt % 2) - 1, bb))
     )
 
-    w0 = prep(kernel0, conv_bias)
     special = tms == 8 and batches == 4
     chunks = 4
-    a0, head, kept = audio_layer(lengths, pieces, w0, norm_gain, norm_shift, special)
+    a0, head, kept = audio_layer(pieces, w0, table, meta, special)
     a0, frames, keep2, send2, hat, slope, rstd, d2 = forward(
-        lengths,
         a0,
         head,
         kept,
@@ -680,9 +683,8 @@
         w0,
         kernel1,
         kernel2,
-        conv_bias,
-        norm_gain,
-        norm_shift,
+        table,
+        meta,
         cot,
         scale,
         chunks,
@@ -690,11 +692,11 @@
     )
     d1 = window(d2, kernel2, hat, slope, rstd)
 
-    def gradient_one(order):
-        return backward(d1, a0, order, kernel1.shape[0], chunks, special)
+    def gradient_one():
+        return backward(d1, a0, kernel1.shape[0], chunks, special)
 
     if not special:
-        keep1, send1 = gradient_one(keep2)
+        keep1, send1 = gradient_one()
 
         def blocks_of(keep, send):
             both = jnp.stack([keep, send.astype(F32)])
@@ -721,16 +723,17 @@
     def to_plane(tox, toy, tod):
         return permute(tox, by_x), permute(toy, by_y), permute(tod, by_xy)
 
-    own2, *out = plane(keep2, permute(send2, by_core), keep2)
-    second = collect(own2, *to_plane(*out))
-    keep1, send1 = gradient_one(own2)
-    own1, *out = plane(keep1, permute(send1, by_core), second)
+    own2, *out = plane(keep2, permute(send2, by_core), int(1e10))
+    second = (own2, *to_plane(*out))
+    keep1, send1 = gradient_one()
+    own1, *out = plane(keep1, permute(send1, by_core))
     own, *out = column((own1, *to_plane(*out)), second)
     arrived = [permute(value, way) for value, way in zip(out, by_z)]
     owned = final(own, *arrived)
     other = permute(owned, by_x)
-    pair = permute(jnp.stack([owned, other]), by_core)
-    left, right = stats(owned, other, pair, left_prev, right_prev)
+    far = permute(owned, by_core), permute(other, by_core)
+    begun = stats((owned, other), ((0, 0), (0, 1)), left_prev, right_prev)
+    left, right = stats(far, ((1, 0), (1, 1)), left_prev, right_prev, begun)
     return frames[None], left, right
 
 

time: 70.7 us -> 66.7 us (0.943)
  Pallas kernels: 19.3 us -> 14.8 us
  starting transfers between devices: 21.1 us -> 22.5 us
  local copies, waits for them, and re-layouts: 2.49 us -> 1.48 us
  other arithmetic: 0.8 us -> 1.57 us
    pallas_call x1, Pallas kernels: 4.87 us -> 2.23 us  [audio_layer(): pl.pallas_call(functools.partial(audio_kernel, special), out_shape=[sds((...]
    pallas_call x1, Pallas kernels: 8.16 us -> 5.89 us  [forward(): pl.pallas_call(functools.partial(forward_kernel, special, groups, scale),...]
    ppermute x18 -> x19, starting transfers between devices: 21.1 us -> 22.5 us  [permute(): return lax.ppermute(value, AXES, route)]
    reshape x1 -> x0, local copies, waits for them, and re-layouts: 0.99 us -> none  [body(): pieces = list(pack(audio.reshape(recordings, piece_rows, 20)))]
    add x0 -> x1, other arithmetic: none -> 0.83 us  [body(): table += jnp.pad(part, ((at, 24 - at - part.shape[0]), (0, 0)))]
    unnamed x22 -> x12, local copies, waits for them, and re-layouts: 1.5 us -> 0.77 us
    pallas_call x6, Pallas kernels: 2.54 us -> 3.25 us  [the longest x2 2.55 us: stats(): pl.pallas_call(functools.partial(stats_kernel, flips, count), out_shape=[...]
    ppermute x18 -> x19, waiting for transfers between devices: 25.8 us -> 25.1 us  [permute(): return lax.ppermute(value, AXES, route)]
  transfers between devices with their start and end apart: 18 -> 19, of which waited for: 10 -> 9; matrix products, arithmetic and copies ran while one was open for 1% -> 3% of each run, Pallas kernels for 12% -> 6%
where the time goes in v4:
time: 66.7 us; the launch traced here: 66.3 us
  waiting for transfers between devices  25.1 us (38%)
  starting transfers between devices  22.5 us (34%)
  Pallas kernels  14.8 us (22%)
  other arithmetic  1.57 us (2%)
  local copies, waits for them, and re-layouts  1.48 us (2%)
  between operations  0.87 us (1%)
    ppermute x19, waiting for transfers between devices, permute(): return lax.ppermute(value, AXES, route)  25.1 us
    ppermute x19, starting transfers between devices, permute(): return lax.ppermute(value, AXES, route)  22.5 us
    pallas_call x1, Pallas kernels, forward(): pl.pallas_call(functools.partial(forward_kernel, special, groups, scale),...  5.89 us
    pallas_call x2, Pallas kernels, stats(): pl.pallas_call(functools.partial(stats_kernel, flips, count), out_shape=[...  2.55 us
    pallas_call x1, Pallas kernels, audio_layer(): pl.pallas_call(functools.partial(audio_kernel, special), out_shape=[sds((...  2.23 us
    pallas_call x1, Pallas kernels, backward(): pl.pallas_call(functools.partial(backward_kernel, special), out_shape=[sd...  1.84 us
    pallas_call x1, Pallas kernels, window(): pl.pallas_call(window_kernel, out_shape=sds((2, groups, channels), BF16),...  1.38 us
  transfers between devices with their start and end apart: 19, of which 9 were waited for; matrix products, arithmetic and copies ran while one was open for 3% of the time, Pallas kernels for 6%

profile of v4, /device:TPU:0, one launch (start us, length us, event | category | flops | bytes accessed | tf_op | source)
XLA Modules:
  0.0 66.3 jit_solution(13947874867664804407)
XLA Ops:
  0.6 0.7 %copy-done.3 = f32[4,1920]{1,0:T(4,128)S(1)} copy-done((f32[4,1920]{1,0:T(4,128)S(1)}, f32[4,1920]{1,0:T(4,128)}, u32[]{:S(2)}) %copy-start.3) | copy-done | bytes 30744
  2.1 2.6 %collective-permute-start.1 = (f32[16,128]{1,0:T(8,128)S(1)}, f32[16,128]{1,0:T(8,128)S(1)}, u32[]{:S(2)}, u32[]{:S(2)}) collective-permute-start(f32[16,128]{1,0:T(8,128)S(1)} %get-tuple-element.40), channel_id=1, source_target_pairs={{0,2},{1,3},{2,0},{3,1},{4,6},{5,7},{6,4},{7,5},{8,10},{9,11},{10,... | collective-permute-start | bytes 24584 | tf_op jit(solution)/shard_map/ppermute | solution.py:610
  4.7 0.7 convert_element_type.34
  5.4 0.7 %slice_bitcast_fusion = bf16[1,512]{1,0:T(2,128)(2,1)S(1)} fusion(bf16[1,384,512]{2,1,0:T(8,128)(2,1)} %param.19), kind=kLoop, calls=%fused_computation.5 | loop fusion | bytes 2048 | tf_op jit(solution)/shard_map/convert_element_type | solution.py:654
  6.1 0.8 %pad_add_fusion.table_ref.rows_ref = f32[24,512]{1,0:T(8,128)S(1)} fusion(f32[1,512]{1,0:T(1,128)S(1)} %bitcast.6, f32[3,512]{1,0:T(4,128)} %param.18, f32[3,512]{1,0:T(4,128)} %param.17, f32[3,512]{1,0:T(4,128)} %param.16, f32[10,512]{1,0:T(8,128)} %param.13, bf16[1,512]{1,0:T(2,128)(2,1)S(1)} %slice_bitcast_fusion), kind=kLoop, calls=%fused_computation | loop fusion | flops 73728 | bytes 91136 | tf_op jit(solution)/shard_map/add | solution.py:658
  7.2 0.6 collective-permute-done.2.p3
  7.8 0.7 collective-permute-start.4
  8.5 4.4 %collective-permute-start.3 = (f32[1,640]{1,0:T(1,128)S(1)}, f32[1,640]{1,0:T(1,128)S(1)}, u32[]{:S(2)}, u32[]{:S(2)}) collective-permute-start(f32[1,640]{1,0:T(1,128)S(1)} %get-tuple-element.76), channel_id=1, source_target_pairs={{0,4},{1,5},{2,6},{3,7},{4,0},{5,1},{6,2},{7,3},{8,12},{9,13},{10,... | collective-permute-start | bytes 7688 | tf_op jit(solution)/shard_map/ppermute | solution.py:610
  12.9 2.2 %audio_layer.1 = (bf16[384,2560]{1,0:T(8,128)(2,1)S(1)}, f32[8,512]{1,0:T(8,128)S(1)}, f32[24,128]{1,0:T(8,128)S(1)}) custom-call(f32[16,128]{1,0:T(8,128)S(1)} %get-tuple-element.38.p0, f32[16,128]{1,0:T(8,128)S(1)} %collective-permute-done.p1, f32[16,128]{1,0:T(8,128)S(1)} %collective-permute-done.1.p2, f32[16,128]{1,0:T(8,128)S(1)} %collective-permute-done.2.p3, ...), custom_call_target="tpu_custom_call" | custom-call | flops 3000000000 | bytes 5242880 | tf_op jit(solution)/shard_map/audio_layer/pallas_call | solution.py:236
  15.1 5.9 %forward.1 = (bf16[400,2560]{1,0:T(8,128)(2,1)S(1)}, bf16[384,512]{1,0:T(8,128)(2,1)}, f32[2,4,384,128]{3,2,1,0:T(8,128)S(1)}, bf16[2,4,384,128]{3,2,1,0:T(8,128...) custom-call(bf16[384,2560]{1,0:T(8,128)(2,1)S(1)} %get-tuple-element, ...), custom_call_target="tpu_custom_call" | custom-call | flops 8000000000 | bytes 10485760 | tf_op jit(solution)/shard_map/forward/pallas_call | solution.py:403
  21.0 1.4 %window.1.d1 = bf16[2,384,512]{2,1,0:T(8,128)(2,1)S(1)} custom-call(bf16[400,512]{1,0:T(8,128)(2,1)S(1)} %get-tuple-element.48.d2_ref, bf16[1536,512]{1,0:T(8,128)(2,1)S(1)} %copy-done.2, f32[2,400,512]{2,1,0:T(8,128)S(1)} %get-tuple-element.49.hat_ref, f32[2,400,512]{2,1,0:T(8,128)S(1)} %get-tuple-element.50.slope_ref, ...), custom_call_target="tpu_custom_call" | custom-call | flops 1500000000 | bytes 3145728 | tf_op jit(solution)/shard_map/window/pallas_call | solution.py:462
  22.4 1.8 %backward.1 = (f32[2,4,384,128]{3,2,1,0:T(8,128)S(1)}, bf16[2,4,384,128]{3,2,1,0:T(8,128)(2,1)S(1)}) custom-call(bf16[2,384,512]{2,1,0:T(8,128)(2,1)S(1)} %window.1.d1, bf16[400,2560]{1,0:T(8,128)(2,1)S(1)} %get-tuple-element.52.a0_ref), custom_call_target="tpu_custom_call" | custom-call | flops 4000000000 | bytes 10485760 | tf_op jit(solution)/shard_map/backward/pallas_call | solution.py:491
  24.8 1.8 %collective-permute-done.5.recv_ref = bf16[2,4,384,128]{3,2,1,0:T(8,128)(2,1)S(1)} collective-permute-done((bf16[2,4,384,128]{3,2,1,0:T(8,128)(2,1)S(1)}, bf16[2,4,384,128]{3,2,1,0:T(8,128)(2,1)S(1)}, u32[]{:S(2)}, u32[]{:S(2)}) %collective-permute-start.5) | collective-permute-done | bytes 786464 | tf_op jit(solution)/shard_map/ppermute | solution.py:610
  26.7 1.3 %collective-permute-start.6 = (bf16[2,384,128]{2,1,0:T(8,128)(2,1)S(1)}, bf16[2,384,128]{2,1,0:T(8,128)(2,1)S(1)}, u32[]{:S(2)}, u32[]{:S(2)}) collective-permute-start(bf16[2,384,128]{2,1,0:T(8,128)(2,1)S(1)} %get-tuple-element.56), channel_id=1, source_target_pairs={{0,2},{1,3},{2,0},{3,1},{4,6},{5,7},{6,4},{7,5},{8,10},{9,11},{10,... | collective-permute-start | bytes 589832 | tf_op jit(solution)/shard_map/ppermute | solution.py:610
  28.0 1.3 %collective-permute-start.7 = (bf16[2,384,128]{2,1,0:T(8,128)(2,1)S(1)}, bf16[2,384,128]{2,1,0:T(8,128)(2,1)S(1)}, u32[]{:S(2)}, u32[]{:S(2)}) collective-permute-start(bf16[2,384,128]{2,1,0:T(8,128)(2,1)S(1)} %get-tuple-element.57), channel_id=1, source_target_pairs={{0,4},{1,5},{2,6},{3,7},{4,0},{5,1},{6,2},{7,3},{8,12},{9,13},{10,... | collective-permute-start | bytes 589832 | tf_op jit(solution)/shard_map/ppermute | solution.py:610
  29.3 1.0 %collective-permute-start.8 = (bf16[2,384,128]{2,1,0:T(8,128)(2,1)S(1)}, bf16[2,384,128]{2,1,0:T(8,128)(2,1)S(1)}, u32[]{:S(2)}, u32[]{:S(2)}) collective-permute-start(bf16[2,384,128]{2,1,0:T(8,128)(2,1)S(1)} %get-tuple-element.58), channel_id=1, source_target_pairs={{0,6},{1,7},{2,4},{3,5},{4,2},{5,3},{6,0},{7,1},{8,14},{9,15},{10,... | collective-permute-start | bytes 589832 | tf_op jit(solution)/shard_map/ppermute | solution.py:610
  30.5 1.3 %collective-permute-start.10 = (bf16[2,384,128]{2,1,0:T(8,128)(2,1)S(1)}, bf16[2,384,128]{2,1,0:T(8,128)(2,1)S(1)}, u32[]{:S(2)}, u32[]{:S(2)}) collective-permute-start(bf16[2,384,128]{2,1,0:T(8,128)(2,1)S(1)} %get-tuple-element.62), channel_id=1, source_target_pairs={{0,2},{1,3},{2,0},{3,1},{4,6},{5,7},{6,4},{7,5},{8,10},{9,11},{10,... | collective-permute-start | bytes 589832 | tf_op jit(solution)/shard_map/ppermute | solution.py:610
  31.8 1.3 %collective-permute-start.11 = (bf16[2,384,128]{2,1,0:T(8,128)(2,1)S(1)}, bf16[2,384,128]{2,1,0:T(8,128)(2,1)S(1)}, u32[]{:S(2)}, u32[]{:S(2)}) collective-permute-start(bf16[2,384,128]{2,1,0:T(8,128)(2,1)S(1)} %get-tuple-element.63), channel_id=1, source_target_pairs={{0,4},{1,5},{2,6},{3,7},{4,0},{5,1},{6,2},{7,3},{8,12},{9,13},{10,... | collective-permute-start | bytes 589832 | tf_op jit(solution)/shard_map/ppermute | solution.py:610
  33.1 1.5 %collective-permute-done.6.refs_1_ = bf16[2,384,128]{2,1,0:T(8,128)(2,1)S(1)} collective-permute-done((bf16[2,384,128]{2,1,0:T(8,128)(2,1)S(1)}, bf16[2,384,128]{2,1,0:T(8,128)(2,1)S(1)}, u32[]{:S(2)}, u32[]{:S(2)}) %collective-permute-start.6) | collective-permute-done | bytes 196640 | tf_op jit(solution)/shard_map/ppermute | solution.py:610
  34.6 1.9 %collective-permute-start.12 = (bf16[2,384,128]{2,1,0:T(8,128)(2,1)S(1)}, bf16[2,384,128]{2,1,0:T(8,128)(2,1)S(1)}, u32[]{:S(2)}, u32[]{:S(2)}) collective-permute-start(bf16[2,384,128]{2,1,0:T(8,128)(2,1)S(1)} %get-tuple-element.64), channel_id=1, source_target_pairs={{0,6},{1,7},{2,4},{3,5},{4,2},{5,3},{6,0},{7,1},{8,14},{9,15},{10,... | collective-permute-start | bytes 589832 | tf_op jit(solution)/shard_map/ppermute | solution.py:610
  36.5 3.5 %collective-permute-done.7.refs_2_ = bf16[2,384,128]{2,1,0:T(8,128)(2,1)S(1)} collective-permute-done((bf16[2,384,128]{2,1,0:T(8,128)(2,1)S(1)}, bf16[2,384,128]{2,1,0:T(8,128)(2,1)S(1)}, u32[]{:S(2)}, u32[]{:S(2)}) %collective-permute-start.7) | collective-permute-done | bytes 196640 | tf_op jit(solution)/shard_map/ppermute | solution.py:610
  40.0 3.0 %collective-permute-done.10.refs_5_ = bf16[2,384,128]{2,1,0:T(8,128)(2,1)S(1)} collective-permute-done((bf16[2,384,128]{2,1,0:T(8,128)(2,1)S(1)}, bf16[2,384,128]{2,1,0:T(8,128)(2,1)S(1)}, u32[]{:S(2)}, u32[]{:S(2)}) %collective-permute-start.10) | collective-permute-done | bytes 196640 | tf_op jit(solution)/shard_map/ppermute | solution.py:610
  43.0 4.3 %collective-permute-done.11.refs_6_ = bf16[2,384,128]{2,1,0:T(8,128)(2,1)S(1)} collective-permute-done((bf16[2,384,128]{2,1,0:T(8,128)(2,1)S(1)}, bf16[2,384,128]{2,1,0:T(8,128)(2,1)S(1)}, u32[]{:S(2)}, u32[]{:S(2)}) %collective-permute-start.11) | collective-permute-done | bytes 196640 | tf_op jit(solution)/shard_map/ppermute | solution.py:610
  47.5 1.6 %collective-permute-start.13 = (bf16[384,128]{1,0:T(8,128)(2,1)S(1)}, bf16[384,128]{1,0:T(8,128)(2,1)S(1)}, u32[]{:S(2)}, u32[]{:S(2)}) collective-permute-start(bf16[384,128]{1,0:T(8,128)(2,1)S(1)} %get-tuple-element.66), channel_id=1, source_target_pairs={{0,8},{1,9},{2,10},{3,11},{4,12},{5,13},{6,14},{7,15},{8,0},{9,1},... | collective-permute-start | bytes 294920 | tf_op jit(solution)/shard_map/ppermute | solution.py:610
  49.2 2.3 %collective-permute-start.14 = (bf16[384,128]{1,0:T(8,128)(2,1)S(1)}, bf16[384,128]{1,0:T(8,128)(2,1)S(1)}, u32[]{:S(2)}, u32[]{:S(2)}) collective-permute-start(bf16[384,128]{1,0:T(8,128)(2,1)S(1)} %get-tuple-element.67), channel_id=1, source_target_pairs={{0,16},{1,17},{2,18},{3,19},{4,20},{5,21},{6,22},{7,23},{8,24},{9,... | collective-permute-start | bytes 294920 | tf_op jit(solution)/shard_map/ppermute | solution.py:610
  51.4 0.6 collective-permute-start.15
  52.0 1.2 %collective-permute-done.13.a = bf16[384,128]{1,0:T(8,128)(2,1)S(1)} collective-permute-done((bf16[384,128]{1,0:T(8,128)(2,1)S(1)}, bf16[384,128]{1,0:T(8,128)(2,1)S(1)}, u32[]{:S(2)}, u32[]{:S(2)}) %collective-permute-start.13) | collective-permute-done | bytes 98336 | tf_op jit(solution)/shard_map/ppermute | solution.py:610
  53.2 5.8 %collective-permute-done.14.b = bf16[384,128]{1,0:T(8,128)(2,1)S(1)} collective-permute-done((bf16[384,128]{1,0:T(8,128)(2,1)S(1)}, bf16[384,128]{1,0:T(8,128)(2,1)S(1)}, u32[]{:S(2)}, u32[]{:S(2)}) %collective-permute-start.14) | collective-permute-done | bytes 98336 | tf_op jit(solution)/shard_map/ppermute | solution.py:610
  59.0 1.2 %collective-permute-start.17 = (bf16[384,128]{1,0:T(8,128)(2,1)S(1)}, bf16[384,128]{1,0:T(8,128)(2,1)S(1)}, u32[]{:S(2)}, u32[]{:S(2)}) collective-permute-start(bf16[384,128]{1,0:T(8,128)(2,1)S(1)} %final.1.refs_0_), channel_id=1, source_target_pairs={{0,2},{1,3},{2,0},{3,1},{4,6},{5,7},{6,4},{7,5},{8,10},{9,11},{10,... | collective-permute-start | bytes 294920 | tf_op jit(solution)/shard_map/ppermute | solution.py:610
  60.3 3.5 %collective-permute-done.17.refs_1_ = bf16[384,128]{1,0:T(8,128)(2,1)S(1)} collective-permute-done((bf16[384,128]{1,0:T(8,128)(2,1)S(1)}, bf16[384,128]{1,0:T(8,128)(2,1)S(1)}, u32[]{:S(2)}, u32[]{:S(2)}) %collective-permute-start.17) | collective-permute-done | bytes 98336 | tf_op jit(solution)/shard_map/ppermute | solution.py:610
  63.7 1.3 %stats.2 = (f32[8,192,192]{2,1,0:T(8,128)}, f32[8,128,128]{2,1,0:T(8,128)}) custom-call(bf16[384,128]{1,0:T(8,128)(2,1)S(1)} %final.1.refs_0_, bf16[384,128]{1,0:T(8,128)(2,1)S(1)} %collective-permute-done.17.refs_1_, f32[8,192,192]{2,1,0:T(8,128)S(1)} %copy-done, f32[8,128,128]{2,1,0:T(8,128)S(1)} %copy-done.1), custom_call_target="tpu_custom_call" | custom-call | flops 80000000 | bytes 1048576 | tf_op jit(solution)/shard_map/stats/pallas_call | solution.py:592
  65.0 1.3 %stats.3 = (f32[8,192,192]{2,1,0:T(8,128)}, f32[8,128,128]{2,1,0:T(8,128)}) custom-call(bf16[384,128]{1,0:T(8,128)(2,1)S(1)} %collective-permute-done.16.refs_0_, bf16[384,128]{1,0:T(8,128)(2,1)S(1)} %collective-permute-done.18.refs_1_, f32[8,192,192]{2,1,0:T(8,128)S(1)} %copy-done, ...), custom_call_target="tpu_custom_call", output_to_operand_aliasing={{0}: (4, {}), {1}: (5, {})} | custom-call | flops 80000000 | bytes 1048576 | tf_op jit(solution)/shard_map/stats/pallas_call | solution.py:592
  (37 shorter events, 2.3 us)
Async XLA Ops:
  0.6 0.8 %copy-start.3 = (f32[4,1920]{1,0:T(4,128)S(1)}, f32[4,1920]{1,0:T(4,128)}, u32[]{:S(2)}) copy-start(f32[4,1920]{1,0:T(4,128)} %audio.1) | copy-start | bytes 92164
  1.6 5.6 %collective-permute-start = (f32[16,128]{1,0:T(8,128)S(1)}, f32[16,128]{1,0:T(8,128)S(1)}, u32[]{:S(2)}, u32[]{:S(2)}) collective-permute-start(f32[16,128]{1,0:T(8,128)S(1)} %get-tuple-element.39), channel_id=1, source_target_pairs={{0,1},{1,0},{2,3},{3,2},{4,5},{5,4},{6,7},{7,6},{8,9},{9,8},{10,11... | collective-permute-start | bytes 24584 | tf_op jit(solution)/shard_map/ppermute | solution.py:610
  2.1 5.1 %collective-permute-start.1 = (f32[16,128]{1,0:T(8,128)S(1)}, f32[16,128]{1,0:T(8,128)S(1)}, u32[]{:S(2)}, u32[]{:S(2)}) collective-permute-start(f32[16,128]{1,0:T(8,128)S(1)} %get-tuple-element.40), channel_id=1, source_target_pairs={{0,2},{1,3},{2,0},{3,1},{4,6},{5,7},{6,4},{7,5},{8,10},{9,11},{10,... | collective-permute-start | bytes 24584 | tf_op jit(solution)/shard_map/ppermute | solution.py:610
  4.7 3.1 %collective-permute-start.2 = (f32[16,128]{1,0:T(8,128)S(1)}, f32[16,128]{1,0:T(8,128)S(1)}, u32[]{:S(2)}, u32[]{:S(2)}) collective-permute-start(f32[16,128]{1,0:T(8,128)S(1)} %get-tuple-element.41), channel_id=1, source_target_pairs={{0,3},{1,2},{2,1},{3,0},{4,7},{5,6},{6,5},{7,4},{8,11},{9,10},{10,... | collective-permute-start | bytes 24584 | tf_op jit(solution)/shard_map/ppermute | solution.py:610
  7.8 7.3 %collective-permute-start.4 = (f32[1,640]{1,0:T(1,128)S(1)}, f32[1,640]{1,0:T(1,128)S(1)}, u32[]{:S(2)}, u32[]{:S(2)}) collective-permute-start(f32[1,640]{1,0:T(1,128)S(1)} %get-tuple-element.75), channel_id=1, source_target_pairs={{4,8},{5,9},{6,10},{7,11},{8,4},{9,5},{10,6},{11,7},{12,16},{13,17... | collective-permute-start | bytes 7688 | tf_op jit(solution)/shard_map/ppermute | solution.py:610
  8.5 6.6 %collective-permute-start.3 = (f32[1,640]{1,0:T(1,128)S(1)}, f32[1,640]{1,0:T(1,128)S(1)}, u32[]{:S(2)}, u32[]{:S(2)}) collective-permute-start(f32[1,640]{1,0:T(1,128)S(1)} %get-tuple-element.76), channel_id=1, source_target_pairs={{0,4},{1,5},{2,6},{3,7},{4,0},{5,1},{6,2},{7,3},{8,12},{9,13},{10,... | collective-permute-start | bytes 7688 | tf_op jit(solution)/shard_map/ppermute | solution.py:610
  12.8 2.3 %copy-start.2 = (bf16[1536,512]{1,0:T(8,128)(2,1)S(1)}, bf16[1536,512]{1,0:T(8,128)(2,1)}, u32[]{:S(2)}) copy-start(bf16[1536,512]{1,0:T(8,128)(2,1)} %k2_ref.3) | copy-start | bytes 4718596
  12.8 2.3 %copy-start.4 = (bf16[1,384,512]{2,1,0:T(8,128)(2,1)S(1)}, bf16[1,384,512]{2,1,0:T(8,128)(2,1)}, u32[]{:S(2)}) copy-start(bf16[1,384,512]{2,1,0:T(8,128)(2,1)} %param.19) | copy-start | bytes 1179652
  12.9 2.3 %copy-start.5 = (bf16[1536,512]{1,0:T(8,128)(2,1)S(1)}, bf16[1536,512]{1,0:T(8,128)(2,1)}, u32[]{:S(2)}) copy-start(bf16[1536,512]{1,0:T(8,128)(2,1)} %k1_ref.1) | copy-start | bytes 4718596
  24.3 2.4 %collective-permute-start.5 = (bf16[2,4,384,128]{3,2,1,0:T(8,128)(2,1)S(1)}, bf16[2,4,384,128]{3,2,1,0:T(8,128)(2,1)S(1)}, u32[]{:S(2)}, u32[]{:S(2)}) collective-permute-start(bf16[2,4,384,128]{3,2,1,0:T(8,128)(2,1)S(1)} %get-tuple-element.54), channel_id=1, source_target_pairs={{0,1},{1,0},{2,3},{3,2},{4,5},{5,4},{6,7},{7,6},{8,9},{9,8},{10,11... | collective-permute-start | bytes 2359304 | tf_op jit(solution)/shard_map/ppermute | solution.py:610
  24.3 6.0 %collective-permute-start.9 = (bf16[2,4,384,128]{3,2,1,0:T(8,128)(2,1)S(1)}, bf16[2,4,384,128]{3,2,1,0:T(8,128)(2,1)S(1)}, u32[]{:S(2)}, u32[]{:S(2)}) collective-permute-start(bf16[2,4,384,128]{3,2,1,0:T(8,128)(2,1)S(1)} %get-tuple-element.60), channel_id=1, source_target_pairs={{0,1},{1,0},{2,3},{3,2},{4,5},{5,4},{6,7},{7,6},{8,9},{9,8},{10,11... | collective-permute-start | bytes 2359304 | tf_op jit(solution)/shard_map/ppermute | solution.py:610
  26.7 7.8 %collective-permute-start.6 = (bf16[2,384,128]{2,1,0:T(8,128)(2,1)S(1)}, bf16[2,384,128]{2,1,0:T(8,128)(2,1)S(1)}, u32[]{:S(2)}, u32[]{:S(2)}) collective-permute-start(bf16[2,384,128]{2,1,0:T(8,128)(2,1)S(1)} %get-tuple-element.56), channel_id=1, source_target_pairs={{0,2},{1,3},{2,0},{3,1},{4,6},{5,7},{6,4},{7,5},{8,10},{9,11},{10,... | collective-permute-start | bytes 589832 | tf_op jit(solution)/shard_map/ppermute | solution.py:610
  28.0 12.0 %collective-permute-start.7 = (bf16[2,384,128]{2,1,0:T(8,128)(2,1)S(1)}, bf16[2,384,128]{2,1,0:T(8,128)(2,1)S(1)}, u32[]{:S(2)}, u32[]{:S(2)}) collective-permute-start(bf16[2,384,128]{2,1,0:T(8,128)(2,1)S(1)} %get-tuple-element.57), channel_id=1, source_target_pairs={{0,4},{1,5},{2,6},{3,7},{4,0},{5,1},{6,2},{7,3},{8,12},{9,13},{10,... | collective-permute-start | bytes 589832 | tf_op jit(solution)/shard_map/ppermute | solution.py:610
  29.3 10.7 %collective-permute-start.8 = (bf16[2,384,128]{2,1,0:T(8,128)(2,1)S(1)}, bf16[2,384,128]{2,1,0:T(8,128)(2,1)S(1)}, u32[]{:S(2)}, u32[]{:S(2)}) collective-permute-start(bf16[2,384,128]{2,1,0:T(8,128)(2,1)S(1)} %get-tuple-element.58), channel_id=1, source_target_pairs={{0,6},{1,7},{2,4},{3,5},{4,2},{5,3},{6,0},{7,1},{8,14},{9,15},{10,... | collective-permute-start | bytes 589832 | tf_op jit(solution)/shard_map/ppermute | solution.py:610
  30.5 33.2 %copy-start = (f32[8,192,192]{2,1,0:T(8,128)S(1)}, f32[8,192,192]{2,1,0:T(8,128)}, u32[]{:S(2)}) copy-start(f32[8,192,192]{2,1,0:T(8,128)} %refs_2_.3) | copy-start | bytes 3538948
  30.5 33.2 %copy-start.1 = (f32[8,128,128]{2,1,0:T(8,128)S(1)}, f32[8,128,128]{2,1,0:T(8,128)}, u32[]{:S(2)}) copy-start(f32[8,128,128]{2,1,0:T(8,128)} %refs_3_.3) | copy-start | bytes 1572868
  30.5 12.5 %collective-permute-start.10 = (bf16[2,384,128]{2,1,0:T(8,128)(2,1)S(1)}, bf16[2,384,128]{2,1,0:T(8,128)(2,1)S(1)}, u32[]{:S(2)}, u32[]{:S(2)}) collective-permute-start(bf16[2,384,128]{2,1,0:T(8,128)(2,1)S(1)} %get-tuple-element.62), channel_id=1, source_target_pairs={{0,2},{1,3},{2,0},{3,1},{4,6},{5,7},{6,4},{7,5},{8,10},{9,11},{10,... | collective-permute-start | bytes 589832 | tf_op jit(solution)/shard_map/ppermute | solution.py:610
  31.8 15.5 %collective-permute-start.11 = (bf16[2,384,128]{2,1,0:T(8,128)(2,1)S(1)}, bf16[2,384,128]{2,1,0:T(8,128)(2,1)S(1)}, u32[]{:S(2)}, u32[]{:S(2)}) collective-permute-start(bf16[2,384,128]{2,1,0:T(8,128)(2,1)S(1)} %get-tuple-element.63), channel_id=1, source_target_pairs={{0,4},{1,5},{2,6},{3,7},{4,0},{5,1},{6,2},{7,3},{8,12},{9,13},{10,... | collective-permute-start | bytes 589832 | tf_op jit(solution)/shard_map/ppermute | solution.py:610
  34.6 12.8 %collective-permute-start.12 = (bf16[2,384,128]{2,1,0:T(8,128)(2,1)S(1)}, bf16[2,384,128]{2,1,0:T(8,128)(2,1)S(1)}, u32[]{:S(2)}, u32[]{:S(2)}) collective-permute-start(bf16[2,384,128]{2,1,0:T(8,128)(2,1)S(1)} %get-tuple-element.64), channel_id=1, source_target_pairs={{0,6},{1,7},{2,4},{3,5},{4,2},{5,3},{6,0},{7,1},{8,14},{9,15},{10,... | collective-permute-start | bytes 589832 | tf_op jit(solution)/shard_map/ppermute | solution.py:610
  47.5 5.7 %collective-permute-start.13 = (bf16[384,128]{1,0:T(8,128)(2,1)S(1)}, bf16[384,128]{1,0:T(8,128)(2,1)S(1)}, u32[]{:S(2)}, u32[]{:S(2)}) collective-permute-start(bf16[384,128]{1,0:T(8,128)(2,1)S(1)} %get-tuple-element.66), channel_id=1, source_target_pairs={{0,8},{1,9},{2,10},{3,11},{4,12},{5,13},{6,14},{7,15},{8,0},{9,1},... | collective-permute-start | bytes 294920 | tf_op jit(solution)/shard_map/ppermute | solution.py:610
  49.2 9.8 %collective-permute-start.14 = (bf16[384,128]{1,0:T(8,128)(2,1)S(1)}, bf16[384,128]{1,0:T(8,128)(2,1)S(1)}, u32[]{:S(2)}, u32[]{:S(2)}) collective-permute-start(bf16[384,128]{1,0:T(8,128)(2,1)S(1)} %get-tuple-element.67), channel_id=1, source_target_pairs={{0,16},{1,17},{2,18},{3,19},{4,20},{5,21},{6,22},{7,23},{8,24},{9,... | collective-permute-start | bytes 294920 | tf_op jit(solution)/shard_map/ppermute | solution.py:610
  51.4 7.6 %collective-permute-start.15 = (bf16[384,128]{1,0:T(8,128)(2,1)S(1)}, bf16[384,128]{1,0:T(8,128)(2,1)S(1)}, u32[]{:S(2)}, u32[]{:S(2)}) collective-permute-start(bf16[384,128]{1,0:T(8,128)(2,1)S(1)} %get-tuple-element.68), channel_id=1, source_target_pairs={{0,24},{1,25},{2,26},{3,27},{4,28},{5,29},{6,30},{7,31},{8,16},{9,... | collective-permute-start | bytes 294920 | tf_op jit(solution)/shard_map/ppermute | solution.py:610
  59.0 4.7 %collective-permute-start.17 = (bf16[384,128]{1,0:T(8,128)(2,1)S(1)}, bf16[384,128]{1,0:T(8,128)(2,1)S(1)}, u32[]{:S(2)}, u32[]{:S(2)}) collective-permute-start(bf16[384,128]{1,0:T(8,128)(2,1)S(1)} %final.1.refs_0_), channel_id=1, source_target_pairs={{0,2},{1,3},{2,0},{3,1},{4,6},{5,7},{6,4},{7,5},{8,10},{9,11},{10,... | collective-permute-start | bytes 294920 | tf_op jit(solution)/shard_map/ppermute | solution.py:610
  60.3 4.8 %collective-permute-start.16 = (bf16[384,128]{1,0:T(8,128)(2,1)S(1)}, bf16[384,128]{1,0:T(8,128)(2,1)S(1)}, u32[]{:S(2)}, u32[]{:S(2)}) collective-permute-start(bf16[384,128]{1,0:T(8,128)(2,1)S(1)} %final.1.refs_0_), channel_id=1, source_target_pairs={{0,1},{1,0},{2,3},{3,2},{4,5},{5,4},{6,7},{7,6},{8,9},{9,8},{10,11... | collective-permute-start | bytes 294920 | tf_op jit(solution)/shard_map/ppermute | solution.py:610
  63.7 1.3 %collective-permute-start.18 = (bf16[384,128]{1,0:T(8,128)(2,1)S(1)}, bf16[384,128]{1,0:T(8,128)(2,1)S(1)}, u32[]{:S(2)}, u32[]{:S(2)}) collective-permute-start(bf16[384,128]{1,0:T(8,128)(2,1)S(1)} %collective-permute-done.17.refs_1_), channel_id=1, source_target_pairs={{0,1},{1,0},{2,3},{3,2},{4,5},{5,4},{6,7},{7,6},{8,9},{9,8},{10,11... | collective-permute-start | bytes 294920 | tf_op jit(solution)/shard_map/ppermute | solution.py:610

commit v5 on v4

--- a/solution.py
+++ b/solution.py
@@ -103,12 +103,12 @@
     return lax.dot_general(a, b, (((1,), (1,)), ((), ())), preferred_element_type=F32)
 
 
-def put_gradient(core, keep_ref, send_ref, pairs, chunk):
-    half = keep_ref.shape[-1] * 2
-    width = keep_ref.shape[-1]
-    for which, out in ((core, keep_ref), (1 - core, send_ref)):
+def put_gradient(halves, pairs):
+    for which, out in halves:
+        width, chunk = out.shape[-1], out.shape[2]
+        half = 2 * width
         start = pl.multiple_of(which * half, half)
-        for row in range(keep_ref.shape[1]):
+        for row in range(out.shape[1]):
             total = None
             for a_ref, offset, d_ref in pairs:
                 groups = d_ref.shape[0]
@@ -389,7 +389,7 @@
     cot_tail = jnp.where(tail_row == TAIL - 1, preceding[:, 128:], 0.0)
     place = base + jnp.where(tail_row == TAIL - 1, -1, groups + tail_row)
     _, d2_ref[groups:rows, :] = layer_two(pl.ds(groups, TAIL), place, cot_tail)
-    put_gradient(here.core, keep_ref, send_ref, [(a1_ref, 0, d2own)], keep_ref.shape[2])
+    put_gradient(((here.core, keep_ref), (1 - here.core, send_ref)), [(a1_ref, 0, d2own)])
 
 
 def forward(
@@ -428,7 +428,7 @@
     )(a0, head, kept, *edges, w0, kernel1, kernel2, table, meta, cot)
 
 
-def window_kernel(d2_ref, k2_ref, hat_ref, slope_ref, rstd_ref, d1, dwin, behind):
+def window_kernel(special, d2_ref, k2_ref, hat_ref, slope_ref, rstd_ref, a0_ref, d1, keep_ref, dwin, behind):
     groups, channels = dwin.shape[1:]
     rows = groups + TAIL
     d2 = d2_ref[...]
@@ -454,49 +454,48 @@
         return carry
 
     lax.fori_loop(0, groups // CH3, step, 0, unroll=UN3)
-
-
-def window(d2, kernel2, hat, slope, rstd):
+    put_gradient(((Place(special).core, keep_ref),), both_taps(a0_ref, d1))
+
+
+def both_taps(a0_ref, d1):
+    return [(a0_ref, 0, d1.at[0]), (a0_ref, 2 * d1.shape[2], d1.at[1])]
+
+
+def window(d2, kernel2, hat, slope, rstd, a0, chunks, special):
     rows, channels = d2.shape
     groups = rows - TAIL
     return pl.pallas_call(
-        window_kernel,
-        out_shape=sds((2, groups, channels), BF16),
-        in_specs=[VM] * 5,
-        out_specs=VM,
+        functools.partial(window_kernel, special),
+        out_shape=[
+            sds((2, groups, channels), BF16),
+            sds((2, chunks, kernel2.shape[0] // chunks, BC), F32),
+        ],
+        in_specs=[VM] * 6,
+        out_specs=[VM] * 2,
         scratch_shapes=[
             pltpu.VMEM((2, groups, channels), F32),
             pltpu.VMEM((groups + 8, channels), F32),
         ],
         compiler_params=params(16),
-        cost_estimate=cost(int(1.5e9), 3 << 20),
+        cost_estimate=cost(int(2.5e9), 3 << 20),
         name="window",
-    )(d2, kernel2, hat, slope, rstd)
-
-
-def backward_kernel(special, d1, a0_ref, keep_ref, send_ref):
-    here = Place(special)
-    channels = d1.shape[2]
-    put_gradient(
-        here.core,
-        keep_ref,
-        send_ref,
-        [(a0_ref, 0, d1.at[0]), (a0_ref, 2 * channels, d1.at[1])],
-        keep_ref.shape[2],
-    )
-
-
-def backward(d1, a0, taps_all, chunks, special):
-    grad = (2, chunks, taps_all // chunks, BC)
+    )(d2, kernel2, hat, slope, rstd, a0)
+
+
+def backward_kernel(special, d1, a0_ref, order_ref, send_ref):
+    put_gradient(((1 - Place(special).core, send_ref),), both_taps(a0_ref, d1))
+
+
+def backward(d1, a0, order, shape, special):
     return pl.pallas_call(
         functools.partial(backward_kernel, special),
-        out_shape=[sds(grad, F32), sds(grad, BF16)],
-        in_specs=[VM] * 2,
-        out_specs=[VM] * 2,
+        out_shape=sds(shape, BF16),
+        in_specs=[VM] * 2 + [pl.BlockSpec(memory_space=pl.ANY)],
+        out_specs=VM,
         compiler_params=params(16),
-        cost_estimate=cost(int(4e9), 10 << 20),
+        cost_estimate=cost(int(2e9), 5 << 20),
         name="backward",
-    )(d1, a0)
+    )(d1, a0, order)
 
 
 def plane_kernel(keep_ref, recv_ref, *outs):
@@ -524,7 +523,7 @@
 def column_kernel(*refs):
     layers, outs = (refs[0:4], refs[4:8]), refs[8:]
     z = Place(True).z
-    for dz, out in enumerate(outs):
+    for dz, out in zip((0, 2, 3, 1), outs):
         zz = z ^ dz
         at = lax.rem(zz, 2)
         for layer, (own, rx, ry, rd) in enumerate(layers):
@@ -690,13 +689,10 @@
         chunks,
         special,
     )
-    d1 = window(d2, kernel2, hat, slope, rstd)
-
-    def gradient_one():
-        return backward(d1, a0, kernel1.shape[0], chunks, special)
+    d1, keep1 = window(d2, kernel2, hat, slope, rstd, a0, chunks, special)
 
     if not special:
-        keep1, send1 = gradient_one()
+        send1 = backward(d1, a0, keep2, keep1.shape, special)
 
         def blocks_of(keep, send):
             both = jnp.stack([keep, send.astype(F32)])
@@ -718,14 +714,14 @@
     by_x = route(lambda tt, bb: (tt, bb ^ 2))
     by_y = route(lambda tt, bb: (tt ^ 1, bb))
     by_xy = route(lambda tt, bb: (tt ^ 1, bb ^ 2))
-    by_z = [route(lambda tt, bb: (tt ^ (2 * k), bb)) for k in range(1, 4)]
+    by_z = [route(lambda tt, bb: (tt ^ (2 * k), bb)) for k in (2, 3, 1)]
 
     def to_plane(tox, toy, tod):
         return permute(tox, by_x), permute(toy, by_y), permute(tod, by_xy)
 
     own2, *out = plane(keep2, permute(send2, by_core), int(1e10))
     second = (own2, *to_plane(*out))
-    keep1, send1 = gradient_one()
+    send1 = backward(d1, a0, own2, keep1.shape, special)
     own1, *out = plane(keep1, permute(send1, by_core))
     own, *out = column((own1, *to_plane(*out)), second)
     arrived = [permute(value, way) for value, way in zip(out, by_z)]

time: 66.7 us -> 64 us (0.960)
  waiting for transfers between devices: 25.1 us -> 22.9 us
    ppermute x19, waiting for transfers between devices: 25.1 us -> 22.9 us  [permute(): return lax.ppermute(value, AXES, route)]
  transfers between devices with their start and end apart: 19 -> 19, of which waited for: 9 -> 8; matrix products, arithmetic and copies ran while one was open for 3% -> 3% of each run, Pallas kernels for 6% -> 10%
where the time goes in v5:
time: 64 us; the launch traced here: 63.6 us
  waiting for transfers between devices  22.9 us (36%)
  starting transfers between devices  21.9 us (34%)
  Pallas kernels  14.9 us (23%)
  other arithmetic  1.57 us (2%)
  local copies, waits for them, and re-layouts  1.48 us (2%)
  between operations  0.86 us (1%)
    ppermute x19, waiting for transfers between devices, permute(): return lax.ppermute(value, AXES, route)  22.9 us
    ppermute x19, starting transfers between devices, permute(): return lax.ppermute(value, AXES, route)  21.9 us
    pallas_call x1, Pallas kernels, forward(): pl.pallas_call(functools.partial(forward_kernel, special, groups, scale),...  5.89 us
    pallas_call x2, Pallas kernels, stats(): pl.pallas_call(functools.partial(stats_kernel, flips, count), out_shape=[...  2.56 us
    pallas_call x1, Pallas kernels, window(): pl.pallas_call(functools.partial(window_kernel, special), out_shape=[sds(...  2.26 us
    pallas_call x1, Pallas kernels, audio_layer(): pl.pallas_call(functools.partial(audio_kernel, special), out_shape=[sds((...  2.23 us
  transfers between devices with their start and end apart: 19, of which 8 were waited for; matrix products, arithmetic and copies ran while one was open for 3% of the time, Pallas kernels for 10%

profile of v5, /device:TPU:0, one launch (start us, length us, event | category | flops | bytes accessed | tf_op | source)
XLA Modules:
  0.0 63.6 jit_solution(4733673527147671122)
XLA Ops:
  0.6 0.7 %copy-done.2 = f32[4,1920]{1,0:T(4,128)S(1)} copy-done((f32[4,1920]{1,0:T(4,128)S(1)}, f32[4,1920]{1,0:T(4,128)}, u32[]{:S(2)}) %copy-start.2) | copy-done | bytes 30744
  1.6 0.5 collective-permute-start
  2.1 2.6 %collective-permute-start.1 = (f32[16,128]{1,0:T(8,128)S(1)}, f32[16,128]{1,0:T(8,128)S(1)}, u32[]{:S(2)}, u32[]{:S(2)}) collective-permute-start(f32[16,128]{1,0:T(8,128)S(1)} %get-tuple-element.40), channel_id=1, source_target_pairs={{0,2},{1,3},{2,0},{3,1},{4,6},{5,7},{6,4},{7,5},{8,10},{9,11},{10,... | collective-permute-start | bytes 24584 | tf_op jit(solution)/shard_map/ppermute | solution.py:609
  4.7 0.7 %convert_element_type.34 = f32[4]{0:T(128)S(1)} convert(s32[4]{0:T(128)} %param.12) | non-fusion elementwise | flops 4 | bytes 32 | tf_op jit(solution)/shard_map/convert_element_type | solution.py:654
  5.4 0.7 %slice_bitcast_fusion = bf16[1,512]{1,0:T(2,128)(2,1)S(1)} fusion(bf16[1,384,512]{2,1,0:T(8,128)(2,1)} %param.19), kind=kLoop, calls=%fused_computation.5 | loop fusion | bytes 2048 | tf_op jit(solution)/shard_map/convert_element_type | solution.py:653
  6.1 0.8 %pad_add_fusion.table_ref.rows_ref = f32[24,512]{1,0:T(8,128)S(1)} fusion(f32[1,512]{1,0:T(1,128)S(1)} %bitcast.6, f32[3,512]{1,0:T(4,128)} %param.18, f32[3,512]{1,0:T(4,128)} %param.17, f32[3,512]{1,0:T(4,128)} %param.16, f32[10,512]{1,0:T(8,128)} %param.13, bf16[1,512]{1,0:T(2,128)(2,1)S(1)} %slice_bitcast_fusion), kind=kLoop, calls=%fused_computation | loop fusion | flops 73728 | bytes 91136 | tf_op jit(solution)/shard_map/add | solution.py:657
  7.2 0.6 collective-permute-done.2.p3
  7.8 0.7 %collective-permute-start.4 = (f32[1,640]{1,0:T(1,128)S(1)}, f32[1,640]{1,0:T(1,128)S(1)}, u32[]{:S(2)}, u32[]{:S(2)}) collective-permute-start(f32[1,640]{1,0:T(1,128)S(1)} %get-tuple-element.75), channel_id=1, source_target_pairs={{4,8},{5,9},{6,10},{7,11},{8,4},{9,5},{10,6},{11,7},{12,16},{13,17... | collective-permute-start | bytes 7688 | tf_op jit(solution)/shard_map/ppermute | solution.py:609
  8.5 4.4 %collective-permute-start.3 = (f32[1,640]{1,0:T(1,128)S(1)}, f32[1,640]{1,0:T(1,128)S(1)}, u32[]{:S(2)}, u32[]{:S(2)}) collective-permute-start(f32[1,640]{1,0:T(1,128)S(1)} %get-tuple-element.76), channel_id=1, source_target_pairs={{0,4},{1,5},{2,6},{3,7},{4,0},{5,1},{6,2},{7,3},{8,12},{9,13},{10,... | collective-permute-start | bytes 7688 | tf_op jit(solution)/shard_map/ppermute | solution.py:609
  12.9 2.2 %audio_layer.1 = (bf16[384,2560]{1,0:T(8,128)(2,1)S(1)}, f32[8,512]{1,0:T(8,128)S(1)}, f32[24,128]{1,0:T(8,128)S(1)}) custom-call(f32[16,128]{1,0:T(8,128)S(1)} %get-tuple-element.38.p0, f32[16,128]{1,0:T(8,128)S(1)} %collective-permute-done.p1, f32[16,128]{1,0:T(8,128)S(1)} %collective-permute-done.1.p2, f32[16,128]{1,0:T(8,128)S(1)} %collective-permute-done.2.p3, ...), custom_call_target="tpu_custom_call" | custom-call | flops 3000000000 | bytes 5242880 | tf_op jit(solution)/shard_map/audio_layer/pallas_call | solution.py:236
  15.1 5.9 %forward.1 = (bf16[400,2560]{1,0:T(8,128)(2,1)S(1)}, bf16[384,512]{1,0:T(8,128)(2,1)}, f32[2,4,384,128]{3,2,1,0:T(8,128)S(1)}, bf16[2,4,384,128]{3,2,1,0:T(8,128...) custom-call(bf16[384,2560]{1,0:T(8,128)(2,1)S(1)} %get-tuple-element, ...), custom_call_target="tpu_custom_call" | custom-call | flops 8000000000 | bytes 10485760 | tf_op jit(solution)/shard_map/forward/pallas_call | solution.py:403
  21.0 2.3 %window.1 = (bf16[2,384,512]{2,1,0:T(8,128)(2,1)S(1)}, f32[2,4,384,128]{3,2,1,0:T(8,128)S(1)}) custom-call(bf16[400,512]{1,0:T(8,128)(2,1)S(1)} %get-tuple-element.48.d2_ref, bf16[1536,512]{1,0:T(8,128)(2,1)S(1)} %copy-done.5, f32[2,400,512]{2,1,0:T(8,128)S(1)} %get-tuple-element.49.hat_ref, f32[2,400,512]{2,1,0:T(8,128)S(1)} %get-tuple-element.50.slope_ref, ...), custom_call_target="tpu_custom_call" | custom-call | flops 2500000000 | bytes 3145728 | tf_op jit(solution)/shard_map/window/pallas_call | solution.py:467
  23.5 1.0 %backward.1 = bf16[2,4,384,128]{3,2,1,0:T(8,128)(2,1)S(1)} custom-call(bf16[2,384,512]{2,1,0:T(8,128)(2,1)S(1)} %get-tuple-element.54.d1, bf16[400,2560]{1,0:T(8,128)(2,1)S(1)} %get-tuple-element.52.a0_ref, f32[2,384,128]{2,1,0:T(8,128)S(1)} %get-tuple-element.57.order_ref.refs_4_), custom_call_target="tpu_custom_call" | custom-call | flops 2000000000 | bytes 5242880 | tf_op jit(solution)/shard_map/backward/pallas_call | solution.py:490
  24.6 0.6 collective-permute-start.6
  25.1 1.2 %collective-permute-start.10 = (bf16[2,384,128]{2,1,0:T(8,128)(2,1)S(1)}, bf16[2,384,128]{2,1,0:T(8,128)(2,1)S(1)}, u32[]{:S(2)}, u32[]{:S(2)}) collective-permute-start(bf16[2,384,128]{2,1,0:T(8,128)(2,1)S(1)} %get-tuple-element.62), channel_id=1, source_target_pairs={{0,2},{1,3},{2,0},{3,1},{4,6},{5,7},{6,4},{7,5},{8,10},{9,11},{10,... | collective-permute-start | bytes 589832 | tf_op jit(solution)/shard_map/ppermute | solution.py:609
  26.3 1.3 %collective-permute-start.11 = (bf16[2,384,128]{2,1,0:T(8,128)(2,1)S(1)}, bf16[2,384,128]{2,1,0:T(8,128)(2,1)S(1)}, u32[]{:S(2)}, u32[]{:S(2)}) collective-permute-start(bf16[2,384,128]{2,1,0:T(8,128)(2,1)S(1)} %get-tuple-element.63), channel_id=1, source_target_pairs={{0,4},{1,5},{2,6},{3,7},{4,0},{5,1},{6,2},{7,3},{8,12},{9,13},{10,... | collective-permute-start | bytes 589832 | tf_op jit(solution)/shard_map/ppermute | solution.py:609
  27.6 1.0 %collective-permute-start.12 = (bf16[2,384,128]{2,1,0:T(8,128)(2,1)S(1)}, bf16[2,384,128]{2,1,0:T(8,128)(2,1)S(1)}, u32[]{:S(2)}, u32[]{:S(2)}) collective-permute-start(bf16[2,384,128]{2,1,0:T(8,128)(2,1)S(1)} %get-tuple-element.64), channel_id=1, source_target_pairs={{0,6},{1,7},{2,4},{3,5},{4,2},{5,3},{6,0},{7,1},{8,14},{9,15},{10,... | collective-permute-start | bytes 589832 | tf_op jit(solution)/shard_map/ppermute | solution.py:609
  28.8 1.3 %collective-permute-start.7 = (bf16[2,384,128]{2,1,0:T(8,128)(2,1)S(1)}, bf16[2,384,128]{2,1,0:T(8,128)(2,1)S(1)}, u32[]{:S(2)}, u32[]{:S(2)}) collective-permute-start(bf16[2,384,128]{2,1,0:T(8,128)(2,1)S(1)} %get-tuple-element.59), channel_id=1, source_target_pairs={{0,2},{1,3},{2,0},{3,1},{4,6},{5,7},{6,4},{7,5},{8,10},{9,11},{10,... | collective-permute-start | bytes 589832 | tf_op jit(solution)/shard_map/ppermute | solution.py:609
  30.0 1.3 %collective-permute-start.8 = (bf16[2,384,128]{2,1,0:T(8,128)(2,1)S(1)}, bf16[2,384,128]{2,1,0:T(8,128)(2,1)S(1)}, u32[]{:S(2)}, u32[]{:S(2)}) collective-permute-start(bf16[2,384,128]{2,1,0:T(8,128)(2,1)S(1)} %get-tuple-element.60), channel_id=1, source_target_pairs={{0,4},{1,5},{2,6},{3,7},{4,0},{5,1},{6,2},{7,3},{8,12},{9,13},{10,... | collective-permute-start | bytes 589832 | tf_op jit(solution)/shard_map/ppermute | solution.py:609
  31.3 1.5 %collective-permute-done.10.refs_5_ = bf16[2,384,128]{2,1,0:T(8,128)(2,1)S(1)} collective-permute-done((bf16[2,384,128]{2,1,0:T(8,128)(2,1)S(1)}, bf16[2,384,128]{2,1,0:T(8,128)(2,1)S(1)}, u32[]{:S(2)}, u32[]{:S(2)}) %collective-permute-start.10) | collective-permute-done | bytes 196640 | tf_op jit(solution)/shard_map/ppermute | solution.py:609
  32.9 1.9 %collective-permute-start.9 = (bf16[2,384,128]{2,1,0:T(8,128)(2,1)S(1)}, bf16[2,384,128]{2,1,0:T(8,128)(2,1)S(1)}, u32[]{:S(2)}, u32[]{:S(2)}) collective-permute-start(bf16[2,384,128]{2,1,0:T(8,128)(2,1)S(1)} %get-tuple-element.61), channel_id=1, source_target_pairs={{0,6},{1,7},{2,4},{3,5},{4,2},{5,3},{6,0},{7,1},{8,14},{9,15},{10,... | collective-permute-start | bytes 589832 | tf_op jit(solution)/shard_map/ppermute | solution.py:609
  34.8 3.5 %collective-permute-done.11.refs_6_ = bf16[2,384,128]{2,1,0:T(8,128)(2,1)S(1)} collective-permute-done((bf16[2,384,128]{2,1,0:T(8,128)(2,1)S(1)}, bf16[2,384,128]{2,1,0:T(8,128)(2,1)S(1)}, u32[]{:S(2)}, u32[]{:S(2)}) %collective-permute-start.11) | collective-permute-done | bytes 196640 | tf_op jit(solution)/shard_map/ppermute | solution.py:609
  38.3 3.0 %collective-permute-done.7.refs_1_ = bf16[2,384,128]{2,1,0:T(8,128)(2,1)S(1)} collective-permute-done((bf16[2,384,128]{2,1,0:T(8,128)(2,1)S(1)}, bf16[2,384,128]{2,1,0:T(8,128)(2,1)S(1)}, u32[]{:S(2)}, u32[]{:S(2)}) %collective-permute-start.7) | collective-permute-done | bytes 196640 | tf_op jit(solution)/shard_map/ppermute | solution.py:609
  41.4 4.2 %collective-permute-done.8.refs_2_ = bf16[2,384,128]{2,1,0:T(8,128)(2,1)S(1)} collective-permute-done((bf16[2,384,128]{2,1,0:T(8,128)(2,1)S(1)}, bf16[2,384,128]{2,1,0:T(8,128)(2,1)S(1)}, u32[]{:S(2)}, u32[]{:S(2)}) %collective-permute-start.8) | collective-permute-done | bytes 196640 | tf_op jit(solution)/shard_map/ppermute | solution.py:609
  45.8 2.6 %collective-permute-start.13 = (bf16[384,128]{1,0:T(8,128)(2,1)S(1)}, bf16[384,128]{1,0:T(8,128)(2,1)S(1)}, u32[]{:S(2)}, u32[]{:S(2)}) collective-permute-start(bf16[384,128]{1,0:T(8,128)(2,1)S(1)} %get-tuple-element.66), channel_id=1, source_target_pairs={{0,16},{1,17},{2,18},{3,19},{4,20},{5,21},{6,22},{7,23},{8,24},{9,... | collective-permute-start | bytes 294920 | tf_op jit(solution)/shard_map/ppermute | solution.py:609
  48.4 1.4 %collective-permute-start.14 = (bf16[384,128]{1,0:T(8,128)(2,1)S(1)}, bf16[384,128]{1,0:T(8,128)(2,1)S(1)}, u32[]{:S(2)}, u32[]{:S(2)}) collective-permute-start(bf16[384,128]{1,0:T(8,128)(2,1)S(1)} %get-tuple-element.67), channel_id=1, source_target_pairs={{0,24},{1,25},{2,26},{3,27},{4,28},{5,29},{6,30},{7,31},{8,16},{9,... | collective-permute-start | bytes 294920 | tf_op jit(solution)/shard_map/ppermute | solution.py:609
  49.8 6.1 %collective-permute-done.13.a = bf16[384,128]{1,0:T(8,128)(2,1)S(1)} collective-permute-done((bf16[384,128]{1,0:T(8,128)(2,1)S(1)}, bf16[384,128]{1,0:T(8,128)(2,1)S(1)}, u32[]{:S(2)}, u32[]{:S(2)}) %collective-permute-start.13) | collective-permute-done | bytes 98336 | tf_op jit(solution)/shard_map/ppermute | solution.py:609
  55.9 0.4 collective-permute-done.15.c
  56.4 1.2 %collective-permute-start.17 = (bf16[384,128]{1,0:T(8,128)(2,1)S(1)}, bf16[384,128]{1,0:T(8,128)(2,1)S(1)}, u32[]{:S(2)}, u32[]{:S(2)}) collective-permute-start(bf16[384,128]{1,0:T(8,128)(2,1)S(1)} %final.1.refs_0_), channel_id=1, source_target_pairs={{0,2},{1,3},{2,0},{3,1},{4,6},{5,7},{6,4},{7,5},{8,10},{9,11},{10,... | collective-permute-start | bytes 294920 | tf_op jit(solution)/shard_map/ppermute | solution.py:609
  57.5 3.5 %collective-permute-done.17.refs_1_ = bf16[384,128]{1,0:T(8,128)(2,1)S(1)} collective-permute-done((bf16[384,128]{1,0:T(8,128)(2,1)S(1)}, bf16[384,128]{1,0:T(8,128)(2,1)S(1)}, u32[]{:S(2)}, u32[]{:S(2)}) %collective-permute-start.17) | collective-permute-done | bytes 98336 | tf_op jit(solution)/shard_map/ppermute | solution.py:609
  61.1 1.3 %stats.2 = (f32[8,192,192]{2,1,0:T(8,128)}, f32[8,128,128]{2,1,0:T(8,128)}) custom-call(bf16[384,128]{1,0:T(8,128)(2,1)S(1)} %final.1.refs_0_, bf16[384,128]{1,0:T(8,128)(2,1)S(1)} %collective-permute-done.17.refs_1_, f32[8,192,192]{2,1,0:T(8,128)S(1)} %copy-done, f32[8,128,128]{2,1,0:T(8,128)S(1)} %copy-done.1), custom_call_target="tpu_custom_call" | custom-call | flops 80000000 | bytes 1048576 | tf_op jit(solution)/shard_map/stats/pallas_call | solution.py:591
  62.4 1.3 %stats.3 = (f32[8,192,192]{2,1,0:T(8,128)}, f32[8,128,128]{2,1,0:T(8,128)}) custom-call(bf16[384,128]{1,0:T(8,128)(2,1)S(1)} %collective-permute-done.16.refs_0_, bf16[384,128]{1,0:T(8,128)(2,1)S(1)} %collective-permute-done.18.refs_1_, f32[8,192,192]{2,1,0:T(8,128)S(1)} %copy-done, ...), custom_call_target="tpu_custom_call", output_to_operand_aliasing={{0}: (4, {}), {1}: (5, {})} | custom-call | flops 80000000 | bytes 1048576 | tf_op jit(solution)/shard_map/stats/pallas_call | solution.py:591
  (37 shorter events, 1.2 us)
Async XLA Ops:
  0.6 0.8 %copy-start.2 = (f32[4,1920]{1,0:T(4,128)S(1)}, f32[4,1920]{1,0:T(4,128)}, u32[]{:S(2)}) copy-start(f32[4,1920]{1,0:T(4,128)} %audio.1) | copy-start | bytes 92164
  1.6 5.6 %collective-permute-start = (f32[16,128]{1,0:T(8,128)S(1)}, f32[16,128]{1,0:T(8,128)S(1)}, u32[]{:S(2)}, u32[]{:S(2)}) collective-permute-start(f32[16,128]{1,0:T(8,128)S(1)} %get-tuple-element.39), channel_id=1, source_target_pairs={{0,1},{1,0},{2,3},{3,2},{4,5},{5,4},{6,7},{7,6},{8,9},{9,8},{10,11... | collective-permute-start | bytes 24584 | tf_op jit(solution)/shard_map/ppermute | solution.py:609
  2.1 5.1 %collective-permute-start.1 = (f32[16,128]{1,0:T(8,128)S(1)}, f32[16,128]{1,0:T(8,128)S(1)}, u32[]{:S(2)}, u32[]{:S(2)}) collective-permute-start(f32[16,128]{1,0:T(8,128)S(1)} %get-tuple-element.40), channel_id=1, source_target_pairs={{0,2},{1,3},{2,0},{3,1},{4,6},{5,7},{6,4},{7,5},{8,10},{9,11},{10,... | collective-permute-start | bytes 24584 | tf_op jit(solution)/shard_map/ppermute | solution.py:609
  4.7 3.1 %collective-permute-start.2 = (f32[16,128]{1,0:T(8,128)S(1)}, f32[16,128]{1,0:T(8,128)S(1)}, u32[]{:S(2)}, u32[]{:S(2)}) collective-permute-start(f32[16,128]{1,0:T(8,128)S(1)} %get-tuple-element.41), channel_id=1, source_target_pairs={{0,3},{1,2},{2,1},{3,0},{4,7},{5,6},{6,5},{7,4},{8,11},{9,10},{10,... | collective-permute-start | bytes 24584 | tf_op jit(solution)/shard_map/ppermute | solution.py:609
  7.8 7.3 %collective-permute-start.4 = (f32[1,640]{1,0:T(1,128)S(1)}, f32[1,640]{1,0:T(1,128)S(1)}, u32[]{:S(2)}, u32[]{:S(2)}) collective-permute-start(f32[1,640]{1,0:T(1,128)S(1)} %get-tuple-element.75), channel_id=1, source_target_pairs={{4,8},{5,9},{6,10},{7,11},{8,4},{9,5},{10,6},{11,7},{12,16},{13,17... | collective-permute-start | bytes 7688 | tf_op jit(solution)/shard_map/ppermute | solution.py:609
  8.5 6.6 %collective-permute-start.3 = (f32[1,640]{1,0:T(1,128)S(1)}, f32[1,640]{1,0:T(1,128)S(1)}, u32[]{:S(2)}, u32[]{:S(2)}) collective-permute-start(f32[1,640]{1,0:T(1,128)S(1)} %get-tuple-element.76), channel_id=1, source_target_pairs={{0,4},{1,5},{2,6},{3,7},{4,0},{5,1},{6,2},{7,3},{8,12},{9,13},{10,... | collective-permute-start | bytes 7688 | tf_op jit(solution)/shard_map/ppermute | solution.py:609
  12.8 2.3 %copy-start.3 = (bf16[1,384,512]{2,1,0:T(8,128)(2,1)S(1)}, bf16[1,384,512]{2,1,0:T(8,128)(2,1)}, u32[]{:S(2)}) copy-start(bf16[1,384,512]{2,1,0:T(8,128)(2,1)} %param.19) | copy-start | bytes 1179652
  12.8 2.3 %copy-start.4 = (bf16[1536,512]{1,0:T(8,128)(2,1)S(1)}, bf16[1536,512]{1,0:T(8,128)(2,1)}, u32[]{:S(2)}) copy-start(bf16[1536,512]{1,0:T(8,128)(2,1)} %k1_ref.1) | copy-start | bytes 4718596
  12.9 2.3 %copy-start.5 = (bf16[1536,512]{1,0:T(8,128)(2,1)S(1)}, bf16[1536,512]{1,0:T(8,128)(2,1)}, u32[]{:S(2)}) copy-start(bf16[1536,512]{1,0:T(8,128)(2,1)} %k2_ref.3) | copy-start | bytes 4718596
  21.0 2.3 %collective-permute-start.5 = (bf16[2,4,384,128]{3,2,1,0:T(8,128)(2,1)S(1)}, bf16[2,4,384,128]{3,2,1,0:T(8,128)(2,1)S(1)}, u32[]{:S(2)}, u32[]{:S(2)}) collective-permute-start(bf16[2,4,384,128]{3,2,1,0:T(8,128)(2,1)S(1)} %get-tuple-element.56), channel_id=1, source_target_pairs={{0,1},{1,0},{2,3},{3,2},{4,5},{5,4},{6,7},{7,6},{8,9},{9,8},{10,11... | collective-permute-start | bytes 2359304 | tf_op jit(solution)/shard_map/ppermute | solution.py:609
  24.6 4.1 %collective-permute-start.6 = (bf16[2,4,384,128]{3,2,1,0:T(8,128)(2,1)S(1)}, bf16[2,4,384,128]{3,2,1,0:T(8,128)(2,1)S(1)}, u32[]{:S(2)}, u32[]{:S(2)}) collective-permute-start(bf16[2,4,384,128]{3,2,1,0:T(8,128)(2,1)S(1)} %backward.1), channel_id=1, source_target_pairs={{0,1},{1,0},{2,3},{3,2},{4,5},{5,4},{6,7},{7,6},{8,9},{9,8},{10,11... | collective-permute-start | bytes 2359304 | tf_op jit(solution)/shard_map/ppermute | solution.py:609
  25.1 7.8 %collective-permute-start.10 = (bf16[2,384,128]{2,1,0:T(8,128)(2,1)S(1)}, bf16[2,384,128]{2,1,0:T(8,128)(2,1)S(1)}, u32[]{:S(2)}, u32[]{:S(2)}) collective-permute-start(bf16[2,384,128]{2,1,0:T(8,128)(2,1)S(1)} %get-tuple-element.62), channel_id=1, source_target_pairs={{0,2},{1,3},{2,0},{3,1},{4,6},{5,7},{6,4},{7,5},{8,10},{9,11},{10,... | collective-permute-start | bytes 589832 | tf_op jit(solution)/shard_map/ppermute | solution.py:609
  26.3 12.0 %collective-permute-start.11 = (bf16[2,384,128]{2,1,0:T(8,128)(2,1)S(1)}, bf16[2,384,128]{2,1,0:T(8,128)(2,1)S(1)}, u32[]{:S(2)}, u32[]{:S(2)}) collective-permute-start(bf16[2,384,128]{2,1,0:T(8,128)(2,1)S(1)} %get-tuple-element.63), channel_id=1, source_target_pairs={{0,4},{1,5},{2,6},{3,7},{4,0},{5,1},{6,2},{7,3},{8,12},{9,13},{10,... | collective-permute-start | bytes 589832 | tf_op jit(solution)/shard_map/ppermute | solution.py:609
  27.6 10.7 %collective-permute-start.12 = (bf16[2,384,128]{2,1,0:T(8,128)(2,1)S(1)}, bf16[2,384,128]{2,1,0:T(8,128)(2,1)S(1)}, u32[]{:S(2)}, u32[]{:S(2)}) collective-permute-start(bf16[2,384,128]{2,1,0:T(8,128)(2,1)S(1)} %get-tuple-element.64), channel_id=1, source_target_pairs={{0,6},{1,7},{2,4},{3,5},{4,2},{5,3},{6,0},{7,1},{8,14},{9,15},{10,... | collective-permute-start | bytes 589832 | tf_op jit(solution)/shard_map/ppermute | solution.py:609
  28.8 32.3 %copy-start = (f32[8,192,192]{2,1,0:T(8,128)S(1)}, f32[8,192,192]{2,1,0:T(8,128)}, u32[]{:S(2)}) copy-start(f32[8,192,192]{2,1,0:T(8,128)} %refs_2_.3) | copy-start | bytes 3538948
  28.8 32.3 %copy-start.1 = (f32[8,128,128]{2,1,0:T(8,128)S(1)}, f32[8,128,128]{2,1,0:T(8,128)}, u32[]{:S(2)}) copy-start(f32[8,128,128]{2,1,0:T(8,128)} %refs_3_.3) | copy-start | bytes 1572868
  28.8 12.6 %collective-permute-start.7 = (bf16[2,384,128]{2,1,0:T(8,128)(2,1)S(1)}, bf16[2,384,128]{2,1,0:T(8,128)(2,1)S(1)}, u32[]{:S(2)}, u32[]{:S(2)}) collective-permute-start(bf16[2,384,128]{2,1,0:T(8,128)(2,1)S(1)} %get-tuple-element.59), channel_id=1, source_target_pairs={{0,2},{1,3},{2,0},{3,1},{4,6},{5,7},{6,4},{7,5},{8,10},{9,11},{10,... | collective-permute-start | bytes 589832 | tf_op jit(solution)/shard_map/ppermute | solution.py:609
  30.0 15.5 %collective-permute-start.8 = (bf16[2,384,128]{2,1,0:T(8,128)(2,1)S(1)}, bf16[2,384,128]{2,1,0:T(8,128)(2,1)S(1)}, u32[]{:S(2)}, u32[]{:S(2)}) collective-permute-start(bf16[2,384,128]{2,1,0:T(8,128)(2,1)S(1)} %get-tuple-element.60), channel_id=1, source_target_pairs={{0,4},{1,5},{2,6},{3,7},{4,0},{5,1},{6,2},{7,3},{8,12},{9,13},{10,... | collective-permute-start | bytes 589832 | tf_op jit(solution)/shard_map/ppermute | solution.py:609
  32.9 12.7 %collective-permute-start.9 = (bf16[2,384,128]{2,1,0:T(8,128)(2,1)S(1)}, bf16[2,384,128]{2,1,0:T(8,128)(2,1)S(1)}, u32[]{:S(2)}, u32[]{:S(2)}) collective-permute-start(bf16[2,384,128]{2,1,0:T(8,128)(2,1)S(1)} %get-tuple-element.61), channel_id=1, source_target_pairs={{0,6},{1,7},{2,4},{3,5},{4,2},{5,3},{6,0},{7,1},{8,14},{9,15},{10,... | collective-permute-start | bytes 589832 | tf_op jit(solution)/shard_map/ppermute | solution.py:609
  45.8 10.1 %collective-permute-start.13 = (bf16[384,128]{1,0:T(8,128)(2,1)S(1)}, bf16[384,128]{1,0:T(8,128)(2,1)S(1)}, u32[]{:S(2)}, u32[]{:S(2)}) collective-permute-start(bf16[384,128]{1,0:T(8,128)(2,1)S(1)} %get-tuple-element.66), channel_id=1, source_target_pairs={{0,16},{1,17},{2,18},{3,19},{4,20},{5,21},{6,22},{7,23},{8,24},{9,... | collective-permute-start | bytes 294920 | tf_op jit(solution)/shard_map/ppermute | solution.py:609
  48.4 7.5 %collective-permute-start.14 = (bf16[384,128]{1,0:T(8,128)(2,1)S(1)}, bf16[384,128]{1,0:T(8,128)(2,1)S(1)}, u32[]{:S(2)}, u32[]{:S(2)}) collective-permute-start(bf16[384,128]{1,0:T(8,128)(2,1)S(1)} %get-tuple-element.67), channel_id=1, source_target_pairs={{0,24},{1,25},{2,26},{3,27},{4,28},{5,29},{6,30},{7,31},{8,16},{9,... | collective-permute-start | bytes 294920 | tf_op jit(solution)/shard_map/ppermute | solution.py:609
  49.8 6.5 %collective-permute-start.15 = (bf16[384,128]{1,0:T(8,128)(2,1)S(1)}, bf16[384,128]{1,0:T(8,128)(2,1)S(1)}, u32[]{:S(2)}, u32[]{:S(2)}) collective-permute-start(bf16[384,128]{1,0:T(8,128)(2,1)S(1)} %get-tuple-element.68), channel_id=1, source_target_pairs={{0,8},{1,9},{2,10},{3,11},{4,12},{5,13},{6,14},{7,15},{8,0},{9,1},... | collective-permute-start | bytes 294920 | tf_op jit(solution)/shard_map/ppermute | solution.py:609
  56.4 4.7 %collective-permute-start.17 = (bf16[384,128]{1,0:T(8,128)(2,1)S(1)}, bf16[384,128]{1,0:T(8,128)(2,1)S(1)}, u32[]{:S(2)}, u32[]{:S(2)}) collective-permute-start(bf16[384,128]{1,0:T(8,128)(2,1)S(1)} %final.1.refs_0_), channel_id=1, source_target_pairs={{0,2},{1,3},{2,0},{3,1},{4,6},{5,7},{6,4},{7,5},{8,10},{9,11},{10,... | collective-permute-start | bytes 294920 | tf_op jit(solution)/shard_map/ppermute | solution.py:609
  57.5 4.8 %collective-permute-start.16 = (bf16[384,128]{1,0:T(8,128)(2,1)S(1)}, bf16[384,128]{1,0:T(8,128)(2,1)S(1)}, u32[]{:S(2)}, u32[]{:S(2)}) collective-permute-start(bf16[384,128]{1,0:T(8,128)(2,1)S(1)} %final.1.refs_0_), channel_id=1, source_target_pairs={{0,1},{1,0},{2,3},{3,2},{4,5},{5,4},{6,7},{7,6},{8,9},{9,8},{10,11... | collective-permute-start | bytes 294920 | tf_op jit(solution)/shard_map/ppermute | solution.py:609
  61.0 1.3 %collective-permute-start.18 = (bf16[384,128]{1,0:T(8,128)(2,1)S(1)}, bf16[384,128]{1,0:T(8,128)(2,1)S(1)}, u32[]{:S(2)}, u32[]{:S(2)}) collective-permute-start(bf16[384,128]{1,0:T(8,128)(2,1)S(1)} %collective-permute-done.17.refs_1_), channel_id=1, source_target_pairs={{0,1},{1,0},{2,3},{3,2},{4,5},{5,4},{6,7},{7,6},{8,9},{9,8},{10,11... | collective-permute-start | bytes 294920 | tf_op jit(solution)/shard_map/ppermute | solution.py:609

commit v6 on v5

--- a/solution.py
+++ b/solution.py
@@ -19,7 +19,7 @@
 CH = 16
 PACK = 6
 CH0, CH1, CH2, CH3 = 16,16,16,16
-UN0, UN1, UN2, UN3 = 12, 25, 24, 24
+UN0, UN1, UN2, UN3 = 24, 25, 24, 24
 TAIL = 16
 
 VM = pl.BlockSpec(memory_space=pltpu.VMEM)
@@ -723,7 +723,9 @@
     second = (own2, *to_plane(*out))
     send1 = backward(d1, a0, own2, keep1.shape, special)
     own1, *out = plane(keep1, permute(send1, by_core))
-    own, *out = column((own1, *to_plane(*out)), second)
+    tox, toy, tod = out
+    first = (own1, permute(toy, by_y), permute(tod, by_xy), permute(tox, by_x))
+    own, *out = column(first, second)
     arrived = [permute(value, way) for value, way in zip(out, by_z)]
     owned = final(own, *arrived)
     other = permute(owned, by_x)

time: 64 us -> 63.4 us (level)
  starting transfers between devices: 21.9 us -> 21.2 us
    ppermute x19, starting transfers between devices: 21.9 us -> 21.2 us  [permute(): return lax.ppermute(value, AXES, route)]
  transfers between devices with their start and end apart: 19 -> 19, of which waited for: 8 -> 8; matrix products, arithmetic and copies ran while one was open for 3% -> 3% of each run, Pallas kernels for 10% -> 9%
where the time goes in v6:
time: 63.4 us; the launch traced here: 63.1 us
  waiting for transfers between devices  23.3 us (37%)
  starting transfers between devices  21.2 us (33%)
  Pallas kernels  14.6 us (23%)
  other arithmetic  1.57 us (2%)
  local copies, waits for them, and re-layouts  1.55 us (2%)
  between operations  0.85 us (1%)
    ppermute x19, waiting for transfers between devices, permute(): return lax.ppermute(value, AXES, route)  23.3 us
    ppermute x19, starting transfers between devices, permute(): return lax.ppermute(value, AXES, route)  21.2 us
    pallas_call x1, Pallas kernels, forward(): pl.pallas_call(functools.partial(forward_kernel, special, groups, scale),...  5.88 us
    pallas_call x2, Pallas kernels, stats(): pl.pallas_call(functools.partial(stats_kernel, flips, count), out_shape=[...  2.55 us
    pallas_call x1, Pallas kernels, window(): pl.pallas_call(functools.partial(window_kernel, special), out_shape=[sds(...  2.26 us
    pallas_call x1, Pallas kernels, audio_layer(): pl.pallas_call(functools.partial(audio_kernel, special), out_shape=[sds((...  1.89 us
  transfers between devices with their start and end apart: 19, of which 8 were waited for; matrix products, arithmetic and copies ran while one was open for 3% of the time, Pallas kernels for 9%

profile of v6, /device:TPU:0, one launch (start us, length us, event | category | flops | bytes accessed | tf_op | source)
XLA Modules:
  0.0 63.1 jit_solution(5051070515904938021)
XLA Ops:
  0.6 0.7 %copy-done.2 = f32[4,1920]{1,0:T(4,128)S(1)} copy-done((f32[4,1920]{1,0:T(4,128)S(1)}, f32[4,1920]{1,0:T(4,128)}, u32[]{:S(2)}) %copy-start.2) | copy-done | bytes 30744
  1.6 0.5 collective-permute-start
  2.1 2.6 %collective-permute-start.1 = (f32[16,128]{1,0:T(8,128)S(1)}, f32[16,128]{1,0:T(8,128)S(1)}, u32[]{:S(2)}, u32[]{:S(2)}) collective-permute-start(f32[16,128]{1,0:T(8,128)S(1)} %get-tuple-element.40), channel_id=1, source_target_pairs={{0,2},{1,3},{2,0},{3,1},{4,6},{5,7},{6,4},{7,5},{8,10},{9,11},{10,... | collective-permute-start | bytes 24584 | tf_op jit(solution)/shard_map/ppermute | solution.py:609
  4.7 0.7 %convert_element_type.34 = f32[4]{0:T(128)S(1)} convert(s32[4]{0:T(128)} %param.12) | non-fusion elementwise | flops 4 | bytes 32 | tf_op jit(solution)/shard_map/convert_element_type | solution.py:654
  5.4 0.7 %slice_bitcast_fusion = bf16[1,512]{1,0:T(2,128)(2,1)S(1)} fusion(bf16[1,384,512]{2,1,0:T(8,128)(2,1)} %param.19), kind=kLoop, calls=%fused_computation.5 | loop fusion | bytes 2048 | tf_op jit(solution)/shard_map/convert_element_type | solution.py:653
  6.1 0.8 %pad_add_fusion.table_ref.rows_ref = f32[24,512]{1,0:T(8,128)S(1)} fusion(f32[1,512]{1,0:T(1,128)S(1)} %bitcast.6, f32[3,512]{1,0:T(4,128)} %param.18, f32[3,512]{1,0:T(4,128)} %param.17, f32[3,512]{1,0:T(4,128)} %param.16, f32[10,512]{1,0:T(8,128)} %param.13, bf16[1,512]{1,0:T(2,128)(2,1)S(1)} %slice_bitcast_fusion), kind=kLoop, calls=%fused_computation | loop fusion | flops 73728 | bytes 91136 | tf_op jit(solution)/shard_map/add | solution.py:657
  7.2 0.6 collective-permute-done.2.p3
  7.8 0.7 %collective-permute-start.4 = (f32[1,640]{1,0:T(1,128)S(1)}, f32[1,640]{1,0:T(1,128)S(1)}, u32[]{:S(2)}, u32[]{:S(2)}) collective-permute-start(f32[1,640]{1,0:T(1,128)S(1)} %get-tuple-element.75), channel_id=1, source_target_pairs={{4,8},{5,9},{6,10},{7,11},{8,4},{9,5},{10,6},{11,7},{12,16},{13,17... | collective-permute-start | bytes 7688 | tf_op jit(solution)/shard_map/ppermute | solution.py:609
  8.5 4.4 %collective-permute-start.3 = (f32[1,640]{1,0:T(1,128)S(1)}, f32[1,640]{1,0:T(1,128)S(1)}, u32[]{:S(2)}, u32[]{:S(2)}) collective-permute-start(f32[1,640]{1,0:T(1,128)S(1)} %get-tuple-element.76), channel_id=1, source_target_pairs={{0,4},{1,5},{2,6},{3,7},{4,0},{5,1},{6,2},{7,3},{8,12},{9,13},{10,... | collective-permute-start | bytes 7688 | tf_op jit(solution)/shard_map/ppermute | solution.py:609
  12.9 1.9 %audio_layer.1 = (bf16[384,2560]{1,0:T(8,128)(2,1)S(1)}, f32[8,512]{1,0:T(8,128)S(1)}, f32[24,128]{1,0:T(8,128)S(1)}) custom-call(f32[16,128]{1,0:T(8,128)S(1)} %get-tuple-element.38.p0, f32[16,128]{1,0:T(8,128)S(1)} %collective-permute-done.p1, f32[16,128]{1,0:T(8,128)S(1)} %collective-permute-done.1.p2, f32[16,128]{1,0:T(8,128)S(1)} %collective-permute-done.2.p3, ...), custom_call_target="tpu_custom_call" | custom-call | flops 3000000000 | bytes 5242880 | tf_op jit(solution)/shard_map/audio_layer/pallas_call | solution.py:236
  14.9 5.9 %forward.1 = (bf16[400,2560]{1,0:T(8,128)(2,1)S(1)}, bf16[384,512]{1,0:T(8,128)(2,1)}, f32[2,4,384,128]{3,2,1,0:T(8,128)S(1)}, bf16[2,4,384,128]{3,2,1,0:T(8,128...) custom-call(bf16[384,2560]{1,0:T(8,128)(2,1)S(1)} %get-tuple-element, ...), custom_call_target="tpu_custom_call" | custom-call | flops 8000000000 | bytes 10485760 | tf_op jit(solution)/shard_map/forward/pallas_call | solution.py:403
  20.7 2.3 %window.1 = (bf16[2,384,512]{2,1,0:T(8,128)(2,1)S(1)}, f32[2,4,384,128]{3,2,1,0:T(8,128)S(1)}) custom-call(bf16[400,512]{1,0:T(8,128)(2,1)S(1)} %get-tuple-element.48.d2_ref, bf16[1536,512]{1,0:T(8,128)(2,1)S(1)} %copy-done.5, f32[2,400,512]{2,1,0:T(8,128)S(1)} %get-tuple-element.49.hat_ref, f32[2,400,512]{2,1,0:T(8,128)S(1)} %get-tuple-element.50.slope_ref, ...), custom_call_target="tpu_custom_call" | custom-call | flops 2500000000 | bytes 3145728 | tf_op jit(solution)/shard_map/window/pallas_call | solution.py:467
  23.2 1.0 %backward.1 = bf16[2,4,384,128]{3,2,1,0:T(8,128)(2,1)S(1)} custom-call(bf16[2,384,512]{2,1,0:T(8,128)(2,1)S(1)} %get-tuple-element.54.d1, bf16[400,2560]{1,0:T(8,128)(2,1)S(1)} %get-tuple-element.52.a0_ref, f32[2,384,128]{2,1,0:T(8,128)S(1)} %get-tuple-element.57.order_ref.refs_4_), custom_call_target="tpu_custom_call" | custom-call | flops 2000000000 | bytes 5242880 | tf_op jit(solution)/shard_map/backward/pallas_call | solution.py:490
  24.3 0.6 collective-permute-start.6
  24.8 1.2 %collective-permute-start.10 = (bf16[2,384,128]{2,1,0:T(8,128)(2,1)S(1)}, bf16[2,384,128]{2,1,0:T(8,128)(2,1)S(1)}, u32[]{:S(2)}, u32[]{:S(2)}) collective-permute-start(bf16[2,384,128]{2,1,0:T(8,128)(2,1)S(1)} %get-tuple-element.62), channel_id=1, source_target_pairs={{0,2},{1,3},{2,0},{3,1},{4,6},{5,7},{6,4},{7,5},{8,10},{9,11},{10,... | collective-permute-start | bytes 589832 | tf_op jit(solution)/shard_map/ppermute | solution.py:609
  26.0 1.6 %collective-permute-start.11 = (bf16[2,384,128]{2,1,0:T(8,128)(2,1)S(1)}, bf16[2,384,128]{2,1,0:T(8,128)(2,1)S(1)}, u32[]{:S(2)}, u32[]{:S(2)}) collective-permute-start(bf16[2,384,128]{2,1,0:T(8,128)(2,1)S(1)} %get-tuple-element.63), channel_id=1, source_target_pairs={{0,4},{1,5},{2,6},{3,7},{4,0},{5,1},{6,2},{7,3},{8,12},{9,13},{10,... | collective-permute-start | bytes 589832 | tf_op jit(solution)/shard_map/ppermute | solution.py:609
  27.6 0.7 %collective-permute-start.12 = (bf16[2,384,128]{2,1,0:T(8,128)(2,1)S(1)}, bf16[2,384,128]{2,1,0:T(8,128)(2,1)S(1)}, u32[]{:S(2)}, u32[]{:S(2)}) collective-permute-start(bf16[2,384,128]{2,1,0:T(8,128)(2,1)S(1)} %get-tuple-element.64), channel_id=1, source_target_pairs={{0,6},{1,7},{2,4},{3,5},{4,2},{5,3},{6,0},{7,1},{8,14},{9,15},{10,... | collective-permute-start | bytes 589832 | tf_op jit(solution)/shard_map/ppermute | solution.py:609
  28.5 1.7 %collective-permute-start.7 = (bf16[2,384,128]{2,1,0:T(8,128)(2,1)S(1)}, bf16[2,384,128]{2,1,0:T(8,128)(2,1)S(1)}, u32[]{:S(2)}, u32[]{:S(2)}) collective-permute-start(bf16[2,384,128]{2,1,0:T(8,128)(2,1)S(1)} %get-tuple-element.59), channel_id=1, source_target_pairs={{0,4},{1,5},{2,6},{3,7},{4,0},{5,1},{6,2},{7,3},{8,12},{9,13},{10,... | collective-permute-start | bytes 589832 | tf_op jit(solution)/shard_map/ppermute | solution.py:609
  30.2 1.1 %collective-permute-start.8 = (bf16[2,384,128]{2,1,0:T(8,128)(2,1)S(1)}, bf16[2,384,128]{2,1,0:T(8,128)(2,1)S(1)}, u32[]{:S(2)}, u32[]{:S(2)}) collective-permute-start(bf16[2,384,128]{2,1,0:T(8,128)(2,1)S(1)} %get-tuple-element.60), channel_id=1, source_target_pairs={{0,6},{1,7},{2,4},{3,5},{4,2},{5,3},{6,0},{7,1},{8,14},{9,15},{10,... | collective-permute-start | bytes 589832 | tf_op jit(solution)/shard_map/ppermute | solution.py:609
  31.2 1.4 %collective-permute-done.10.refs_5_ = bf16[2,384,128]{2,1,0:T(8,128)(2,1)S(1)} collective-permute-done((bf16[2,384,128]{2,1,0:T(8,128)(2,1)S(1)}, bf16[2,384,128]{2,1,0:T(8,128)(2,1)S(1)}, u32[]{:S(2)}, u32[]{:S(2)}) %collective-permute-start.10) | collective-permute-done | bytes 196640 | tf_op jit(solution)/shard_map/ppermute | solution.py:609
  32.6 1.2 %collective-permute-start.9 = (bf16[2,384,128]{2,1,0:T(8,128)(2,1)S(1)}, bf16[2,384,128]{2,1,0:T(8,128)(2,1)S(1)}, u32[]{:S(2)}, u32[]{:S(2)}) collective-permute-start(bf16[2,384,128]{2,1,0:T(8,128)(2,1)S(1)} %get-tuple-element.61), channel_id=1, source_target_pairs={{0,2},{1,3},{2,0},{3,1},{4,6},{5,7},{6,4},{7,5},{8,10},{9,11},{10,... | collective-permute-start | bytes 589832 | tf_op jit(solution)/shard_map/ppermute | solution.py:609
  33.8 8.5 %collective-permute-done.11.refs_6_ = bf16[2,384,128]{2,1,0:T(8,128)(2,1)S(1)} collective-permute-done((bf16[2,384,128]{2,1,0:T(8,128)(2,1)S(1)}, bf16[2,384,128]{2,1,0:T(8,128)(2,1)S(1)}, u32[]{:S(2)}, u32[]{:S(2)}) %collective-permute-start.11) | collective-permute-done | bytes 196640 | tf_op jit(solution)/shard_map/ppermute | solution.py:609
  42.3 3.0 %collective-permute-done.7.refs_1_ = bf16[2,384,128]{2,1,0:T(8,128)(2,1)S(1)} collective-permute-done((bf16[2,384,128]{2,1,0:T(8,128)(2,1)S(1)}, bf16[2,384,128]{2,1,0:T(8,128)(2,1)S(1)}, u32[]{:S(2)}, u32[]{:S(2)}) %collective-permute-start.7) | collective-permute-done | bytes 196640 | tf_op jit(solution)/shard_map/ppermute | solution.py:609
  45.5 2.6 %collective-permute-start.13 = (bf16[384,128]{1,0:T(8,128)(2,1)S(1)}, bf16[384,128]{1,0:T(8,128)(2,1)S(1)}, u32[]{:S(2)}, u32[]{:S(2)}) collective-permute-start(bf16[384,128]{1,0:T(8,128)(2,1)S(1)} %get-tuple-element.66), channel_id=1, source_target_pairs={{0,16},{1,17},{2,18},{3,19},{4,20},{5,21},{6,22},{7,23},{8,24},{9,... | collective-permute-start | bytes 294920 | tf_op jit(solution)/shard_map/ppermute | solution.py:609
  48.2 1.4 %collective-permute-start.14 = (bf16[384,128]{1,0:T(8,128)(2,1)S(1)}, bf16[384,128]{1,0:T(8,128)(2,1)S(1)}, u32[]{:S(2)}, u32[]{:S(2)}) collective-permute-start(bf16[384,128]{1,0:T(8,128)(2,1)S(1)} %get-tuple-element.67), channel_id=1, source_target_pairs={{0,24},{1,25},{2,26},{3,27},{4,28},{5,29},{6,30},{7,31},{8,16},{9,... | collective-permute-start | bytes 294920 | tf_op jit(solution)/shard_map/ppermute | solution.py:609
  49.7 4.8 %collective-permute-done.13.a = bf16[384,128]{1,0:T(8,128)(2,1)S(1)} collective-permute-done((bf16[384,128]{1,0:T(8,128)(2,1)S(1)}, bf16[384,128]{1,0:T(8,128)(2,1)S(1)}, u32[]{:S(2)}, u32[]{:S(2)}) %collective-permute-start.13) | collective-permute-done | bytes 98336 | tf_op jit(solution)/shard_map/ppermute | solution.py:609
  54.5 0.9 %collective-permute-done.14.b = bf16[384,128]{1,0:T(8,128)(2,1)S(1)} collective-permute-done((bf16[384,128]{1,0:T(8,128)(2,1)S(1)}, bf16[384,128]{1,0:T(8,128)(2,1)S(1)}, u32[]{:S(2)}, u32[]{:S(2)}) %collective-permute-start.14) | collective-permute-done | bytes 98336 | tf_op jit(solution)/shard_map/ppermute | solution.py:609
  55.4 0.4 collective-permute-done.15.c
  55.8 0.9 %collective-permute-start.17 = (bf16[384,128]{1,0:T(8,128)(2,1)S(1)}, bf16[384,128]{1,0:T(8,128)(2,1)S(1)}, u32[]{:S(2)}, u32[]{:S(2)}) collective-permute-start(bf16[384,128]{1,0:T(8,128)(2,1)S(1)} %final.1.refs_0_), channel_id=1, source_target_pairs={{0,2},{1,3},{2,0},{3,1},{4,6},{5,7},{6,4},{7,5},{8,10},{9,11},{10,... | collective-permute-start | bytes 294920 | tf_op jit(solution)/shard_map/ppermute | solution.py:609
  56.7 3.8 %collective-permute-done.17.refs_1_ = bf16[384,128]{1,0:T(8,128)(2,1)S(1)} collective-permute-done((bf16[384,128]{1,0:T(8,128)(2,1)S(1)}, bf16[384,128]{1,0:T(8,128)(2,1)S(1)}, u32[]{:S(2)}, u32[]{:S(2)}) %collective-permute-start.17) | collective-permute-done | bytes 98336 | tf_op jit(solution)/shard_map/ppermute | solution.py:609
  60.5 1.3 %stats.2 = (f32[8,192,192]{2,1,0:T(8,128)}, f32[8,128,128]{2,1,0:T(8,128)}) custom-call(bf16[384,128]{1,0:T(8,128)(2,1)S(1)} %final.1.refs_0_, bf16[384,128]{1,0:T(8,128)(2,1)S(1)} %collective-permute-done.17.refs_1_, f32[8,192,192]{2,1,0:T(8,128)S(1)} %copy-done, f32[8,128,128]{2,1,0:T(8,128)S(1)} %copy-done.1), custom_call_target="tpu_custom_call" | custom-call | flops 80000000 | bytes 1048576 | tf_op jit(solution)/shard_map/stats/pallas_call | solution.py:591
  61.8 1.3 %stats.3 = (f32[8,192,192]{2,1,0:T(8,128)}, f32[8,128,128]{2,1,0:T(8,128)}) custom-call(bf16[384,128]{1,0:T(8,128)(2,1)S(1)} %collective-permute-done.16.refs_0_, bf16[384,128]{1,0:T(8,128)(2,1)S(1)} %collective-permute-done.18.refs_1_, f32[8,192,192]{2,1,0:T(8,128)S(1)} %copy-done, ...), custom_call_target="tpu_custom_call", output_to_operand_aliasing={{0}: (4, {}), {1}: (5, {})} | custom-call | flops 80000000 | bytes 1048576 | tf_op jit(solution)/shard_map/stats/pallas_call | solution.py:591
  (37 shorter events, 1.5 us)
Async XLA Ops:
  0.6 0.8 %copy-start.2 = (f32[4,1920]{1,0:T(4,128)S(1)}, f32[4,1920]{1,0:T(4,128)}, u32[]{:S(2)}) copy-start(f32[4,1920]{1,0:T(4,128)} %audio.1) | copy-start | bytes 92164
  1.6 5.6 %collective-permute-start = (f32[16,128]{1,0:T(8,128)S(1)}, f32[16,128]{1,0:T(8,128)S(1)}, u32[]{:S(2)}, u32[]{:S(2)}) collective-permute-start(f32[16,128]{1,0:T(8,128)S(1)} %get-tuple-element.39), channel_id=1, source_target_pairs={{0,1},{1,0},{2,3},{3,2},{4,5},{5,4},{6,7},{7,6},{8,9},{9,8},{10,11... | collective-permute-start | bytes 24584 | tf_op jit(solution)/shard_map/ppermute | solution.py:609
  2.1 5.1 %collective-permute-start.1 = (f32[16,128]{1,0:T(8,128)S(1)}, f32[16,128]{1,0:T(8,128)S(1)}, u32[]{:S(2)}, u32[]{:S(2)}) collective-permute-start(f32[16,128]{1,0:T(8,128)S(1)} %get-tuple-element.40), channel_id=1, source_target_pairs={{0,2},{1,3},{2,0},{3,1},{4,6},{5,7},{6,4},{7,5},{8,10},{9,11},{10,... | collective-permute-start | bytes 24584 | tf_op jit(solution)/shard_map/ppermute | solution.py:609
  4.7 3.1 %collective-permute-start.2 = (f32[16,128]{1,0:T(8,128)S(1)}, f32[16,128]{1,0:T(8,128)S(1)}, u32[]{:S(2)}, u32[]{:S(2)}) collective-permute-start(f32[16,128]{1,0:T(8,128)S(1)} %get-tuple-element.41), channel_id=1, source_target_pairs={{0,3},{1,2},{2,1},{3,0},{4,7},{5,6},{6,5},{7,4},{8,11},{9,10},{10,... | collective-permute-start | bytes 24584 | tf_op jit(solution)/shard_map/ppermute | solution.py:609
  7.8 6.9 %collective-permute-start.4 = (f32[1,640]{1,0:T(1,128)S(1)}, f32[1,640]{1,0:T(1,128)S(1)}, u32[]{:S(2)}, u32[]{:S(2)}) collective-permute-start(f32[1,640]{1,0:T(1,128)S(1)} %get-tuple-element.75), channel_id=1, source_target_pairs={{4,8},{5,9},{6,10},{7,11},{8,4},{9,5},{10,6},{11,7},{12,16},{13,17... | collective-permute-start | bytes 7688 | tf_op jit(solution)/shard_map/ppermute | solution.py:609
  8.5 6.3 %collective-permute-start.3 = (f32[1,640]{1,0:T(1,128)S(1)}, f32[1,640]{1,0:T(1,128)S(1)}, u32[]{:S(2)}, u32[]{:S(2)}) collective-permute-start(f32[1,640]{1,0:T(1,128)S(1)} %get-tuple-element.76), channel_id=1, source_target_pairs={{0,4},{1,5},{2,6},{3,7},{4,0},{5,1},{6,2},{7,3},{8,12},{9,13},{10,... | collective-permute-start | bytes 7688 | tf_op jit(solution)/shard_map/ppermute | solution.py:609
  12.8 1.9 %copy-start.3 = (bf16[1,384,512]{2,1,0:T(8,128)(2,1)S(1)}, bf16[1,384,512]{2,1,0:T(8,128)(2,1)}, u32[]{:S(2)}) copy-start(bf16[1,384,512]{2,1,0:T(8,128)(2,1)} %param.19) | copy-start | bytes 1179652
  12.8 1.9 %copy-start.4 = (bf16[1536,512]{1,0:T(8,128)(2,1)S(1)}, bf16[1536,512]{1,0:T(8,128)(2,1)}, u32[]{:S(2)}) copy-start(bf16[1536,512]{1,0:T(8,128)(2,1)} %k1_ref.1) | copy-start | bytes 4718596
  12.9 2.0 %copy-start.5 = (bf16[1536,512]{1,0:T(8,128)(2,1)S(1)}, bf16[1536,512]{1,0:T(8,128)(2,1)}, u32[]{:S(2)}) copy-start(bf16[1536,512]{1,0:T(8,128)(2,1)} %k2_ref.3) | copy-start | bytes 4718596
  20.7 2.3 %collective-permute-start.5 = (bf16[2,4,384,128]{3,2,1,0:T(8,128)(2,1)S(1)}, bf16[2,4,384,128]{3,2,1,0:T(8,128)(2,1)S(1)}, u32[]{:S(2)}, u32[]{:S(2)}) collective-permute-start(bf16[2,4,384,128]{3,2,1,0:T(8,128)(2,1)S(1)} %get-tuple-element.56), channel_id=1, source_target_pairs={{0,1},{1,0},{2,3},{3,2},{4,5},{5,4},{6,7},{7,6},{8,9},{9,8},{10,11... | collective-permute-start | bytes 2359304 | tf_op jit(solution)/shard_map/ppermute | solution.py:609
  24.3 4.1 %collective-permute-start.6 = (bf16[2,4,384,128]{3,2,1,0:T(8,128)(2,1)S(1)}, bf16[2,4,384,128]{3,2,1,0:T(8,128)(2,1)S(1)}, u32[]{:S(2)}, u32[]{:S(2)}) collective-permute-start(bf16[2,4,384,128]{3,2,1,0:T(8,128)(2,1)S(1)} %backward.1), channel_id=1, source_target_pairs={{0,1},{1,0},{2,3},{3,2},{4,5},{5,4},{6,7},{7,6},{8,9},{9,8},{10,11... | collective-permute-start | bytes 2359304 | tf_op jit(solution)/shard_map/ppermute | solution.py:609
  24.8 7.8 %collective-permute-start.10 = (bf16[2,384,128]{2,1,0:T(8,128)(2,1)S(1)}, bf16[2,384,128]{2,1,0:T(8,128)(2,1)S(1)}, u32[]{:S(2)}, u32[]{:S(2)}) collective-permute-start(bf16[2,384,128]{2,1,0:T(8,128)(2,1)S(1)} %get-tuple-element.62), channel_id=1, source_target_pairs={{0,2},{1,3},{2,0},{3,1},{4,6},{5,7},{6,4},{7,5},{8,10},{9,11},{10,... | collective-permute-start | bytes 589832 | tf_op jit(solution)/shard_map/ppermute | solution.py:609
  26.0 16.2 %collective-permute-start.11 = (bf16[2,384,128]{2,1,0:T(8,128)(2,1)S(1)}, bf16[2,384,128]{2,1,0:T(8,128)(2,1)S(1)}, u32[]{:S(2)}, u32[]{:S(2)}) collective-permute-start(bf16[2,384,128]{2,1,0:T(8,128)(2,1)S(1)} %get-tuple-element.63), channel_id=1, source_target_pairs={{0,4},{1,5},{2,6},{3,7},{4,0},{5,1},{6,2},{7,3},{8,12},{9,13},{10,... | collective-permute-start | bytes 589832 | tf_op jit(solution)/shard_map/ppermute | solution.py:609
  27.6 14.6 %collective-permute-start.12 = (bf16[2,384,128]{2,1,0:T(8,128)(2,1)S(1)}, bf16[2,384,128]{2,1,0:T(8,128)(2,1)S(1)}, u32[]{:S(2)}, u32[]{:S(2)}) collective-permute-start(bf16[2,384,128]{2,1,0:T(8,128)(2,1)S(1)} %get-tuple-element.64), channel_id=1, source_target_pairs={{0,6},{1,7},{2,4},{3,5},{4,2},{5,3},{6,0},{7,1},{8,14},{9,15},{10,... | collective-permute-start | bytes 589832 | tf_op jit(solution)/shard_map/ppermute | solution.py:609
  28.5 32.0 %copy-start = (f32[8,192,192]{2,1,0:T(8,128)S(1)}, f32[8,192,192]{2,1,0:T(8,128)}, u32[]{:S(2)}) copy-start(f32[8,192,192]{2,1,0:T(8,128)} %refs_2_.3) | copy-start | bytes 3538948
  28.5 32.0 %copy-start.1 = (f32[8,128,128]{2,1,0:T(8,128)S(1)}, f32[8,128,128]{2,1,0:T(8,128)}, u32[]{:S(2)}) copy-start(f32[8,128,128]{2,1,0:T(8,128)} %refs_3_.3) | copy-start | bytes 1572868
  28.5 16.8 %collective-permute-start.7 = (bf16[2,384,128]{2,1,0:T(8,128)(2,1)S(1)}, bf16[2,384,128]{2,1,0:T(8,128)(2,1)S(1)}, u32[]{:S(2)}, u32[]{:S(2)}) collective-permute-start(bf16[2,384,128]{2,1,0:T(8,128)(2,1)S(1)} %get-tuple-element.59), channel_id=1, source_target_pairs={{0,4},{1,5},{2,6},{3,7},{4,0},{5,1},{6,2},{7,3},{8,12},{9,13},{10,... | collective-permute-start | bytes 589832 | tf_op jit(solution)/shard_map/ppermute | solution.py:609
  30.2 15.1 %collective-permute-start.8 = (bf16[2,384,128]{2,1,0:T(8,128)(2,1)S(1)}, bf16[2,384,128]{2,1,0:T(8,128)(2,1)S(1)}, u32[]{:S(2)}, u32[]{:S(2)}) collective-permute-start(bf16[2,384,128]{2,1,0:T(8,128)(2,1)S(1)} %get-tuple-element.60), channel_id=1, source_target_pairs={{0,6},{1,7},{2,4},{3,5},{4,2},{5,3},{6,0},{7,1},{8,14},{9,15},{10,... | collective-permute-start | bytes 589832 | tf_op jit(solution)/shard_map/ppermute | solution.py:609
  32.6 12.7 %collective-permute-start.9 = (bf16[2,384,128]{2,1,0:T(8,128)(2,1)S(1)}, bf16[2,384,128]{2,1,0:T(8,128)(2,1)S(1)}, u32[]{:S(2)}, u32[]{:S(2)}) collective-permute-start(bf16[2,384,128]{2,1,0:T(8,128)(2,1)S(1)} %get-tuple-element.61), channel_id=1, source_target_pairs={{0,2},{1,3},{2,0},{3,1},{4,6},{5,7},{6,4},{7,5},{8,10},{9,11},{10,... | collective-permute-start | bytes 589832 | tf_op jit(solution)/shard_map/ppermute | solution.py:609
  45.5 9.0 %collective-permute-start.13 = (bf16[384,128]{1,0:T(8,128)(2,1)S(1)}, bf16[384,128]{1,0:T(8,128)(2,1)S(1)}, u32[]{:S(2)}, u32[]{:S(2)}) collective-permute-start(bf16[384,128]{1,0:T(8,128)(2,1)S(1)} %get-tuple-element.66), channel_id=1, source_target_pairs={{0,16},{1,17},{2,18},{3,19},{4,20},{5,21},{6,22},{7,23},{8,24},{9,... | collective-permute-start | bytes 294920 | tf_op jit(solution)/shard_map/ppermute | solution.py:609
  48.2 7.2 %collective-permute-start.14 = (bf16[384,128]{1,0:T(8,128)(2,1)S(1)}, bf16[384,128]{1,0:T(8,128)(2,1)S(1)}, u32[]{:S(2)}, u32[]{:S(2)}) collective-permute-start(bf16[384,128]{1,0:T(8,128)(2,1)S(1)} %get-tuple-element.67), channel_id=1, source_target_pairs={{0,24},{1,25},{2,26},{3,27},{4,28},{5,29},{6,30},{7,31},{8,16},{9,... | collective-permute-start | bytes 294920 | tf_op jit(solution)/shard_map/ppermute | solution.py:609
  49.5 6.2 %collective-permute-start.15 = (bf16[384,128]{1,0:T(8,128)(2,1)S(1)}, bf16[384,128]{1,0:T(8,128)(2,1)S(1)}, u32[]{:S(2)}, u32[]{:S(2)}) collective-permute-start(bf16[384,128]{1,0:T(8,128)(2,1)S(1)} %get-tuple-element.68), channel_id=1, source_target_pairs={{0,8},{1,9},{2,10},{3,11},{4,12},{5,13},{6,14},{7,15},{8,0},{9,1},... | collective-permute-start | bytes 294920 | tf_op jit(solution)/shard_map/ppermute | solution.py:609
  55.8 4.7 %collective-permute-start.17 = (bf16[384,128]{1,0:T(8,128)(2,1)S(1)}, bf16[384,128]{1,0:T(8,128)(2,1)S(1)}, u32[]{:S(2)}, u32[]{:S(2)}) collective-permute-start(bf16[384,128]{1,0:T(8,128)(2,1)S(1)} %final.1.refs_0_), channel_id=1, source_target_pairs={{0,2},{1,3},{2,0},{3,1},{4,6},{5,7},{6,4},{7,5},{8,10},{9,11},{10,... | collective-permute-start | bytes 294920 | tf_op jit(solution)/shard_map/ppermute | solution.py:609
  56.7 5.1 %collective-permute-start.16 = (bf16[384,128]{1,0:T(8,128)(2,1)S(1)}, bf16[384,128]{1,0:T(8,128)(2,1)S(1)}, u32[]{:S(2)}, u32[]{:S(2)}) collective-permute-start(bf16[384,128]{1,0:T(8,128)(2,1)S(1)} %final.1.refs_0_), channel_id=1, source_target_pairs={{0,1},{1,0},{2,3},{3,2},{4,5},{5,4},{6,7},{7,6},{8,9},{9,8},{10,11... | collective-permute-start | bytes 294920 | tf_op jit(solution)/shard_map/ppermute | solution.py:609
  60.5 1.3 %collective-permute-start.18 = (bf16[384,128]{1,0:T(8,128)(2,1)S(1)}, bf16[384,128]{1,0:T(8,128)(2,1)S(1)}, u32[]{:S(2)}, u32[]{:S(2)}) collective-permute-start(bf16[384,128]{1,0:T(8,128)(2,1)S(1)} %collective-permute-done.17.refs_1_), channel_id=1, source_target_pairs={{0,1},{1,0},{2,3},{3,2},{4,5},{5,4},{6,7},{7,6},{8,9},{9,8},{10,11... | collective-permute-start | bytes 294920 | tf_op jit(solution)/shard_map/ppermute | solution.py:609

commit v7 on v6

--- a/solution.py
+++ b/solution.py
@@ -584,7 +584,7 @@
         copy.wait()
 
 
-def stats(pieces, flips, lprev, rprev, begun=()):
+def stats(pieces, flips, lprev, rprev, begun=(), flops=int(1e8)):
     count = len(pieces)
     slots = 2 * count
     hbm = pl.BlockSpec(memory_space=pl.ANY)
@@ -600,9 +600,24 @@
             pltpu.SemaphoreType.DMA((2, slots)),
         ],
         compiler_params=params(),
-        cost_estimate=cost(slots * int(2e7), slots << 18),
+        cost_estimate=cost(flops, slots << 18),
         name="stats",
     )(*pieces, lprev, rprev, *begun)
+
+
+def relay_kernel(source, order, out):
+    out[...] = source[...]
+
+
+def relay(source, order):
+    return pl.pallas_call(
+        relay_kernel,
+        out_shape=sds(source.shape, source.dtype),
+        in_specs=[VM, pl.BlockSpec(memory_space=pl.ANY)],
+        out_specs=VM,
+        compiler_params=params(),
+        name="relay",
+    )(source, order)
 
 
 def permute(value, route):
@@ -729,9 +744,12 @@
     arrived = [permute(value, way) for value, way in zip(out, by_z)]
     owned = final(own, *arrived)
     other = permute(owned, by_x)
-    far = permute(owned, by_core), permute(other, by_core)
-    begun = stats((owned, other), ((0, 0), (0, 1)), left_prev, right_prev)
-    left, right = stats(far, ((1, 0), (1, 1)), left_prev, right_prev, begun)
+    near = permute(owned, by_core)
+    begun = stats((owned, near), ((0, 0), (1, 0)), left_prev, right_prev, flops=int(2e9))
+    other = relay(other, begun[0])
+    far = permute(other, by_core)
+    begun = stats((other,), ((0, 1),), left_prev, right_prev, begun, int(1e10))
+    left, right = stats((far,), ((1, 1),), left_prev, right_prev, begun)
     return frames[None], left, right
 
 

time: 63.4 us -> 65.3 us (1.030)
  local copies, waits for them, and re-layouts: 1.55 us -> 2.95 us
  Pallas kernels: 14.6 us -> 15.4 us
    unnamed x12 -> x14, local copies, waits for them, and re-layouts: 0.84 us -> 2.24 us
    pallas_call x2 -> x3, Pallas kernels: 2.55 us -> 3.38 us  [stats(): pl.pallas_call(functools.partial(stats_kernel, flips, count), out_shape=[...]
  transfers between devices with their start and end apart: 19 -> 19, of which waited for: 8 -> 10; matrix products, arithmetic and copies ran while one was open for 3% -> 3% of each run, Pallas kernels for 9% -> 10%
where the time goes in v7:
time: 65.3 us; the launch traced here: 64.9 us
  waiting for transfers between devices  22.7 us (35%)
  starting transfers between devices  21.4 us (33%)
  Pallas kernels  15.4 us (24%)
  local copies, waits for them, and re-layouts  2.95 us (5%)
  other arithmetic  1.57 us (2%)
  between operations  0.86 us (1%)
    ppermute x19, waiting for transfers between devices, permute(): return lax.ppermute(value, AXES, route)  22.7 us
    ppermute x19, starting transfers between devices, permute(): return lax.ppermute(value, AXES, route)  21.4 us
    pallas_call x1, Pallas kernels, forward(): pl.pallas_call(functools.partial(forward_kernel, special, groups, scale),...  5.88 us
    pallas_call x3, Pallas kernels, stats(): pl.pallas_call(functools.partial(stats_kernel, flips, count), out_shape=[...  3.38 us
    pallas_call x1, Pallas kernels, window(): pl.pallas_call(functools.partial(window_kernel, special), out_shape=[sds(...  2.26 us
    unnamed x14, local copies, waits for them, and re-layouts  2.24 us
    pallas_call x1, Pallas kernels, audio_layer(): pl.pallas_call(functools.partial(audio_kernel, special), out_shape=[sds((...  1.89 us
  transfers between devices with their start and end apart: 19, of which 10 were waited for; matrix products, arithmetic and copies ran while one was open for 3% of the time, Pallas kernels for 10%

profile of v7, /device:TPU:0, one launch (start us, length us, event | category | flops | bytes accessed | tf_op | source)
XLA Modules:
  0.0 64.9 jit_solution(18263262307711256095)
XLA Ops:
  0.6 0.7 %copy-done.3 = f32[4,1920]{1,0:T(4,128)S(1)} copy-done((f32[4,1920]{1,0:T(4,128)S(1)}, f32[4,1920]{1,0:T(4,128)}, u32[]{:S(2)}) %copy-start.3) | copy-done | bytes 30744
  2.1 2.6 %collective-permute-start.1 = (f32[16,128]{1,0:T(8,128)S(1)}, f32[16,128]{1,0:T(8,128)S(1)}, u32[]{:S(2)}, u32[]{:S(2)}) collective-permute-start(f32[16,128]{1,0:T(8,128)S(1)} %get-tuple-element.42), channel_id=1, source_target_pairs={{0,2},{1,3},{2,0},{3,1},{4,6},{5,7},{6,4},{7,5},{8,10},{9,11},{10,... | collective-permute-start | bytes 24584 | tf_op jit(solution)/shard_map/ppermute | solution.py:624
  4.7 0.7 %convert_element_type.34 = f32[4]{0:T(128)S(1)} convert(s32[4]{0:T(128)} %param.12) | non-fusion elementwise | flops 4 | bytes 32 | tf_op jit(solution)/shard_map/convert_element_type | solution.py:669
  5.4 0.7 %slice_bitcast_fusion = bf16[1,512]{1,0:T(2,128)(2,1)S(1)} fusion(bf16[1,384,512]{2,1,0:T(8,128)(2,1)} %param.19), kind=kLoop, calls=%fused_computation.5 | loop fusion | bytes 2048 | tf_op jit(solution)/shard_map/convert_element_type | solution.py:668
  6.1 0.8 %pad_add_fusion.table_ref.rows_ref = f32[24,512]{1,0:T(8,128)S(1)} fusion(f32[1,512]{1,0:T(1,128)S(1)} %bitcast.6, f32[3,512]{1,0:T(4,128)} %param.18, f32[3,512]{1,0:T(4,128)} %param.17, f32[3,512]{1,0:T(4,128)} %param.16, f32[10,512]{1,0:T(8,128)} %param.13, bf16[1,512]{1,0:T(2,128)(2,1)S(1)} %slice_bitcast_fusion), kind=kLoop, calls=%fused_computation | loop fusion | flops 73728 | bytes 91136 | tf_op jit(solution)/shard_map/add | solution.py:672
  7.2 0.6 collective-permute-done.2.p3
  7.8 0.7 %collective-permute-start.4 = (f32[1,640]{1,0:T(1,128)S(1)}, f32[1,640]{1,0:T(1,128)S(1)}, u32[]{:S(2)}, u32[]{:S(2)}) collective-permute-start(f32[1,640]{1,0:T(1,128)S(1)} %get-tuple-element.79), channel_id=1, source_target_pairs={{4,8},{5,9},{6,10},{7,11},{8,4},{9,5},{10,6},{11,7},{12,16},{13,17... | collective-permute-start | bytes 7688 | tf_op jit(solution)/shard_map/ppermute | solution.py:624
  8.5 4.4 %collective-permute-start.3 = (f32[1,640]{1,0:T(1,128)S(1)}, f32[1,640]{1,0:T(1,128)S(1)}, u32[]{:S(2)}, u32[]{:S(2)}) collective-permute-start(f32[1,640]{1,0:T(1,128)S(1)} %get-tuple-element.80), channel_id=1, source_target_pairs={{0,4},{1,5},{2,6},{3,7},{4,0},{5,1},{6,2},{7,3},{8,12},{9,13},{10,... | collective-permute-start | bytes 7688 | tf_op jit(solution)/shard_map/ppermute | solution.py:624
  12.9 1.9 %audio_layer.1 = (bf16[384,2560]{1,0:T(8,128)(2,1)S(1)}, f32[8,512]{1,0:T(8,128)S(1)}, f32[24,128]{1,0:T(8,128)S(1)}) custom-call(f32[16,128]{1,0:T(8,128)S(1)} %get-tuple-element.40.p0, f32[16,128]{1,0:T(8,128)S(1)} %collective-permute-done.p1, f32[16,128]{1,0:T(8,128)S(1)} %collective-permute-done.1.p2, f32[16,128]{1,0:T(8,128)S(1)} %collective-permute-done.2.p3, ...), custom_call_target="tpu_custom_call" | custom-call | flops 3000000000 | bytes 5242880 | tf_op jit(solution)/shard_map/audio_layer/pallas_call | solution.py:236
  14.9 5.9 %forward.1 = (bf16[400,2560]{1,0:T(8,128)(2,1)S(1)}, bf16[384,512]{1,0:T(8,128)(2,1)}, f32[2,4,384,128]{3,2,1,0:T(8,128)S(1)}, bf16[2,4,384,128]{3,2,1,0:T(8,128...) custom-call(bf16[384,2560]{1,0:T(8,128)(2,1)S(1)} %get-tuple-element, ...), custom_call_target="tpu_custom_call" | custom-call | flops 8000000000 | bytes 10485760 | tf_op jit(solution)/shard_map/forward/pallas_call | solution.py:403
  20.7 2.3 %window.1 = (bf16[2,384,512]{2,1,0:T(8,128)(2,1)S(1)}, f32[2,4,384,128]{3,2,1,0:T(8,128)S(1)}) custom-call(bf16[400,512]{1,0:T(8,128)(2,1)S(1)} %get-tuple-element.50.d2_ref, bf16[1536,512]{1,0:T(8,128)(2,1)S(1)} %copy-done.6, f32[2,400,512]{2,1,0:T(8,128)S(1)} %get-tuple-element.51.hat_ref, f32[2,400,512]{2,1,0:T(8,128)S(1)} %get-tuple-element.52.slope_ref, ...), custom_call_target="tpu_custom_call" | custom-call | flops 2500000000 | bytes 3145728 | tf_op jit(solution)/shard_map/window/pallas_call | solution.py:467
  23.2 1.0 %backward.1 = bf16[2,4,384,128]{3,2,1,0:T(8,128)(2,1)S(1)} custom-call(bf16[2,384,512]{2,1,0:T(8,128)(2,1)S(1)} %get-tuple-element.56.d1, bf16[400,2560]{1,0:T(8,128)(2,1)S(1)} %get-tuple-element.54.a0_ref, f32[2,384,128]{2,1,0:T(8,128)S(1)} %get-tuple-element.59.order_ref.refs_4_), custom_call_target="tpu_custom_call" | custom-call | flops 2000000000 | bytes 5242880 | tf_op jit(solution)/shard_map/backward/pallas_call | solution.py:490
  24.3 0.6 collective-permute-start.6
  24.8 1.2 %collective-permute-start.10 = (bf16[2,384,128]{2,1,0:T(8,128)(2,1)S(1)}, bf16[2,384,128]{2,1,0:T(8,128)(2,1)S(1)}, u32[]{:S(2)}, u32[]{:S(2)}) collective-permute-start(bf16[2,384,128]{2,1,0:T(8,128)(2,1)S(1)} %get-tuple-element.64), channel_id=1, source_target_pairs={{0,2},{1,3},{2,0},{3,1},{4,6},{5,7},{6,4},{7,5},{8,10},{9,11},{10,... | collective-permute-start | bytes 589832 | tf_op jit(solution)/shard_map/ppermute | solution.py:624
  26.0 1.6 %collective-permute-start.11 = (bf16[2,384,128]{2,1,0:T(8,128)(2,1)S(1)}, bf16[2,384,128]{2,1,0:T(8,128)(2,1)S(1)}, u32[]{:S(2)}, u32[]{:S(2)}) collective-permute-start(bf16[2,384,128]{2,1,0:T(8,128)(2,1)S(1)} %get-tuple-element.65), channel_id=1, source_target_pairs={{0,4},{1,5},{2,6},{3,7},{4,0},{5,1},{6,2},{7,3},{8,12},{9,13},{10,... | collective-permute-start | bytes 589832 | tf_op jit(solution)/shard_map/ppermute | solution.py:624
  27.6 0.7 %collective-permute-start.12 = (bf16[2,384,128]{2,1,0:T(8,128)(2,1)S(1)}, bf16[2,384,128]{2,1,0:T(8,128)(2,1)S(1)}, u32[]{:S(2)}, u32[]{:S(2)}) collective-permute-start(bf16[2,384,128]{2,1,0:T(8,128)(2,1)S(1)} %get-tuple-element.66), channel_id=1, source_target_pairs={{0,6},{1,7},{2,4},{3,5},{4,2},{5,3},{6,0},{7,1},{8,14},{9,15},{10,... | collective-permute-start | bytes 589832 | tf_op jit(solution)/shard_map/ppermute | solution.py:624
  28.5 1.7 %collective-permute-start.7 = (bf16[2,384,128]{2,1,0:T(8,128)(2,1)S(1)}, bf16[2,384,128]{2,1,0:T(8,128)(2,1)S(1)}, u32[]{:S(2)}, u32[]{:S(2)}) collective-permute-start(bf16[2,384,128]{2,1,0:T(8,128)(2,1)S(1)} %get-tuple-element.61), channel_id=1, source_target_pairs={{0,4},{1,5},{2,6},{3,7},{4,0},{5,1},{6,2},{7,3},{8,12},{9,13},{10,... | collective-permute-start | bytes 589832 | tf_op jit(solution)/shard_map/ppermute | solution.py:624
  30.2 1.1 %collective-permute-start.8 = (bf16[2,384,128]{2,1,0:T(8,128)(2,1)S(1)}, bf16[2,384,128]{2,1,0:T(8,128)(2,1)S(1)}, u32[]{:S(2)}, u32[]{:S(2)}) collective-permute-start(bf16[2,384,128]{2,1,0:T(8,128)(2,1)S(1)} %get-tuple-element.62), channel_id=1, source_target_pairs={{0,6},{1,7},{2,4},{3,5},{4,2},{5,3},{6,0},{7,1},{8,14},{9,15},{10,... | collective-permute-start | bytes 589832 | tf_op jit(solution)/shard_map/ppermute | solution.py:624
  31.2 1.4 %collective-permute-done.10.refs_5_ = bf16[2,384,128]{2,1,0:T(8,128)(2,1)S(1)} collective-permute-done((bf16[2,384,128]{2,1,0:T(8,128)(2,1)S(1)}, bf16[2,384,128]{2,1,0:T(8,128)(2,1)S(1)}, u32[]{:S(2)}, u32[]{:S(2)}) %collective-permute-start.10) | collective-permute-done | bytes 196640 | tf_op jit(solution)/shard_map/ppermute | solution.py:624
  32.6 1.2 %collective-permute-start.9 = (bf16[2,384,128]{2,1,0:T(8,128)(2,1)S(1)}, bf16[2,384,128]{2,1,0:T(8,128)(2,1)S(1)}, u32[]{:S(2)}, u32[]{:S(2)}) collective-permute-start(bf16[2,384,128]{2,1,0:T(8,128)(2,1)S(1)} %get-tuple-element.63), channel_id=1, source_target_pairs={{0,2},{1,3},{2,0},{3,1},{4,6},{5,7},{6,4},{7,5},{8,10},{9,11},{10,... | collective-permute-start | bytes 589832 | tf_op jit(solution)/shard_map/ppermute | solution.py:624
  33.8 8.5 %collective-permute-done.11.refs_6_ = bf16[2,384,128]{2,1,0:T(8,128)(2,1)S(1)} collective-permute-done((bf16[2,384,128]{2,1,0:T(8,128)(2,1)S(1)}, bf16[2,384,128]{2,1,0:T(8,128)(2,1)S(1)}, u32[]{:S(2)}, u32[]{:S(2)}) %collective-permute-start.11) | collective-permute-done | bytes 196640 | tf_op jit(solution)/shard_map/ppermute | solution.py:624
  42.3 3.0 %collective-permute-done.7.refs_1_ = bf16[2,384,128]{2,1,0:T(8,128)(2,1)S(1)} collective-permute-done((bf16[2,384,128]{2,1,0:T(8,128)(2,1)S(1)}, bf16[2,384,128]{2,1,0:T(8,128)(2,1)S(1)}, u32[]{:S(2)}, u32[]{:S(2)}) %collective-permute-start.7) | collective-permute-done | bytes 196640 | tf_op jit(solution)/shard_map/ppermute | solution.py:624
  45.5 2.6 %collective-permute-start.13 = (bf16[384,128]{1,0:T(8,128)(2,1)S(1)}, bf16[384,128]{1,0:T(8,128)(2,1)S(1)}, u32[]{:S(2)}, u32[]{:S(2)}) collective-permute-start(bf16[384,128]{1,0:T(8,128)(2,1)S(1)} %get-tuple-element.68), channel_id=1, source_target_pairs={{0,16},{1,17},{2,18},{3,19},{4,20},{5,21},{6,22},{7,23},{8,24},{9,... | collective-permute-start | bytes 294920 | tf_op jit(solution)/shard_map/ppermute | solution.py:624
  48.2 1.4 %collective-permute-start.14 = (bf16[384,128]{1,0:T(8,128)(2,1)S(1)}, bf16[384,128]{1,0:T(8,128)(2,1)S(1)}, u32[]{:S(2)}, u32[]{:S(2)}) collective-permute-start(bf16[384,128]{1,0:T(8,128)(2,1)S(1)} %get-tuple-element.69), channel_id=1, source_target_pairs={{0,24},{1,25},{2,26},{3,27},{4,28},{5,29},{6,30},{7,31},{8,16},{9,... | collective-permute-start | bytes 294920 | tf_op jit(solution)/shard_map/ppermute | solution.py:624
  49.7 4.8 %collective-permute-done.13.a = bf16[384,128]{1,0:T(8,128)(2,1)S(1)} collective-permute-done((bf16[384,128]{1,0:T(8,128)(2,1)S(1)}, bf16[384,128]{1,0:T(8,128)(2,1)S(1)}, u32[]{:S(2)}, u32[]{:S(2)}) %collective-permute-start.13) | collective-permute-done | bytes 98336 | tf_op jit(solution)/shard_map/ppermute | solution.py:624
  54.5 0.9 %collective-permute-done.14.b = bf16[384,128]{1,0:T(8,128)(2,1)S(1)} collective-permute-done((bf16[384,128]{1,0:T(8,128)(2,1)S(1)}, bf16[384,128]{1,0:T(8,128)(2,1)S(1)}, u32[]{:S(2)}, u32[]{:S(2)}) %collective-permute-start.14) | collective-permute-done | bytes 98336 | tf_op jit(solution)/shard_map/ppermute | solution.py:624
  55.9 0.9 %collective-permute-start.16 = (bf16[384,128]{1,0:T(8,128)(2,1)S(1)}, bf16[384,128]{1,0:T(8,128)(2,1)S(1)}, u32[]{:S(2)}, u32[]{:S(2)}) collective-permute-start(bf16[384,128]{1,0:T(8,128)(2,1)S(1)} %final.1.refs_0_), channel_id=1, source_target_pairs={{0,2},{1,3},{2,0},{3,1},{4,6},{5,7},{6,4},{7,5},{8,10},{9,11},{10,... | collective-permute-start | bytes 294920 | tf_op jit(solution)/shard_map/ppermute | solution.py:624
  57.2 1.3 %stats.3 = (f32[8,192,192]{2,1,0:T(8,128)}, f32[8,128,128]{2,1,0:T(8,128)}) custom-call(bf16[384,128]{1,0:T(8,128)(2,1)S(1)} %final.1.refs_0_, bf16[384,128]{1,0:T(8,128)(2,1)S(1)} %collective-permute-done.17.refs_1_, f32[8,192,192]{2,1,0:T(8,128)S(1)} %copy-done.1, f32[8,128,128]{2,1,0:T(8,128)S(1)} %copy-done.2), custom_call_target="tpu_custom_call" | custom-call | flops 2000000000 | bytes 1048576 | tf_op jit(solution)/shard_map/stats/pallas_call | solution.py:591
  58.4 2.6 %collective-permute-done.16.source = bf16[384,128]{1,0:T(8,128)(2,1)S(1)} collective-permute-done((bf16[384,128]{1,0:T(8,128)(2,1)S(1)}, bf16[384,128]{1,0:T(8,128)(2,1)S(1)}, u32[]{:S(2)}, u32[]{:S(2)}) %collective-permute-start.16) | collective-permute-done | bytes 98336 | tf_op jit(solution)/shard_map/ppermute | solution.py:624
  61.1 1.4 %copy-done = f32[8,192,192]{2,1,0:T(8,128)S(1)} copy-done((f32[8,192,192]{2,1,0:T(8,128)S(1)}, f32[8,192,192]{2,1,0:T(8,128)}, u32[]{:S(2)}) %copy-start) | copy-done | bytes 1179672
  62.6 1.1 %stats.4 = (f32[8,192,192]{2,1,0:T(8,128)}, f32[8,128,128]{2,1,0:T(8,128)}) custom-call(bf16[384,128]{1,0:T(8,128)(2,1)S(1)} %relay.1.refs_0_, f32[8,192,192]{2,1,0:T(8,128)S(1)} %copy-done.1, f32[8,128,128]{2,1,0:T(8,128)S(1)} %copy-done.2, f32[8,192,192]{2,1,0:T(8,128)} %get-tuple-element.71.order.refs_3_, ...), custom_call_target="tpu_custom_call", output_to_operand_aliasing={{0}: (3, {}), {1}: (4, {})} | custom-call | flops 10000000000 | bytes 524288 | tf_op jit(solution)/shard_map/stats/pallas_call | solution.py:591
  63.9 1.0 %stats.5 = (f32[8,192,192]{2,1,0:T(8,128)}, f32[8,128,128]{2,1,0:T(8,128)}) custom-call(bf16[384,128]{1,0:T(8,128)(2,1)S(1)} %collective-permute-done.18.refs_0_, f32[8,192,192]{2,1,0:T(8,128)S(1)} %copy-done.1, f32[8,128,128]{2,1,0:T(8,128)S(1)} %copy-done.2, ...), custom_call_target="tpu_custom_call", output_to_operand_aliasing={{0}: (3, {}), {1}: (4, {})} | custom-call | flops 100000000 | bytes 524288 | tf_op jit(solution)/shard_map/stats/pallas_call | solution.py:591
  (41 shorter events, 3.1 us)
Async XLA Ops:
  0.6 0.8 %copy-start.3 = (f32[4,1920]{1,0:T(4,128)S(1)}, f32[4,1920]{1,0:T(4,128)}, u32[]{:S(2)}) copy-start(f32[4,1920]{1,0:T(4,128)} %audio.1) | copy-start | bytes 92164
  1.6 5.6 %collective-permute-start = (f32[16,128]{1,0:T(8,128)S(1)}, f32[16,128]{1,0:T(8,128)S(1)}, u32[]{:S(2)}, u32[]{:S(2)}) collective-permute-start(f32[16,128]{1,0:T(8,128)S(1)} %get-tuple-element.41), channel_id=1, source_target_pairs={{0,1},{1,0},{2,3},{3,2},{4,5},{5,4},{6,7},{7,6},{8,9},{9,8},{10,11... | collective-permute-start | bytes 24584 | tf_op jit(solution)/shard_map/ppermute | solution.py:624
  2.1 5.1 %collective-permute-start.1 = (f32[16,128]{1,0:T(8,128)S(1)}, f32[16,128]{1,0:T(8,128)S(1)}, u32[]{:S(2)}, u32[]{:S(2)}) collective-permute-start(f32[16,128]{1,0:T(8,128)S(1)} %get-tuple-element.42), channel_id=1, source_target_pairs={{0,2},{1,3},{2,0},{3,1},{4,6},{5,7},{6,4},{7,5},{8,10},{9,11},{10,... | collective-permute-start | bytes 24584 | tf_op jit(solution)/shard_map/ppermute | solution.py:624
  4.7 3.1 %collective-permute-start.2 = (f32[16,128]{1,0:T(8,128)S(1)}, f32[16,128]{1,0:T(8,128)S(1)}, u32[]{:S(2)}, u32[]{:S(2)}) collective-permute-start(f32[16,128]{1,0:T(8,128)S(1)} %get-tuple-element.43), channel_id=1, source_target_pairs={{0,3},{1,2},{2,1},{3,0},{4,7},{5,6},{6,5},{7,4},{8,11},{9,10},{10,... | collective-permute-start | bytes 24584 | tf_op jit(solution)/shard_map/ppermute | solution.py:624
  7.8 6.9 %collective-permute-start.4 = (f32[1,640]{1,0:T(1,128)S(1)}, f32[1,640]{1,0:T(1,128)S(1)}, u32[]{:S(2)}, u32[]{:S(2)}) collective-permute-start(f32[1,640]{1,0:T(1,128)S(1)} %get-tuple-element.79), channel_id=1, source_target_pairs={{4,8},{5,9},{6,10},{7,11},{8,4},{9,5},{10,6},{11,7},{12,16},{13,17... | collective-permute-start | bytes 7688 | tf_op jit(solution)/shard_map/ppermute | solution.py:624
  8.5 6.3 %collective-permute-start.3 = (f32[1,640]{1,0:T(1,128)S(1)}, f32[1,640]{1,0:T(1,128)S(1)}, u32[]{:S(2)}, u32[]{:S(2)}) collective-permute-start(f32[1,640]{1,0:T(1,128)S(1)} %get-tuple-element.80), channel_id=1, source_target_pairs={{0,4},{1,5},{2,6},{3,7},{4,0},{5,1},{6,2},{7,3},{8,12},{9,13},{10,... | collective-permute-start | bytes 7688 | tf_op jit(solution)/shard_map/ppermute | solution.py:624
  12.8 1.9 %copy-start.4 = (bf16[1,384,512]{2,1,0:T(8,128)(2,1)S(1)}, bf16[1,384,512]{2,1,0:T(8,128)(2,1)}, u32[]{:S(2)}) copy-start(bf16[1,384,512]{2,1,0:T(8,128)(2,1)} %param.19) | copy-start | bytes 1179652
  12.8 1.9 %copy-start.5 = (bf16[1536,512]{1,0:T(8,128)(2,1)S(1)}, bf16[1536,512]{1,0:T(8,128)(2,1)}, u32[]{:S(2)}) copy-start(bf16[1536,512]{1,0:T(8,128)(2,1)} %k1_ref.1) | copy-start | bytes 4718596
  12.9 2.0 %copy-start.6 = (bf16[1536,512]{1,0:T(8,128)(2,1)S(1)}, bf16[1536,512]{1,0:T(8,128)(2,1)}, u32[]{:S(2)}) copy-start(bf16[1536,512]{1,0:T(8,128)(2,1)} %k2_ref.3) | copy-start | bytes 4718596
  20.7 2.3 %collective-permute-start.5 = (bf16[2,4,384,128]{3,2,1,0:T(8,128)(2,1)S(1)}, bf16[2,4,384,128]{3,2,1,0:T(8,128)(2,1)S(1)}, u32[]{:S(2)}, u32[]{:S(2)}) collective-permute-start(bf16[2,4,384,128]{3,2,1,0:T(8,128)(2,1)S(1)} %get-tuple-element.58), channel_id=1, source_target_pairs={{0,1},{1,0},{2,3},{3,2},{4,5},{5,4},{6,7},{7,6},{8,9},{9,8},{10,11... | collective-permute-start | bytes 2359304 | tf_op jit(solution)/shard_map/ppermute | solution.py:624
  24.3 4.1 %collective-permute-start.6 = (bf16[2,4,384,128]{3,2,1,0:T(8,128)(2,1)S(1)}, bf16[2,4,384,128]{3,2,1,0:T(8,128)(2,1)S(1)}, u32[]{:S(2)}, u32[]{:S(2)}) collective-permute-start(bf16[2,4,384,128]{3,2,1,0:T(8,128)(2,1)S(1)} %backward.1), channel_id=1, source_target_pairs={{0,1},{1,0},{2,3},{3,2},{4,5},{5,4},{6,7},{7,6},{8,9},{9,8},{10,11... | collective-permute-start | bytes 2359304 | tf_op jit(solution)/shard_map/ppermute | solution.py:624
  24.8 7.8 %collective-permute-start.10 = (bf16[2,384,128]{2,1,0:T(8,128)(2,1)S(1)}, bf16[2,384,128]{2,1,0:T(8,128)(2,1)S(1)}, u32[]{:S(2)}, u32[]{:S(2)}) collective-permute-start(bf16[2,384,128]{2,1,0:T(8,128)(2,1)S(1)} %get-tuple-element.64), channel_id=1, source_target_pairs={{0,2},{1,3},{2,0},{3,1},{4,6},{5,7},{6,4},{7,5},{8,10},{9,11},{10,... | collective-permute-start | bytes 589832 | tf_op jit(solution)/shard_map/ppermute | solution.py:624
  26.0 16.2 %collective-permute-start.11 = (bf16[2,384,128]{2,1,0:T(8,128)(2,1)S(1)}, bf16[2,384,128]{2,1,0:T(8,128)(2,1)S(1)}, u32[]{:S(2)}, u32[]{:S(2)}) collective-permute-start(bf16[2,384,128]{2,1,0:T(8,128)(2,1)S(1)} %get-tuple-element.65), channel_id=1, source_target_pairs={{0,4},{1,5},{2,6},{3,7},{4,0},{5,1},{6,2},{7,3},{8,12},{9,13},{10,... | collective-permute-start | bytes 589832 | tf_op jit(solution)/shard_map/ppermute | solution.py:624
  27.6 14.6 %collective-permute-start.12 = (bf16[2,384,128]{2,1,0:T(8,128)(2,1)S(1)}, bf16[2,384,128]{2,1,0:T(8,128)(2,1)S(1)}, u32[]{:S(2)}, u32[]{:S(2)}) collective-permute-start(bf16[2,384,128]{2,1,0:T(8,128)(2,1)S(1)} %get-tuple-element.66), channel_id=1, source_target_pairs={{0,6},{1,7},{2,4},{3,5},{4,2},{5,3},{6,0},{7,1},{8,14},{9,15},{10,... | collective-permute-start | bytes 589832 | tf_op jit(solution)/shard_map/ppermute | solution.py:624
  28.5 28.7 %copy-start.1 = (f32[8,192,192]{2,1,0:T(8,128)S(1)}, f32[8,192,192]{2,1,0:T(8,128)}, u32[]{:S(2)}) copy-start(f32[8,192,192]{2,1,0:T(8,128)} %refs_1_.3) | copy-start | bytes 3538948
  28.5 28.7 %copy-start.2 = (f32[8,128,128]{2,1,0:T(8,128)S(1)}, f32[8,128,128]{2,1,0:T(8,128)}, u32[]{:S(2)}) copy-start(f32[8,128,128]{2,1,0:T(8,128)} %refs_2_.5) | copy-start | bytes 1572868
  28.5 16.8 %collective-permute-start.7 = (bf16[2,384,128]{2,1,0:T(8,128)(2,1)S(1)}, bf16[2,384,128]{2,1,0:T(8,128)(2,1)S(1)}, u32[]{:S(2)}, u32[]{:S(2)}) collective-permute-start(bf16[2,384,128]{2,1,0:T(8,128)(2,1)S(1)} %get-tuple-element.61), channel_id=1, source_target_pairs={{0,4},{1,5},{2,6},{3,7},{4,0},{5,1},{6,2},{7,3},{8,12},{9,13},{10,... | collective-permute-start | bytes 589832 | tf_op jit(solution)/shard_map/ppermute | solution.py:624
  30.2 15.1 %collective-permute-start.8 = (bf16[2,384,128]{2,1,0:T(8,128)(2,1)S(1)}, bf16[2,384,128]{2,1,0:T(8,128)(2,1)S(1)}, u32[]{:S(2)}, u32[]{:S(2)}) collective-permute-start(bf16[2,384,128]{2,1,0:T(8,128)(2,1)S(1)} %get-tuple-element.62), channel_id=1, source_target_pairs={{0,6},{1,7},{2,4},{3,5},{4,2},{5,3},{6,0},{7,1},{8,14},{9,15},{10,... | collective-permute-start | bytes 589832 | tf_op jit(solution)/shard_map/ppermute | solution.py:624
  32.6 12.7 %collective-permute-start.9 = (bf16[2,384,128]{2,1,0:T(8,128)(2,1)S(1)}, bf16[2,384,128]{2,1,0:T(8,128)(2,1)S(1)}, u32[]{:S(2)}, u32[]{:S(2)}) collective-permute-start(bf16[2,384,128]{2,1,0:T(8,128)(2,1)S(1)} %get-tuple-element.63), channel_id=1, source_target_pairs={{0,2},{1,3},{2,0},{3,1},{4,6},{5,7},{6,4},{7,5},{8,10},{9,11},{10,... | collective-permute-start | bytes 589832 | tf_op jit(solution)/shard_map/ppermute | solution.py:624
  45.5 9.0 %collective-permute-start.13 = (bf16[384,128]{1,0:T(8,128)(2,1)S(1)}, bf16[384,128]{1,0:T(8,128)(2,1)S(1)}, u32[]{:S(2)}, u32[]{:S(2)}) collective-permute-start(bf16[384,128]{1,0:T(8,128)(2,1)S(1)} %get-tuple-element.68), channel_id=1, source_target_pairs={{0,16},{1,17},{2,18},{3,19},{4,20},{5,21},{6,22},{7,23},{8,24},{9,... | collective-permute-start | bytes 294920 | tf_op jit(solution)/shard_map/ppermute | solution.py:624
  48.2 7.2 %collective-permute-start.14 = (bf16[384,128]{1,0:T(8,128)(2,1)S(1)}, bf16[384,128]{1,0:T(8,128)(2,1)S(1)}, u32[]{:S(2)}, u32[]{:S(2)}) collective-permute-start(bf16[384,128]{1,0:T(8,128)(2,1)S(1)} %get-tuple-element.69), channel_id=1, source_target_pairs={{0,24},{1,25},{2,26},{3,27},{4,28},{5,29},{6,30},{7,31},{8,16},{9,... | collective-permute-start | bytes 294920 | tf_op jit(solution)/shard_map/ppermute | solution.py:624
  49.5 6.2 %collective-permute-start.15 = (bf16[384,128]{1,0:T(8,128)(2,1)S(1)}, bf16[384,128]{1,0:T(8,128)(2,1)S(1)}, u32[]{:S(2)}, u32[]{:S(2)}) collective-permute-start(bf16[384,128]{1,0:T(8,128)(2,1)S(1)} %get-tuple-element.70), channel_id=1, source_target_pairs={{0,8},{1,9},{2,10},{3,11},{4,12},{5,13},{6,14},{7,15},{8,0},{9,1},... | collective-permute-start | bytes 294920 | tf_op jit(solution)/shard_map/ppermute | solution.py:624
  55.8 1.4 %collective-permute-start.17 = (bf16[384,128]{1,0:T(8,128)(2,1)S(1)}, bf16[384,128]{1,0:T(8,128)(2,1)S(1)}, u32[]{:S(2)}, u32[]{:S(2)}) collective-permute-start(bf16[384,128]{1,0:T(8,128)(2,1)S(1)} %final.1.refs_0_), channel_id=1, source_target_pairs={{0,1},{1,0},{2,3},{3,2},{4,5},{5,4},{6,7},{7,6},{8,9},{9,8},{10,11... | collective-permute-start | bytes 294920 | tf_op jit(solution)/shard_map/ppermute | solution.py:624
  55.9 5.2 %collective-permute-start.16 = (bf16[384,128]{1,0:T(8,128)(2,1)S(1)}, bf16[384,128]{1,0:T(8,128)(2,1)S(1)}, u32[]{:S(2)}, u32[]{:S(2)}) collective-permute-start(bf16[384,128]{1,0:T(8,128)(2,1)S(1)} %final.1.refs_0_), channel_id=1, source_target_pairs={{0,2},{1,3},{2,0},{3,1},{4,6},{5,7},{6,4},{7,5},{8,10},{9,11},{10,... | collective-permute-start | bytes 294920 | tf_op jit(solution)/shard_map/ppermute | solution.py:624
  61.1 1.4 %copy-start = (f32[8,192,192]{2,1,0:T(8,128)S(1)}, f32[8,192,192]{2,1,0:T(8,128)}, u32[]{:S(2)}) copy-start(f32[8,192,192]{2,1,0:T(8,128)} %get-tuple-element.71.order.refs_3_) | copy-start | bytes 3538948
  62.5 1.4 %collective-permute-start.18 = (bf16[384,128]{1,0:T(8,128)(2,1)S(1)}, bf16[384,128]{1,0:T(8,128)(2,1)S(1)}, u32[]{:S(2)}, u32[]{:S(2)}) collective-permute-start(bf16[384,128]{1,0:T(8,128)(2,1)S(1)} %relay.1.refs_0_), channel_id=1, source_target_pairs={{0,1},{1,0},{2,3},{3,2},{4,5},{5,4},{6,7},{7,6},{8,9},{9,8},{10,11... | collective-permute-start | bytes 294920 | tf_op jit(solution)/shard_map/ppermute | solution.py:624
